TPU v7x, 32 devices: a whole 2x2x4 slice. The times are simulated.
32 devices in a mesh: dp: 4 (over z), row: 4 (over x, core), col: 2 (over y).
Axes of the slice: x: 2, y: 2, z: 4, core: 2. Of those that a mesh axis runs over, the one named last changes fastest.
Arguments:
- tokens: bfloat16 [4096, 2048], P(('dp', 'row'), 'col'), may hold values from -8 to 8
- cotangent: bfloat16 [4096, 2048], P(('dp', 'row'), 'col'), may hold values from -8 to 8
- doc_lengths: int32 [12], replicated, may hold values from 1 to 1022, as said below
- doc_groups: int32 [12], replicated, may hold values from 0 to 3, as said below
- w_qkv: float32 [2048, 3, 2048], P(('col', 'dp'), None, 'row'), may hold values from -0.125 to 0.125
- w_up: float32 [2048, 4, 2048], P(('col', 'dp'), None, 'row'), may hold values from -0.125 to 0.125
- w_dense: float32 [2048, 2048], P(('row', 'dp'), 'col'), may hold values from -1.5 to 1.5
- w_down: float32 [2048, 4, 2048], P(('row', 'dp'), None, 'col'), may hold values from -0.0625 to 0.0625
- vectors: float32 [11, 2048], replicated, may hold values from -0.8 to 1.3
- m_qkv: float32 [2048, 3, 2048], P(('col', 'dp'), None, 'row'), may hold values from -40 to 40
- v_qkv: float32 [2048, 3, 2048], P(('col', 'dp'), None, 'row'), may hold values from 217.088 to 860.16
- m_up: float32 [2048, 4, 2048], P(('col', 'dp'), None, 'row'), may hold values from -12 to 12
- v_up: float32 [2048, 4, 2048], P(('col', 'dp'), None, 'row'), may hold values from 19.6608 to 77.824
- m_dense: float32 [2048, 2048], P(('row', 'dp'), 'col'), may hold values from -4 to 4
- v_dense: float32 [2048, 2048], P(('row', 'dp'), 'col'), may hold values from 1.68 to 6.8
- m_down: float32 [2048, 4, 2048], P(('row', 'dp'), None, 'col'), may hold values from -24 to 24
- v_down: float32 [2048, 4, 2048], P(('row', 'dp'), None, 'col'), may hold values from 77.824 to 311.296
- m_vec: float32 [11, 2048], replicated, may hold values from -44.8 to 44.8
- v_vec: float32 [11, 2048], replicated, may hold values from 16.384 to 2048
Outputs:
- block_out: bfloat16 [4096, 2048], P(('dp', 'row'), 'col')
- grad_tokens: float32 [4096, 2048], P(('dp', 'row'), 'col')
- m_qkv_next: float32 [2048, 3, 2048], P(('col', 'dp'), None, 'row')
- v_qkv_next: float32 [2048, 3, 2048], P(('col', 'dp'), None, 'row')
- w_qkv_next: float32 [2048, 3, 2048], P(('col', 'dp'), None, 'row')
- m_up_next: float32 [2048, 4, 2048], P(('col', 'dp'), None, 'row')
- v_up_next: float32 [2048, 4, 2048], P(('col', 'dp'), None, 'row')
- w_up_next: float32 [2048, 4, 2048], P(('col', 'dp'), None, 'row')
- m_dense_next: float32 [2048, 2048], P(('row', 'dp'), 'col')
- v_dense_next: float32 [2048, 2048], P(('row', 'dp'), 'col')
- w_dense_next: float32 [2048, 2048], P(('row', 'dp'), 'col')
- m_down_next: float32 [2048, 4, 2048], P(('row', 'dp'), None, 'col')
- v_down_next: float32 [2048, 4, 2048], P(('row', 'dp'), None, 'col')
- w_down_next: float32 [2048, 4, 2048], P(('row', 'dp'), None, 'col')
- m_vec_next: float32 [11, 2048], replicated
- v_vec_next: float32 [11, 2048], replicated
- vec_next: float32 [11, 2048], replicated
Inputs may be any that keep to these rules, and one draw needn't show every extreme that they name: `doc_lengths`: the sequences of one group hold at most 1024 tokens together, exactly 1024 in at least one group; in each group one sequence is longer than 768 and the others are shorter than 128. `doc_groups`: every data group holds exactly 3 sequences.
All inputs are finite; a program needn't handle non-finite values.
Results may differ from a plain program's by a relative error of at most 0.012.
Values may be sent and summed in bfloat16 or wider, within the bound.
A program may use at most 256 MiB of HBM per device.

v0:
```python
import jax
import jax.numpy as jnp
from jax import lax
from jax.sharding import PartitionSpec as P

D = 2048
HDIM = 64
ROT = 32
FF = 8192
BLK = 512
STEP = 10


eps_norm = 1e-05


def seq_layout(doc_lengths, doc_groups, group_id, slot_count):
    in_group = (doc_groups == group_id).astype(jnp.int32)
    group_sizes = doc_lengths * in_group
    seq_ends = jnp.cumsum(group_sizes, dtype=jnp.int32)
    starts = seq_ends - group_sizes
    total_len = jnp.sum(group_sizes, dtype=jnp.int32)
    places = jnp.arange(slot_count, dtype=jnp.int32)
    member = (
        (places[:, None] >= starts[None, :])
        & (places[:, None] < seq_ends[None, :])
        & (in_group[None, :] == 1)
    )
    member = member.astype(jnp.int32)
    number = jnp.arange(doc_lengths.shape[0], dtype=jnp.int32) + 1
    segment = jnp.sum(member * number[None, :], axis=1, dtype=jnp.int32) - 1
    seq_first = jnp.sum(member * starts[None, :], axis=1, dtype=jnp.int32)
    position = jnp.where(segment >= 0, places - seq_first, places - total_len)
    return (segment, position, total_len)


def turn_angles(position):
    half_rot = ROT // 2
    freq_base = jnp.power(10000.0, -2.0 * jnp.arange(half_rot, dtype=jnp.float32) / ROT)
    angle = position.astype(jnp.float32)[:, None] * freq_base[None, :]
    return (jnp.cos(angle), jnp.sin(angle))


def rotate(heads_view, cos_part, sin_part):
    half_rot = ROT // 2
    lead_part = heads_view[..., :half_rot]
    trail_part = heads_view[..., half_rot:ROT]
    cos_wide = cos_part[:, None, :]
    sin_wide = sin_part[:, None, :]
    return jnp.concatenate(
        [
            lead_part * cos_wide - trail_part * sin_wide,
            trail_part * cos_wide + lead_part * sin_wide,
            heads_view[..., ROT:],
        ],
        axis=-1,
    )


def unrotate(grad_view, cos_part, sin_part):
    half_rot = ROT // 2
    lead_part = grad_view[..., :half_rot]
    trail_part = grad_view[..., half_rot:ROT]
    cos_wide = cos_part[:, None, :]
    sin_wide = sin_part[:, None, :]
    return jnp.concatenate(
        [
            lead_part * cos_wide + trail_part * sin_wide,
            trail_part * cos_wide - lead_part * sin_wide,
            grad_view[..., ROT:],
        ],
        axis=-1,
    )


def block_scores(query_block, key_block, segment, places, row_begin, row_end, score_scale):
    scores = (
        jnp.einsum("qhd,khd->hqk", query_block, key_block, preferred_element_type=jnp.float32)
        * score_scale
    )
    allowed = (segment[row_begin:row_end, None] == segment[None, :row_end]) & (
        places[row_begin:row_end, None] >= places[None, :row_end]
    )
    return jnp.where(allowed[None], scores, -1e30)


def adamw(weight, first_moment, second_moment, gradient, rate, decay):
    first_next = 0.9 * first_moment + 0.1 * gradient
    second_next = 0.95 * second_moment + 0.05 * gradient * gradient
    correct_one = 1.0 - 0.9**STEP
    correct_two = 1.0 - 0.95**STEP
    update = first_next / correct_one / (jnp.sqrt(second_next / correct_two) + 1e-08)
    return (first_next, second_next, weight - rate * (update + decay * weight))


def per_device(
    tokens,
    cotangent,
    doc_lengths,
    doc_groups,
    w_qkv,
    w_up,
    w_dense,
    w_down,
    vectors,
    m_qkv,
    v_qkv,
    m_up,
    v_up,
    m_dense,
    v_dense,
    m_down,
    v_down,
    m_vec,
    v_vec,
):
    row_count = lax.axis_size("row")
    col_count = lax.axis_size("col")
    row_id = lax.axis_index("row")
    col_id = lax.axis_index("col")
    group_id = lax.axis_index("dp")
    tok_dev, col_width = tokens.shape
    slot_count = tok_dev * row_count
    full_width = col_width * col_count
    row_width = full_width // row_count
    part_width = row_width // col_count
    heads_dev = part_width // HDIM
    score_scale = HDIM ** (-0.5)
    segment, position, total_len = seq_layout(doc_lengths, doc_groups, group_id, slot_count)
    cos_part, sin_part = turn_angles(position)
    places = jnp.arange(slot_count, dtype=jnp.int32)
    col_start = col_id * col_width
    part_start = (row_id * col_count + col_id) * part_width
    zero_index = jnp.int32(0)
    wide_tokens = lax.all_gather(tokens, "col", axis=1, tiled=True)
    tokens_wide = wide_tokens.astype(jnp.float32)
    mean_tok = jnp.mean(tokens_wide, axis=-1, keepdims=True)
    var_tok = jnp.mean(tokens_wide * tokens_wide, axis=-1, keepdims=True) - mean_tok * mean_tok
    inv_std = lax.rsqrt(var_tok + eps_norm)
    centred = (tokens_wide - mean_tok) * inv_std
    normed = (centred * vectors[0] + vectors[1]).astype(jnp.bfloat16)
    qkv_block, up_block, dense_block, down_block = (
        lax.all_gather(w_qkv.astype(jnp.bfloat16), "dp", axis=0, tiled=True),
        lax.all_gather(w_up.astype(jnp.bfloat16), "dp", axis=0, tiled=True),
        lax.all_gather(w_dense.astype(jnp.bfloat16), "dp", axis=0, tiled=True),
        lax.all_gather(w_down.astype(jnp.bfloat16), "dp", axis=0, tiled=True),
    )
    bias_qkv = lax.dynamic_slice(vectors[2:5], (zero_index, part_start), (3, part_width))
    bias_up = lax.dynamic_slice(vectors[5:9], (zero_index, part_start), (4, part_width))
    sent_rows = lax.dynamic_slice_in_dim(normed, col_start, col_width, 1)
    normed_all = lax.all_gather(sent_rows, "row", axis=0, tiled=True)
    part_qkv = jnp.einsum("tc,ckj->tkj", normed_all, qkv_block, preferred_element_type=jnp.float32)
    part_up = jnp.einsum("tc,ckj->tkj", normed_all, up_block, preferred_element_type=jnp.float32)
    pre_qkv, pre_up = (
        lax.psum_scatter(part_qkv, "col", scatter_dimension=2, tiled=True),
        lax.psum_scatter(part_up, "col", scatter_dimension=2, tiled=True),
    )
    pre_qkv = pre_qkv + bias_qkv[None]
    pre_up = pre_up + bias_up[None]
    heads_view = pre_qkv.reshape(slot_count, 3, heads_dev, HDIM)
    queries = rotate(heads_view[:, 0], cos_part, sin_part).astype(jnp.bfloat16)
    key_rows = rotate(heads_view[:, 1], cos_part, sin_part).astype(jnp.bfloat16)
    values = heads_view[:, 2].astype(jnp.bfloat16)
    attn_blocks = []
    total_blocks = []
    for block_id in range(slot_count // BLK):
        row_begin = block_id * BLK
        row_end = row_begin + BLK
        scores = block_scores(
            queries[row_begin:row_end],
            key_rows[:row_end],
            segment,
            places,
            row_begin,
            row_end,
            score_scale,
        )
        top_score = jnp.max(scores, axis=-1, keepdims=True)
        weights = jnp.exp(scores - top_score)
        denominator = jnp.sum(weights, axis=-1, keepdims=True)
        probs_low = (weights / denominator).astype(jnp.bfloat16)
        attn_blocks.append(
            jnp.einsum(
                "hqk,khd->qhd", probs_low, values[:row_end], preferred_element_type=jnp.float32
            )
        )
        total_blocks.append(top_score + jnp.log(denominator))
    attn_send = (
        jnp.concatenate(attn_blocks, axis=0).reshape(slot_count, 1, part_width).astype(jnp.bfloat16)
    )
    hidden_send = jax.nn.gelu(pre_up, approximate=True).astype(jnp.bfloat16)
    attn_rows, hidden_all = (
        lax.all_gather(attn_send, "col", axis=2, tiled=True),
        lax.all_gather(hidden_send, "col", axis=2, tiled=True),
    )
    attn_flat = attn_rows.reshape(slot_count, row_width)
    branch = lax.psum_scatter(
        jnp.dot(attn_flat, dense_block, preferred_element_type=jnp.float32)
        + jnp.einsum("tij,jio->to", hidden_all, down_block, preferred_element_type=jnp.float32),
        "row",
        scatter_dimension=0,
        tiled=True,
    )
    out_bias = lax.dynamic_slice_in_dim(vectors[9] + vectors[10], col_start, col_width, 0)
    block_out = (tokens.astype(jnp.float32) + branch + out_bias[None, :]).astype(jnp.bfloat16)
    own_places = row_id * tok_dev + jnp.arange(tok_dev, dtype=jnp.int32)
    own_valid = own_places < total_len
    back_own = jnp.where(own_valid[:, None], cotangent, jnp.zeros_like(cotangent))
    back_all = lax.all_gather(back_own, "row", axis=0, tiled=True)
    part_attn = jnp.einsum(
        "to,jo->tj", back_all, dense_block, preferred_element_type=jnp.float32
    ).reshape(slot_count, 1, row_width)
    part_hidden = jnp.einsum(
        "to,jio->tij", back_all, down_block, preferred_element_type=jnp.float32
    )
    d_attn, d_hidden = (
        lax.psum_scatter(part_attn, "col", scatter_dimension=2, tiled=True),
        lax.psum_scatter(part_hidden, "col", scatter_dimension=2, tiled=True),
    )
    d_attn_low = d_attn.reshape(slot_count, heads_dev, HDIM).astype(jnp.bfloat16)
    unused_value, gelu_back = jax.vjp(lambda inputs: jax.nn.gelu(inputs, approximate=True), pre_up)
    d_pre_up = gelu_back(d_hidden)[0].astype(jnp.bfloat16)
    d_query_blocks = []
    d_key_sum = jnp.zeros((slot_count, heads_dev, HDIM), jnp.float32)
    d_value_sum = jnp.zeros((slot_count, heads_dev, HDIM), jnp.float32)
    for block_id in range(slot_count // BLK):
        row_begin = block_id * BLK
        row_end = row_begin + BLK
        query_block = queries[row_begin:row_end]
        scores = block_scores(
            query_block, key_rows[:row_end], segment, places, row_begin, row_end, score_scale
        )
        probs_full = jnp.exp(scores - total_blocks[block_id])
        probs_low = probs_full.astype(jnp.bfloat16)
        d_out_block = d_attn_low[row_begin:row_end]
        d_probs = jnp.einsum(
            "qhd,khd->hqk", d_out_block, values[:row_end], preferred_element_type=jnp.float32
        )
        delta_rows = jnp.sum(probs_full * d_probs, axis=-1, keepdims=True)
        d_scores = (probs_full * (d_probs - delta_rows)).astype(jnp.bfloat16)
        d_query_blocks.append(
            jnp.einsum(
                "hqk,khd->qhd", d_scores, key_rows[:row_end], preferred_element_type=jnp.float32
            )
            * score_scale
        )
        padding = ((0, slot_count - row_end), (0, 0), (0, 0))
        d_key_sum = d_key_sum + jnp.pad(
            jnp.einsum("hqk,qhd->khd", d_scores, query_block, preferred_element_type=jnp.float32)
            * score_scale,
            padding,
        )
        d_value_sum = d_value_sum + jnp.pad(
            jnp.einsum("hqk,qhd->khd", probs_low, d_out_block, preferred_element_type=jnp.float32),
            padding,
        )
    d_queries = unrotate(jnp.concatenate(d_query_blocks, axis=0), cos_part, sin_part)
    d_keys = unrotate(d_key_sum, cos_part, sin_part)
    d_qkv = (
        jnp.stack([d_queries, d_keys, d_value_sum], axis=1)
        .reshape(slot_count, 3, part_width)
        .astype(jnp.bfloat16)
    )
    qkv_grads, up_grads = (
        lax.all_gather(d_qkv, "col", axis=2, tiled=True),
        lax.all_gather(d_pre_up, "col", axis=2, tiled=True),
    )
    g_qkv = jnp.einsum("tc,tkj->ckj", normed_all, qkv_grads, preferred_element_type=jnp.float32)
    g_up = jnp.einsum("tc,tkj->ckj", normed_all, up_grads, preferred_element_type=jnp.float32)
    g_dense = jnp.einsum("tj,to->jo", attn_flat, back_all, preferred_element_type=jnp.float32)
    g_down = jnp.einsum("tij,to->jio", hidden_all, back_all, preferred_element_type=jnp.float32)
    red_qkv, red_up, red_dense, red_down = (
        lax.psum_scatter(g_qkv, "dp", scatter_dimension=0, tiled=True),
        lax.psum_scatter(g_up, "dp", scatter_dimension=0, tiled=True),
        lax.psum_scatter(g_dense, "dp", scatter_dimension=0, tiled=True),
        lax.psum_scatter(g_down, "dp", scatter_dimension=0, tiled=True),
    )
    d_normed = lax.psum_scatter(
        (
            jnp.einsum("tkj,ckj->tc", qkv_grads, qkv_block, preferred_element_type=jnp.float32)
            + jnp.einsum("tkj,ckj->tc", up_grads, up_block, preferred_element_type=jnp.float32)
        ).astype(jnp.bfloat16),
        "row",
        scatter_dimension=0,
        tiled=True,
    ).astype(jnp.float32)
    gain_cols = lax.dynamic_slice_in_dim(vectors[0], col_start, col_width, 0)
    centred_cols = lax.dynamic_slice_in_dim(centred, col_start, col_width, 1)
    d_hat = d_normed * gain_cols[None, :]
    sum_hat, sum_cross = lax.psum(
        (jnp.sum(d_hat, axis=-1), jnp.sum(d_hat * centred_cols, axis=-1)), "col"
    )
    back_float = back_own.astype(jnp.float32)
    grad_tokens = (
        inv_std
        * (d_hat - sum_hat[:, None] / full_width - centred_cols * sum_cross[:, None] / full_width)
        + back_float
    )
    vec_part = jnp.zeros((11, full_width), jnp.float32)
    norm_rows = jnp.stack([jnp.sum(d_normed * centred_cols, axis=0), jnp.sum(d_normed, axis=0)])
    vec_part = lax.dynamic_update_slice(vec_part, norm_rows, (zero_index, col_start))
    head_rows = jnp.concatenate(
        [jnp.sum(d_qkv.astype(jnp.float32), axis=0), jnp.sum(d_pre_up.astype(jnp.float32), axis=0)],
        axis=0,
    )
    vec_part = lax.dynamic_update_slice(vec_part, head_rows, (jnp.int32(2), part_start))
    out_sums = jnp.sum(back_float, axis=0)
    vec_part = lax.dynamic_update_slice(
        vec_part, jnp.stack([out_sums, out_sums]), (jnp.int32(9), col_start)
    )
    vec_grad = lax.psum(vec_part, ("dp", "row", "col"))
    qkv_new = adamw(w_qkv, m_qkv, v_qkv, red_qkv, D ** (-0.5), 0.1)
    up_new = adamw(w_up, m_up, v_up, red_up, D ** (-0.5), 0.1)
    dense_new = adamw(w_dense, m_dense, v_dense, red_dense, max(D // 128, 4) ** (-0.5), 0.1)
    down_new = adamw(w_down, m_down, v_down, red_down, FF ** (-0.5), 0.1)
    vec_new = adamw(vectors, m_vec, v_vec, vec_grad, 0.5, 0.0)
    return (
        block_out,
        grad_tokens,
        qkv_new[0],
        qkv_new[1],
        qkv_new[2],
        up_new[0],
        up_new[1],
        up_new[2],
        dense_new[0],
        dense_new[1],
        dense_new[2],
        down_new[0],
        down_new[1],
        down_new[2],
        vec_new[0],
        vec_new[1],
        vec_new[2],
    )


def solution(mesh):
    placed = (
        P(("dp", "row"), "col"),
        P(("dp", "row"), "col"),
        P(),
        P(),
        P(("col", "dp"), None, "row"),
        P(("col", "dp"), None, "row"),
        P(("row", "dp"), "col"),
        P(("row", "dp"), None, "col"),
        P(),
        P(("col", "dp"), None, "row"),
        P(("col", "dp"), None, "row"),
        P(("col", "dp"), None, "row"),
        P(("col", "dp"), None, "row"),
        P(("row", "dp"), "col"),
        P(("row", "dp"), "col"),
        P(("row", "dp"), None, "col"),
        P(("row", "dp"), None, "col"),
        P(),
        P(),
    )
    return jax.shard_map(
        per_device,
        mesh=mesh,
        in_specs=placed,
        out_specs=(
            P(("dp", "row"), "col"),
            P(("dp", "row"), "col"),
            P(("col", "dp"), None, "row"),
            P(("col", "dp"), None, "row"),
            P(("col", "dp"), None, "row"),
            P(("col", "dp"), None, "row"),
            P(("col", "dp"), None, "row"),
            P(("col", "dp"), None, "row"),
            P(("row", "dp"), "col"),
            P(("row", "dp"), "col"),
            P(("row", "dp"), "col"),
            P(("row", "dp"), None, "col"),
            P(("row", "dp"), None, "col"),
            P(("row", "dp"), None, "col"),
            P(),
            P(),
            P(),
        ),
        check_vma=False,
    )
```

profile of v0, /device:TPU:0, one launch (start us, length us, event | category | flops | bytes accessed | tf_op | source)
XLA Modules:
  0.0 1536.4 jit_solution(14600298835788059222)
XLA Ops:
  10.1 23.5 %all-gather.12.cloned.1.call-done = bf16[256,2048]{1,0:T(8,128)(2,1)} async-done(((bf16[256,1024]{1,0:T(8,128)(2,1)}), bf16[256,2048]{1,0:T(8,128)(2,1)}) %all-gather.12.cloned.1.call-update) | async-done | bytes 1048592 | tf_op jit(solution)/shard_map/all_gather | solution.py:135
  33.6 1.7 convert_reduce_fusion.2
  35.9 1.6 fusion.16
  40.9 21.6 %all-gather.14.cloned.1.call-done = bf16[1024,1024]{1,0:T(8,128)(2,1)} async-done(((bf16[256,1024]{1,0:T(8,128)(2,1)}), bf16[1024,1024]{1,0:T(8,128)(2,1)}) %all-gather.14.cloned.1.call-update) | async-done | bytes 2097168 | tf_op jit(solution)/shard_map/all_gather | solution.py:151
  62.5 65.7 %all-gather.16.cloned.1.call-done = bf16[1024,3,512]{2,0,1:T(8,128)(2,1)} async-done(((bf16[256,3,512]{2,0,1:T(8,128)(2,1)}), bf16[1024,3,512]{2,0,1:T(8,128)(2,1)}) %all-gather.16.cloned.1.call-update) | async-done | bytes 3145744 | tf_op jit(solution)/shard_map/all_gather | solution.py:143
  128.2 8.6 fusion.30
  138.8 1.6 convert_reduce_fusion.4
  145.0 67.7 %reduce-scatter.11.cloned.1.call-done = f32[1024,3,256]{2,0,1:T(8,128)} async-done(((f32[1024,3,512]{2,0,1:T(8,128)}), f32[1024,3,256]{2,0,1:T(8,128)}) %reduce-scatter.11.cloned.1.call-update) | async-done | bytes 3145744 | tf_op jit(solution)/shard_map/reduce_scatter | solution.py:155
  212.8 3.8 broadcast_add_fusion
  216.6 2.4 copy.98
  223.0 1.8 fusion.96
  224.8 1.9 fusion
  228.2 2.1 fusion.59
  231.4 6.0 all-gather.28.cloned.1.call-done
  237.4 23.4 %all-gather.18.cloned.1.call-done = bf16[1024,1,512]{0,2,1:T(8,128)(2,1)} async-done(((bf16[1024,1,256]{0,2,1:T(8,128)(2,1)}), bf16[1024,1,512]{0,2,1:T(8,128)(2,1)}) %all-gather.18.cloned.1.call-update) | async-done | bytes 1048592 | tf_op jit(solution)/shard_map/all_gather | solution.py:193
  260.8 4.5 fusion.65
  265.4 44.0 %reduce-scatter.27.cloned.1.call-done = f32[128,1024]{1,0:T(8,128)} async-done(((f32[512,1024]{1,0:T(8,128)}), f32[128,1024]{1,0:T(8,128)}) %reduce-scatter.27.cloned.1.call-update) | async-done | bytes 524304 | tf_op jit(solution)/shard_map/reduce_scatter | solution.py:275
  309.4 3.3 multiply_subtract_fusion.3
  314.4 3.8 copy.146
  318.3 21.8 %all-gather.20.cloned.1.call-done = bf16[512,1024]{1,0:T(8,128)(2,1)} async-done(((bf16[128,1024]{1,0:T(8,128)(2,1)}), bf16[512,1024]{1,0:T(8,128)(2,1)}) %all-gather.20.cloned.1.call-update) | async-done | bytes 1048592 | tf_op jit(solution)/shard_map/all_gather | solution.py:145
  340.1 3.8 convolution_bitcast_fusion.2
  344.0 78.5 %all-gather.22.cloned.1.call-done = bf16[1024,4,512]{2,0,1:T(8,128)(2,1)} async-done(((bf16[256,4,512]{2,0,1:T(8,128)(2,1)}), bf16[1024,4,512]{2,0,1:T(8,128)(2,1)}) %all-gather.22.cloned.1.call-update) | async-done | bytes 4194320 | tf_op jit(solution)/shard_map/all_gather | solution.py:144
  422.5 8.9 fusion.28
  431.5 72.3 %all-gather.26.cloned.1.call-done = bf16[512,4,1024]{2,0,1:T(8,128)(2,1)} async-done(((bf16[128,4,1024]{2,0,1:T(8,128)(2,1)}), bf16[512,4,1024]{2,0,1:T(8,128)(2,1)}) %all-gather.26.cloned.1.call-update) | async-done | bytes 4194320 | tf_op jit(solution)/shard_map/all_gather | solution.py:146
  503.8 9.0 convolution_bitcast_fusion.1
  513.5 23.5 %reduce-scatter.17.cloned.1.call-done = f32[1024,1,256]{2,0,1:T(8,128)} async-done(((f32[1024,1,512]{2,0,1:T(8,128)}), f32[1024,1,256]{2,0,1:T(8,128)}) %reduce-scatter.17.cloned.1.call-update) | async-done | bytes 1048592 | tf_op jit(solution)/shard_map/reduce_scatter | solution.py:217
  540.3 3.3 multiply_reduce_fusion.1
  547.1 2.5 multiply_reduce_fusion
  549.7 1.7 multiply_convert_fusion
  554.9 3.0 fusion.51
  557.9 5.1 fusion.48
  564.8 73.7 %reduce-scatter.13.cloned.1.call-done = f32[1024,4,256]{2,0,1:T(8,128)} async-done(((f32[1024,4,512]{2,0,1:T(8,128)}), f32[1024,4,256]{2,0,1:T(8,128)}) %reduce-scatter.13.cloned.1.call-update) | async-done | bytes 4194320 | tf_op jit(solution)/shard_map/reduce_scatter | solution.py:156
  638.6 101.6 %reduce-scatter.19.cloned.1.call-done = f32[1024,4,256]{2,0,1:T(8,128)} async-done(((f32[1024,4,512]{2,0,1:T(8,128)}), f32[1024,4,256]{2,0,1:T(8,128)}) %reduce-scatter.19.cloned.1.call-update) | async-done | bytes 4194320 | tf_op jit(solution)/shard_map/reduce_scatter | solution.py:218
  740.1 7.0 convert_reduce_fusion
  748.0 39.2 %all-gather.30.cloned.1.call-done = bf16[1024,3,512]{2,0,1:T(8,128)(2,1)} async-done(((bf16[1024,3,256]{2,0,1:T(8,128)(2,1)}), bf16[1024,3,512]{2,0,1:T(8,128)(2,1)}) %all-gather.30.cloned.1.call-update) | async-done | bytes 3145744 | tf_op jit(solution)/shard_map/all_gather | solution.py:265
  787.1 6.9 fusion.98
  794.1 51.8 %all-gather.32.cloned.1.call-done = bf16[1024,4,512]{2,0,1:T(8,128)(2,1)} async-done(((bf16[1024,4,256]{2,0,1:T(8,128)(2,1)}), bf16[1024,4,512]{2,0,1:T(8,128)(2,1)}) %all-gather.32.cloned.1.call-update) | async-done | bytes 4194320 | tf_op jit(solution)/shard_map/all_gather | solution.py:266
  845.9 10.5 fusion.11
  858.1 3.3 fusion.67
  861.4 43.3 %all-gather.24.cloned.1.call-done = bf16[1024,4,512]{2,0,1:T(8,128)(2,1)} async-done(((bf16[1024,4,256]{2,0,1:T(8,128)(2,1)}), bf16[1024,4,512]{2,0,1:T(8,128)(2,1)}) %all-gather.24.cloned.1.call-update) | async-done | bytes 4194320 | tf_op jit(solution)/shard_map/all_gather | solution.py:194
  904.7 11.1 bitcast_add_fusion.1
  916.5 22.7 %reduce-scatter.21.cloned.1.call-done = bf16[256,1024]{1,0:T(8,128)(2,1)} async-done(((bf16[1024,1024]{1,0:T(8,128)(2,1)}), bf16[256,1024]{1,0:T(8,128)(2,1)}) %reduce-scatter.21.cloned.1.call-update) | async-done | bytes 524304 | tf_op jit(solution)/shard_map/reduce_scatter | solution.py:278
  942.9 10.7 fusion.24
  953.7 10.6 convolution_bitcast_fusion
  964.4 8.7 fusion.26
  973.1 2.9 copy.120
  976.0 2.9 copy.116
  979.0 3.0 copy.118
  982.0 5.3 all-reduce.2
  987.3 2.3 add_convert_fusion
  991.0 124.6 %all-reduce.5.cloned.1.call-done = f32[11,2048]{1,0:T(8,128)} async-done(((f32[11,2048]{1,0:T(8,128)}), f32[11,2048]{1,0:T(8,128)}) %all-reduce.5.cloned.1.call-update) | async-done | bytes 90128 | tf_op jit(solution)/shard_map/psum | solution.py:311
  1115.7 1.7 multiply_subtract_fusion.4
  1117.4 144.1 %reduce-scatter.25.cloned.1.call-done = f32[256,4,512]{2,0,1:T(8,128)} async-done(((f32[1024,4,512]{2,0,1:T(8,128)}), f32[256,4,512]{2,0,1:T(8,128)}) %reduce-scatter.25.cloned.1.call-update) | async-done | bytes 2097168 | tf_op jit(solution)/shard_map/reduce_scatter | solution.py:274
  1261.5 6.4 multiply_subtract_fusion.1
  1268.0 2.7 copy.121
  1270.6 2.7 copy.122
  1273.3 2.7 copy.123
  1276.0 133.3 %reduce-scatter.29.cloned.1.call-done = f32[128,4,1024]{0,2,1:T(8,128)} async-done(((f32[512,4,1024]{0,2,1:T(8,128)}), f32[128,4,1024]{0,2,1:T(8,128)}) %reduce-scatter.29.cloned.1.call-update) | async-done | bytes 2097168 | tf_op jit(solution)/shard_map/reduce_scatter | solution.py:276
  1409.2 6.6 multiply_subtract_fusion
  1415.8 3.3 copy.124
  1419.1 3.3 copy.125
  1422.5 2.0 copy.126
  1424.4 98.7 %reduce-scatter.23.cloned.1.call-done = f32[256,3,512]{2,0,1:T(8,128)} async-done(((f32[1024,3,512]{2,0,1:T(8,128)}), f32[256,3,512]{2,0,1:T(8,128)}) %reduce-scatter.23.cloned.1.call-update) | async-done | bytes 1572880 | tf_op jit(solution)/shard_map/reduce_scatter | solution.py:273
  1523.1 5.9 multiply_subtract_fusion.2
  (200 shorter events, 42.8 us)
Async XLA Ops:
  7.2 26.4 %all-gather.12.cloned.1.call-start = ((), (), s32[]{:S(2)}) async-start(), calls=%async_computation.10 | async-start | bytes 1572864 | tf_op jit(solution)/shard_map/all_gather | solution.py:135
  7.9 54.6 %all-gather.14.cloned.1.call-start = ((), (), s32[]{:S(2)}) async-start(), calls=%async_computation.11 | async-start | bytes 2621440 | tf_op jit(solution)/shard_map/all_gather | solution.py:151
  9.5 0.6 copy-start.24
  35.9 4.0 copy-start.8
  37.5 1.3 copy-start.3
  39.8 88.4 %all-gather.16.cloned.1.call-start = ((), (), s32[]{:S(2)}) async-start(), calls=%async_computation.12 | async-start | bytes 3932160 | tf_op jit(solution)/shard_map/all_gather | solution.py:143
  40.9 171.9 %reduce-scatter.11.cloned.1.call-start = ((), (), s32[]{:S(2)}) async-start(), calls=%async_computation.13 | async-start | bytes 9437184 | tf_op jit(solution)/shard_map/reduce_scatter | solution.py:155
  136.8 0.7 copy-start.35
  136.8 0.7 copy-start.36
  136.8 2.0 copy-start.17
  136.8 100.6 %all-gather.28.cloned.1.call-start = ((), (), s32[]{:S(2)}) async-start(), calls=%async_computation.21 | async-start | bytes 2621440 | tf_op jit(solution)/shard_map/all_gather | solution.py:209
  140.4 120.4 %all-gather.18.cloned.1.call-start = ((), (), s32[]{:S(2)}) async-start(), calls=%async_computation.14 | async-start | bytes 1572864 | tf_op jit(solution)/shard_map/all_gather | solution.py:193
  219.2 8.3 copy-start.10
  219.5 1.2 copy-start.19
  221.5 5.1 copy-start.1
  221.6 1.4 copy-start.15
  223.0 3.7 copy-start.22
  224.8 3.3 copy-start
  224.8 3.4 copy-start.26
  226.7 1.5 copy-start.28
  231.2 78.2 %reduce-scatter.27.cloned.1.call-start = ((), (), s32[]{:S(2)}) async-start(), calls=%async_computation.29 | async-start | bytes 2621440 | tf_op jit(solution)/shard_map/reduce_scatter | solution.py:275
  265.3 47.4 %copy-start.5 = (f32[256,4,512]{2,1,0:T(4,128)S(1)}, f32[256,4,512]{2,1,0:T(4,128)}, u32[]{:S(2)}) copy-start(f32[256,4,512]{2,1,0:T(4,128)} %param.24) | copy-start | bytes 6291460
  265.3 74.7 %all-gather.20.cloned.1.call-start = ((), (), s32[]{:S(2)}) async-start(), calls=%async_computation.15 | async-start | bytes 1310720 | tf_op jit(solution)/shard_map/all_gather | solution.py:145
  312.7 109.8 %all-gather.22.cloned.1.call-start = ((), (), s32[]{:S(2)}) async-start(), calls=%async_computation.16 | async-start | bytes 5242880 | tf_op jit(solution)/shard_map/all_gather | solution.py:144
  314.3 25.8 %copy-start.39 = (bf16[1024,1024]{1,0:T(8,128)(2,1)S(1)}, bf16[1024,1024]{1,0:T(8,128)(2,1)}, u32[]{:S(2)}) copy-start(bf16[1024,1024]{1,0:T(8,128)(2,1)} %all-gather.28.cloned.1.call-done) | copy-start | bytes 6291460
  314.3 189.5 %all-gather.26.cloned.1.call-start = ((), (), s32[]{:S(2)}) async-start(), calls=%async_computation.19 | async-start | bytes 5242880 | tf_op jit(solution)/shard_map/all_gather | solution.py:146
  318.2 218.8 %reduce-scatter.17.cloned.1.call-start = ((), (), s32[]{:S(2)}) async-start(), calls=%async_computation.22 | async-start | bytes 3145728 | tf_op jit(solution)/shard_map/reduce_scatter | solution.py:217
  343.9 78.6 %copy-start.38 = (bf16[1024,1024]{1,0:T(8,128)(2,1)S(1)}, bf16[1024,1024]{1,0:T(8,128)(2,1)}, u32[]{:S(2)}) copy-start(bf16[1024,1024]{1,0:T(8,128)(2,1)} %all-gather.14.cloned.1.call-done) | copy-start | bytes 6291460
  343.9 294.6 %reduce-scatter.13.cloned.1.call-start = ((), (), s32[]{:S(2)}) async-start(), calls=%async_computation.17 | async-start | bytes 12582912 | tf_op jit(solution)/shard_map/reduce_scatter | solution.py:156
  431.4 72.4 %copy-start.40 = (bf16[1024,1024]{1,0:T(8,128)(2,1)S(1)}, bf16[1024,1024]{1,0:T(8,128)(2,1)}, u32[]{:S(2)}) copy-start(bf16[1024,1024]{1,0:T(8,128)(2,1)} %all-gather.28.cloned.1.call-done) | copy-start | bytes 6291460
  431.4 308.7 %reduce-scatter.19.cloned.1.call-start = ((), (), s32[]{:S(2)}) async-start(), calls=%async_computation.24 | async-start | bytes 12582912 | tf_op jit(solution)/shard_map/reduce_scatter | solution.py:218
  512.8 0.7 copy-start.23
  512.8 0.7 copy-start.27
  512.8 0.7 copy-start.29
  512.8 27.5 %copy-start.11 = (bf16[1024,3,4,64]{0,3,2,1:T(8,128)(2,1)S(1)}, bf16[1024,3,4,64]{0,3,2,1:T(8,128)(2,1)}, u32[]{:S(2)}) copy-start(bf16[1024,3,4,64]{0,3,2,1:T(8,128)(2,1)} %copy-done.10) | copy-start | bytes 4718596
  512.8 274.3 %all-gather.30.cloned.1.call-start = ((), (), s32[]{:S(2)}) async-start(), calls=%async_computation.23 | async-start | bytes 4718592 | tf_op jit(solution)/shard_map/all_gather | solution.py:265
  540.3 3.5 copy-start.2
  540.3 5.4 slice-start
  543.8 3.4 slice-start.1
  563.2 1.6 copy-start.18
  564.7 281.2 %all-gather.32.cloned.1.call-start = ((), (), s32[]{:S(2)}) async-start(), calls=%async_computation.25 | async-start | bytes 6291456 | tf_op jit(solution)/shard_map/all_gather | solution.py:266
  747.1 40.0 %copy-start.37 = (bf16[1024,3,512]{2,0,1:T(8,128)(2,1)S(1)}, bf16[1024,3,512]{2,0,1:T(8,128)(2,1)}, u32[]{:S(2)}) copy-start(bf16[1024,3,512]{2,0,1:T(8,128)(2,1)} %all-gather.16.cloned.1.call-done) | copy-start | bytes 9437188
  747.2 157.5 %all-gather.24.cloned.1.call-start = ((), (), s32[]{:S(2)}) async-start(), calls=%async_computation.18 | async-start | bytes 6291456 | tf_op jit(solution)/shard_map/all_gather | solution.py:194
  747.7 191.5 %reduce-scatter.21.cloned.1.call-start = ((), (), s32[]{:S(2)}) async-start(), calls=%async_computation.26 | async-start | bytes 2621440 | tf_op jit(solution)/shard_map/reduce_scatter | solution.py:278
  856.4 1.3 copy-start.13
  856.4 1.7 copy-start.14
  856.4 130.9 %reduce-scatter.15.cloned.1.call-start = ((), (), s32[]{:S(2)}) async-start(), calls=%async_computation.20 | async-start | bytes 5242880 | tf_op jit(solution)/shard_map/reduce_scatter | solution.py:197
  915.8 0.7 copy-start.25
  915.8 0.7 copy-start.32
  915.8 23.4 %copy-start.4 = (f32[256,2048]{1,0:T(8,128)S(1)}, f32[256,2048]{1,0:T(8,128)}, u32[]{:S(2)}) copy-start(f32[256,2048]{1,0:T(8,128)} %copy-done.3) | copy-start | bytes 6291460
  915.8 199.8 %all-reduce.5.cloned.1.call-start = ((), (), s32[]{:S(2)}) async-start(), calls=%async_computation.31 | async-start | bytes 262144 | tf_op jit(solution)/shard_map/psum | solution.py:311
  942.0 0.7 copy-start.16
  942.6 318.9 %reduce-scatter.25.cloned.1.call-start = ((), (), s32[]{:S(2)}) async-start(), calls=%async_computation.28 | async-start | bytes 10485760 | tf_op jit(solution)/shard_map/reduce_scatter | solution.py:274
  953.6 455.6 %reduce-scatter.29.cloned.1.call-start = ((), (), s32[]{:S(2)}) async-start(), calls=%async_computation.30 | async-start | bytes 10485760 | tf_op jit(solution)/shard_map/reduce_scatter | solution.py:276
  964.4 558.8 %reduce-scatter.23.cloned.1.call-start = ((), (), s32[]{:S(2)}) async-start(), calls=%async_computation.27 | async-start | bytes 7864320 | tf_op jit(solution)/shard_map/reduce_scatter | solution.py:273
  979.0 3.0 copy-start.30
  979.0 3.0 copy-start.31
  981.9 7.7 copy-start.9
  981.9 7.7 copy-start.12
  981.9 7.7 copy-start.34
  989.6 126.0 %copy-start.20 = (f32[11,2048]{1,0:T(8,128)S(1)}, f32[11,2048]{1,0:T(8,128)}, u32[]{:S(2)}) copy-start(f32[11,2048]{1,0:T(8,128)} %param.37) | copy-start | bytes 270340
  989.6 126.0 %copy-start.21 = (f32[11,2048]{1,0:T(8,128)S(1)}, f32[11,2048]{1,0:T(8,128)}, u32[]{:S(2)}) copy-start(f32[11,2048]{1,0:T(8,128)} %param.36) | copy-start | bytes 270340
  1273.3 136.0 %copy-start.6 = (f32[128,4,1024]{0,2,1:T(8,128)S(1)}, f32[128,4,1024]{0,2,1:T(8,128)}, u32[]{:S(2)}) copy-start(f32[128,4,1024]{0,2,1:T(8,128)} %copy.120) | copy-start | bytes 6291460
  1419.1 3.3 copy-start.7
  (1 other events, 0.6 us)
Sparse Core Ops, SparseCore 0:
  9.6 23.9 all-gather.11
  39.9 22.5 all-gather.13
  64.7 63.4 all-gather.15
  136.9 75.7 reduce-scatter.10
  214.8 22.5 all-gather.27
  239.5 21.3 all-gather.17
  265.4 43.8 reduce-scatter.26
  312.8 27.2 all-gather.19
  342.2 80.2 all-gather.21
  424.5 79.2 all-gather.25
  506.7 30.3 reduce-scatter.16
  539.3 99.2 reduce-scatter.12
  640.9 99.2 reduce-scatter.18
  742.2 44.8 all-gather.29
  789.2 56.7 all-gather.31
  847.9 56.7 all-gather.23
  907.8 31.3 reduce-scatter.20
  941.6 44.5 reduce-scatter.14
  993.2 122.4 all-reduce.4
  1118.0 143.4 reduce-scatter.24
  1264.0 145.2 reduce-scatter.28
  1411.6 111.4 reduce-scatter.22
where the time goes:
time: 1550 us; the launch traced here: 1540 us
  waiting for transfers between devices  1280 us (83%)
  matrix products  120 us (8%)
  other arithmetic  61.3 us (4%)
  local copies, waits for them, and re-layouts  50 us (3%)
  between operations  15.5 us (1%)
    reduce_scatter x1, waiting for transfers between devices, per_device(): lax.psum_scatter(g_up, 'dp', scatter_dimension=0, tiled=True)  144 us
    reduce_scatter x1, waiting for transfers between devices, per_device(): lax.psum_scatter(g_down, 'dp', scatter_dimension=0, tiled=True)  133 us
    psum x1, waiting for transfers between devices, per_device(): vec_grad = lax.psum(vec_part, ('dp', 'row', 'col'))  125 us
    reduce_scatter x1, waiting for transfers between devices, per_device(): lax.psum_scatter(part_hidden, 'col', scatter_dimension=2, tiled=True)  102 us
    reduce_scatter x1, waiting for transfers between devices, per_device(): lax.psum_scatter(g_qkv, 'dp', scatter_dimension=0, tiled=True)  98.7 us
    all_gather x1, waiting for transfers between devices, per_device(): lax.all_gather(w_up.astype(jnp.bfloat16), 'dp', axis=0, tiled=True)  78.5 us
    reduce_scatter x1, waiting for transfers between devices, per_device(): lax.psum_scatter(part_up, 'col', scatter_dimension=2, tiled=True)  73.7 us
    all_gather x1, waiting for transfers between devices, per_device(): lax.all_gather(w_down.astype(jnp.bfloat16), 'dp', axis=0, tiled=True)  72.3 us
  transfers between devices with their start and end apart: 22, of which 21 were waited for; matrix products, arithmetic and copies ran while one was open for 13% of the time, Pallas kernels for 0%

commit v1 on v0

v1 whole, which is shorter than its diff:
```python
import functools

import jax
import jax.numpy as jnp
from jax import lax
from jax.experimental import pallas as pl
from jax.experimental.pallas import tpu as pltpu
from jax.sharding import PartitionSpec as P

D = 2048
HDIM = 64
ROT = 32
FF = 8192
BLK = 512
STEP = 10
LINE = 4


eps_norm = 1e-05
f32 = jnp.float32
bf16 = jnp.bfloat16


def seq_layout(doc_lengths, doc_groups, group_id, places):
    in_group = (doc_groups == group_id).astype(jnp.int32)
    group_sizes = doc_lengths * in_group
    seq_ends = jnp.cumsum(group_sizes, dtype=jnp.int32)
    starts = seq_ends - group_sizes
    total_len = jnp.sum(group_sizes, dtype=jnp.int32)
    member = (
        (places[:, None] >= starts[None, :])
        & (places[:, None] < seq_ends[None, :])
        & (in_group[None, :] == 1)
    )
    member = member.astype(jnp.int32)
    number = jnp.arange(doc_lengths.shape[0], dtype=jnp.int32) + 1
    segment = jnp.sum(member * number[None, :], axis=1, dtype=jnp.int32) - 1
    seq_first = jnp.sum(member * starts[None, :], axis=1, dtype=jnp.int32)
    position = jnp.where(segment >= 0, places - seq_first, places - total_len)
    return (segment, position, total_len)


def turn_angles(position):
    half_rot = ROT // 2
    freq_base = jnp.power(10000.0, -2.0 * jnp.arange(half_rot, dtype=jnp.float32) / ROT)
    angle = position.astype(jnp.float32)[:, None] * freq_base[None, :]
    return (jnp.cos(angle), jnp.sin(angle))


def rotate(heads_view, cos_part, sin_part):
    half_rot = ROT // 2
    lead_part = heads_view[..., :half_rot]
    trail_part = heads_view[..., half_rot:ROT]
    cos_wide = cos_part[..., None, :]
    sin_wide = sin_part[..., None, :]
    return jnp.concatenate(
        [
            lead_part * cos_wide - trail_part * sin_wide,
            trail_part * cos_wide + lead_part * sin_wide,
            heads_view[..., ROT:],
        ],
        axis=-1,
    )


def adamw(weight, first_moment, second_moment, gradient, rate, decay):
    first_next = 0.9 * first_moment + 0.1 * gradient
    second_next = 0.95 * second_moment + 0.05 * gradient * gradient
    correct_one = 1.0 - 0.9**STEP
    correct_two = 1.0 - 0.95**STEP
    update = first_next / correct_one / (jnp.sqrt(second_next / correct_two) + 1e-08)
    return (first_next, second_next, weight - rate * (update + decay * weight))


class Copies:
    def __init__(self, send_sems, recv_sems):
        self.send_sems, self.recv_sems, self.sent, self.received = send_sems, recv_sems, 0, 0

    def slot(self):
        self.received += 1
        return self.received - 1

    def make(self, src, dst, device, slot=None):
        slot = self.slot() if slot is None else slot
        self.sent += 1
        return pltpu.make_async_remote_copy(
            src_ref=src, dst_ref=dst, send_sem=self.send_sems.at[self.sent - 1], recv_sem=self.recv_sems.at[slot],
            device_id=device, device_id_type=pl.DeviceIdType.MESH)

def neighbours(tier_count):
    dp_id, row_id, col_id = lax.axis_index("dp"), lax.axis_index("row"), lax.axis_index("col")
    line_id, tier_id = dp_id // tier_count, dp_id % tier_count
    flips = [line_id, line_id + 1 - 2 * (line_id % 2), (line_id + 2) % 4, 3 - line_id]
    line = [(flip * tier_count + tier_id, row_id, col_id) for flip in flips]
    core = (dp_id, row_id + 1 - 2 * (row_id % 2), col_id)
    far = (dp_id, (row_id + 2) % 4, col_id)
    col = (dp_id, row_id, 1 - col_id)
    return line_id, flips, line, core, far, col

def meet(peers):
    barrier = pltpu.get_barrier_semaphore()
    for peer in peers:
        pl.semaphore_signal(barrier, inc=1, device_id=peer, device_id_type=pl.DeviceIdType.MESH)
    pl.semaphore_wait(barrier, len(peers))


CH = 2

def gather_kernel(tier_count, order, tok, cot, norm_ref, wq, wu, dh, x_out, b_out, wq_out, wu_out, d_out,
                  tz, cz, ty, xs, send_sems, recv_sems, local_sems):
    line_id, flips, line, core, far, col = neighbours(tier_count)
    bit = (line_id % 2 + lax.axis_index("col")) % 2
    middle = (line_id == 1) | (line_id == 2)
    rows, half = tok.shape
    chunk = rows // CH
    copies = Copies(send_sems, recv_sems)
    sent, mid_sent, local_left, last = [], [], [], []
    n_local = [0]

    def local(src, dst):
        copy = pltpu.make_async_copy(src, dst, local_sems.at[n_local[0]])
        n_local[0] += 1
        copy.start()
        local_left.append(copy)
        return copy

    def settle(copy):
        copy.wait()
        local_left[:] = [c for c in local_left if c is not copy]

    def send(src, dst, device, slot=None):
        copy = copies.make(src, dst, device, slot)
        copy.start()
        sent.append(copy)
        return copy

    def cut(c):
        return pl.ds(c * chunk, chunk)

    class Stream:
        def __init__(self, own, stage, out, normed):
            self.own, self.stage, self.out, self.normed = own, stage, out, normed
            self.line, self.swap, self.spread, self.keep, self.relayed = {}, {}, {}, {}, {}

        def start(self, c):
            own, stage = self.own.at[cut(c)], self.stage
            own_copy = local(own, stage.at[0, cut(c)])
            near = send(own, stage.at[1, cut(c)], line[1])
            two = send(own, stage.at[2, cut(c)], line[2])
            slot = copies.slot()
            three = copies.make(own, stage.at[3, cut(c)], line[3], slot)
            relay = copies.make(stage.at[2, cut(c)], stage.at[3, cut(c)], line[1], slot)
            pl.when(middle)(three.start)
            mid_sent.extend([three, relay])
            self.line[c] = own_copy, near, two, three, relay

        def swap_cols(self, c, p):
            own_copy, near, two, three, relay = self.line[c]
            if p == 0:
                settle(own_copy)
                near.wait_recv()
            else:
                two.wait_recv()
                pl.when(middle)(relay.start)
                three.wait_recv()
            if self.normed:
                dst = ty.at[p, cut(c)]
            else:
                dst = self.out.at[p, 0, cut(c), pl.ds(half, half)]
                self.keep[c, p] = local(self.stage.at[2 * p + bit, cut(c)], self.out.at[p, 0, cut(c), pl.ds(0, half)])
            self.swap[c, p] = send(self.stage.at[2 * p + 1 - bit, cut(c)], dst, col)

        def give(self, c, p):
            self.swap[c, p].wait_recv()
            if self.normed:
                norm(c, p)
                src = xs.at[p, cut(c)]
                local(src, self.out.at[p, 0, cut(c)])
            else:
                settle(self.keep[c, p])
                src = self.out.at[p, 0, cut(c)]
            self.spread[c, p] = send(src, self.out.at[p, 2, cut(c)], far)
            last.append(send(src, self.out.at[p, 1, cut(c)], core))

        def relay(self, c, p):
            self.spread[c, p].wait_recv()
            last.append(send(self.out.at[p, 2, cut(c)], self.out.at[p, 3, cut(c)], core))

    def norm(c, p):
        step = 64
        def body(i, carry):
            at = pl.ds(pl.multiple_of(c * chunk + i * step, step), step)
            one = tz[2 * p + bit, at, :].astype(f32)
            two = ty[p, at, :].astype(f32)
            width = 2 * half
            mean = (jnp.sum(one, axis=-1, keepdims=True) + jnp.sum(two, axis=-1, keepdims=True)) / width
            square = (jnp.sum(one * one, axis=-1, keepdims=True) + jnp.sum(two * two, axis=-1, keepdims=True)) / width
            inv = lax.rsqrt(square - mean * mean + eps_norm)
            xs[p, at, pl.ds(0, half)] = ((one - mean) * inv * norm_ref[0:1, 0:half] + norm_ref[1:2, 0:half]).astype(bf16)
            xs[p, at, pl.ds(half, half)] = ((two - mean) * inv * norm_ref[0:1, half:] + norm_ref[1:2, half:]).astype(bf16)
            return carry
        lax.fori_loop(0, chunk // step, body, 0)

    class Weight:
        def __init__(self, src, out):
            self.src, self.out, self.got = src, out, {}

        def own(self):
            local(self.src.at[line_id], self.out.at[0, line_id])
            last.append(send(self.src.at[line_id], self.out.at[1, line_id], col))

        def start(self):
            for s in (1, 2, 3):
                self.got[s] = send(self.src.at[flips[s]], self.out.at[0, line_id], line[s])

        def swap(self):
            for s in (1, 2, 3):
                self.got[s].wait_recv()
                last.append(send(self.out.at[0, flips[s]], self.out.at[1, flips[s]], col))

    part = dh.shape[0] // 5

    def dense(i):
        at = pl.ds(i * part, part)
        last.append(send(dh.at[at], d_out.at[at, pl.ds(half, half)], col))

    meet([line[1], line[2], line[3], core, far, col])
    T = Stream(tok, tz, x_out, True)
    C = Stream(cot, cz, b_out, False)
    Q = Weight(wq, wq_out)
    U = Weight(wu, wu_out)
    for what, *args in order:
        if what == "Ts": T.start(*args)
        if what == "Ty": T.swap_cols(*args)
        if what == "Tx": T.give(*args)
        if what == "Tk": T.relay(*args)
        if what == "Cs": C.start(*args)
        if what == "Cy": C.swap_cols(*args)
        if what == "Cx": C.give(*args)
        if what == "Ck": C.relay(*args)
        if what == "Qo": Q.own()
        if what == "Qs": Q.start()
        if what == "Qy": Q.swap()
        if what == "Uo": U.own()
        if what == "Us": U.start()
        if what == "Uy": U.swap()
        if what == "D": dense(*args)
        if what == "Dl": local(dh, d_out.at[:, pl.ds(0, half)])
    for copy in last:
        copy.wait_recv()
    for copy in list(local_left):
        settle(copy)
    for copy in sent:
        copy.wait_send()
    for copy in mid_sent:
        pl.when(middle)(copy.wait_send)

ORDER_A = [("Ts",0),("Ts",1),("Qo",),("Uo",),("D",0),("Dl",),
 ("Ty",0,0),("Ty",0,1),("Tx",0,0),("Tx",0,1),
 ("Ty",1,0),("Ty",1,1),("Cs",0),("Tx",1,0),("Tx",1,1),("D",1),("D",2),
 ("Tk",0,0),("Tk",0,1),("Cy",0,0),("Cy",0,1),("Qs",),("Cs",1),("Cx",0,0),("Cx",0,1),("Tk",1,0),("Tk",1,1),
 ("Qy",),("Cy",1,0),("Cy",1,1),("Us",),("Cx",1,0),("Cx",1,1),("D",3),("D",4),("Ck",0,0),("Ck",0,1),
 ("Uy",),("Ck",1,0),("Ck",1,1)]

def gather(tier_count, tok, cot, norm_vec, wq, wu, dh, order=ORDER_A):
    rows, half = tok.shape
    sds = jax.ShapeDtypeStruct
    any_ = pl.BlockSpec(memory_space=pl.ANY)
    return pl.pallas_call(
        functools.partial(gather_kernel, tier_count, order),
        out_shape=[sds((2, 4, rows, 2 * half), bf16), sds((2, 4, rows, 2 * half), bf16),
                   sds((2, *wq.shape), bf16), sds((2, *wu.shape), bf16), sds((dh.shape[0], 2 * half), bf16)],
        in_specs=[any_, any_, pl.BlockSpec(memory_space=pltpu.VMEM), any_, any_, any_],
        out_specs=[any_] * 5,
        scratch_shapes=[pltpu.VMEM((4, rows, half), bf16), pltpu.VMEM((4, rows, half), bf16), pltpu.VMEM((2, rows, half), bf16),
                        pltpu.VMEM((2, rows, 2 * half), bf16),
                        pltpu.SemaphoreType.DMA((80,)), pltpu.SemaphoreType.DMA((80,)), pltpu.SemaphoreType.DMA((24,))],
        compiler_params=pltpu.CompilerParams(collective_id=1, has_side_effects=True, vmem_limit_bytes=32 << 20),
    )(tok, cot, norm_vec, wq, wu, dh)


def per_device(
    tokens,
    cotangent,
    doc_lengths,
    doc_groups,
    w_qkv,
    w_up,
    w_dense,
    w_down,
    vectors,
    m_qkv,
    v_qkv,
    m_up,
    v_up,
    m_dense,
    v_dense,
    m_down,
    v_down,
    m_vec,
    v_vec,
):
    dp_count = lax.axis_size("dp")
    tier_count = dp_count // LINE
    dp_id = lax.axis_index("dp")
    line_id = dp_id // tier_count
    tier_id = dp_id % tier_count
    row_count = lax.axis_size("row")
    col_count = lax.axis_size("col")
    assert row_count == 4 and col_count == 2 and dp_count % LINE == 0
    row_id = lax.axis_index("row")
    col_id = lax.axis_index("col")
    tok_dev, half_width = tokens.shape
    slot_count = tok_dev * row_count
    full_width = half_width * col_count
    row_width = full_width // row_count
    part = row_width // LINE
    heads_dev = part // HDIM
    score_scale = HDIM ** (-0.5)
    zero_index = jnp.int32(0)
    tier_groups = [[line * tier_count + tier for tier in range(tier_count)] for line in range(LINE)]

    def over_line(value, bits):
        pairs = [(i, ((i // tier_count) ^ bits) * tier_count + i % tier_count) for i in range(dp_count)]
        return lax.ppermute(value, "dp", pairs)

    def over_row(value, bits):
        return lax.ppermute(value, "row", [(i, i ^ bits) for i in range(row_count)])

    def over_col(value):
        return lax.ppermute(value, "col", [(0, 1), (1, 0)])

    def reorder(blocks, place):
        one = (place & 1) == 1
        two = (place & 2) == 2
        blocks = [jnp.where(one, blocks[i ^ 1], blocks[i]) for i in range(4)]
        return [jnp.where(two, blocks[i ^ 2], blocks[i]) for i in range(4)]

    def sum_all(value):
        value = sum(reorder([value] + [over_line(value, s) for s in (1, 2, 3)], line_id))
        value = sum(reorder([value] + [over_row(value, s) for s in (1, 2, 3)], row_id))
        value = value + over_col(value)
        if tier_count > 1:
            value = lax.psum(value, "dp", axis_index_groups=tier_groups)
        return value

    odd = ((line_id & 1) ^ col_id) == 1
    first_bits = (line_id & 1) ^ col_id
    part_start = row_id * row_width + line_id * part
    col_start = col_id * half_width

    def by_half(vector):
        mine = lax.dynamic_slice_in_dim(vector, col_start, half_width, 0)
        other = lax.dynamic_slice_in_dim(vector, (1 - col_id) * half_width, half_width, 0)
        return jnp.concatenate([mine, other])

    places = jnp.concatenate(
        [(row_id ^ t) * tok_dev + jnp.arange(tok_dev, dtype=jnp.int32) for t in range(4)]
    )
    segments, cosines, sines = [], [], []
    for p in range(2):
        group_id = (line_id ^ first_bits ^ (2 * p)) * tier_count + tier_id
        segment, position, unused = seq_layout(doc_lengths, doc_groups, group_id, places)
        cos_part, sin_part = turn_angles(position)
        segments.append(segment)
        cosines.append(cos_part)
        sines.append(sin_part)
    cos_part = jnp.stack(cosines)
    sin_part = jnp.stack(sines)
    total_len = jnp.sum(jnp.where(doc_groups == dp_id, doc_lengths, 0), dtype=jnp.int32)
    own_valid = places[:tok_dev] < total_len
    back_own = jnp.where(own_valid[:, None], cotangent, jnp.zeros_like(cotangent))

    def tier_gather(value):
        if tier_count > 1:
            value = lax.all_gather(value, "dp", axis=0, tiled=True, axis_index_groups=tier_groups)
        return value

    def pieces_of(weight):
        low = tier_gather(weight.astype(bf16))
        rows, parts = low.shape[:2]
        return low.reshape(rows, parts, LINE, part).transpose(2, 0, 1, 3).reshape(LINE, rows, parts * part)

    down_low = tier_gather(w_down.astype(bf16)).transpose(1, 0, 2).reshape(4 * part, half_width)
    out_low = jnp.concatenate([tier_gather(w_dense.astype(bf16)), down_low], axis=0)
    norm_vec = jnp.stack([by_half(vectors[0]), by_half(vectors[1])])
    normed, back, qkv_mat, up_mat, out_mat = gather(
        tier_count, tokens, back_own, norm_vec, pieces_of(w_qkv), pieces_of(w_up), out_low
    )
    rows_all = 2 * slot_count
    normed = normed.reshape(rows_all, full_width)
    back = back.reshape(rows_all, full_width)
    qkv_mat = qkv_mat.reshape(full_width, 3 * part)
    up_mat = up_mat.reshape(full_width, 4 * part)
    dense_mat = out_mat[:part]
    down_mat = out_mat[part:]

    bias_qkv = lax.dynamic_slice(vectors[2:5], (zero_index, part_start), (3, part)).reshape(3 * part)
    bias_up = lax.dynamic_slice(vectors[5:9], (zero_index, part_start), (4, part)).reshape(4 * part)

    def mm(a, b):
        return jnp.dot(a, b, preferred_element_type=f32)

    def mm_t(a, b):
        return lax.dot_general(a, b, (((1,), (1,)), ((), ())), preferred_element_type=f32)

    def t_mm(a, b):
        return lax.dot_general(a, b, (((0,), (0,)), ((), ())), preferred_element_type=f32)

    pre_qkv = mm(normed, qkv_mat) + bias_qkv
    heads_view = pre_qkv.reshape(2, slot_count, 3, heads_dev, HDIM)
    queries = rotate(heads_view[:, :, 0], cos_part, sin_part).astype(bf16)
    key_rows = rotate(heads_view[:, :, 1], cos_part, sin_part).astype(bf16)
    values = heads_view[:, :, 2].astype(bf16)
    segment_all = jnp.stack(segments)
    allowed = (segment_all[:, :, None] == segment_all[:, None, :]) & (
        places[None, :, None] >= places[None, None, :]
    )

    def scores_of():
        scores = (
            jnp.einsum("pqhd,pkhd->phqk", queries, key_rows, preferred_element_type=f32) * score_scale
        )
        return jnp.where(allowed[:, None], scores, -1e30)

    scores = scores_of()
    top_score = jnp.max(scores, axis=-1, keepdims=True)
    weights = jnp.exp(scores - top_score)
    denominator = jnp.sum(weights, axis=-1, keepdims=True)
    probs_low = (weights / denominator).astype(bf16)
    attn = jnp.einsum("phqk,pkhd->pqhd", probs_low, values, preferred_element_type=f32)
    attn = attn.reshape(rows_all, part).astype(bf16)
    total = top_score + jnp.log(denominator)

    pre_up = mm(normed, up_mat) + bias_up
    hidden = jax.nn.gelu(pre_up, approximate=True).astype(bf16)

    def scatter_rows(partial):
        low = partial.astype(bf16).reshape(2, 4, tok_dev, full_width)
        kept = []
        for p in range(2):
            near = low[p, 0::2].astype(f32) + over_row(low[p, 1::2], 1).astype(f32)
            mine = near[0] + over_row(near[1].astype(bf16), 2).astype(f32)
            kept.append(mine.astype(bf16))
        out = None
        for p in (1, 0):
            mine = kept[p][:, :half_width]
            theirs = over_col(kept[p][:, half_width:])
            even_block = jnp.where(odd, theirs, mine)
            odd_block = jnp.where(odd, mine, theirs)
            first = over_line(even_block, 2) if p else even_block
            both = first.astype(f32) + over_line(odd_block, 2 * p + 1).astype(f32)
            out = both if out is None else out + both
        return out

    branch = scatter_rows(mm(attn, dense_mat) + mm(hidden, down_mat))
    out_bias = lax.dynamic_slice_in_dim(vectors[9] + vectors[10], col_start, half_width, 0)
    block_out = (tokens.astype(f32) + branch + out_bias[None, :]).astype(bf16)

    d_attn = mm_t(back, dense_mat).astype(bf16).reshape(2, slot_count, heads_dev, HDIM)
    d_hidden = mm_t(back, down_mat)
    unused_value, gelu_back = jax.vjp(lambda inputs: jax.nn.gelu(inputs, approximate=True), pre_up)
    d_pre_up = gelu_back(d_hidden)[0].astype(bf16)

    probs_full = jnp.exp(scores_of() - total)
    probs_back = probs_full.astype(bf16)
    d_probs = jnp.einsum("pqhd,pkhd->phqk", d_attn, values, preferred_element_type=f32)
    delta_rows = jnp.sum(probs_full * d_probs, axis=-1, keepdims=True)
    d_scores = (probs_full * (d_probs - delta_rows)).astype(bf16)
    d_queries = jnp.einsum("phqk,pkhd->pqhd", d_scores, key_rows, preferred_element_type=f32) * score_scale
    d_keys = jnp.einsum("phqk,pqhd->pkhd", d_scores, queries, preferred_element_type=f32) * score_scale
    d_values = jnp.einsum("phqk,pqhd->pkhd", probs_back, d_attn, preferred_element_type=f32)
    d_qkv = jnp.stack(
        [rotate(d_queries, cos_part, -sin_part), rotate(d_keys, cos_part, -sin_part), d_values], axis=2
    )
    d_qkv = d_qkv.astype(bf16).reshape(rows_all, 3 * part)

    def scatter_out(grad):
        return grad[:, :half_width] + over_col(grad[:, half_width:].astype(bf16)).astype(f32)

    def tier_sum(value):
        if tier_count > 1:
            value = lax.psum_scatter(
                value, "dp", scatter_dimension=0, tiled=True, axis_index_groups=tier_groups
            )
        return value

    red_dense = tier_sum(scatter_out(t_mm(attn, back)))
    red_down = scatter_out(t_mm(hidden, back)).reshape(4, part, half_width).transpose(1, 0, 2)
    red_down = tier_sum(red_down)

    def scatter_in(grad, parts):
        half = grad[:half_width] + over_col(grad[half_width:].astype(bf16)).astype(f32)
        low = half.astype(bf16)
        rows = half_width // LINE
        pieces = []
        for s in range(LINE):
            piece = lax.dynamic_slice_in_dim(low, (line_id ^ s) * rows, rows, 0)
            piece = over_line(piece, s) if s else piece
            pieces.append(piece.reshape(rows, parts, part))
        own = jnp.concatenate(reorder(pieces, line_id), axis=2)
        return tier_sum(own.astype(f32))

    red_up = scatter_in(t_mm(normed, d_pre_up), 4)
    red_qkv = scatter_in(t_mm(normed, d_qkv), 3)

    d_normed = scatter_rows(mm_t(d_qkv, qkv_mat) + mm_t(d_pre_up, up_mat))
    tokens_own = tokens.astype(f32)
    own_sums = jnp.stack([jnp.sum(tokens_own, axis=-1), jnp.sum(tokens_own * tokens_own, axis=-1)])
    own_sums = (own_sums + over_col(own_sums)) / full_width
    mean_own = own_sums[0][:, None]
    inv_own = lax.rsqrt(own_sums[1][:, None] - mean_own * mean_own + eps_norm)
    centred = (tokens_own - mean_own) * inv_own
    gain_cols = lax.dynamic_slice_in_dim(vectors[0], col_start, half_width, 0)
    d_hat = d_normed * gain_cols[None, :]
    hat_sums = jnp.stack([jnp.sum(d_hat, axis=-1), jnp.sum(d_hat * centred, axis=-1)])
    hat_sums = (hat_sums + over_col(hat_sums)) / full_width
    back_float = back_own.astype(f32)
    grad_tokens = inv_own * (d_hat - hat_sums[0][:, None] - centred * hat_sums[1][:, None]) + back_float

    early = jnp.zeros((9, full_width), f32)
    early = lax.dynamic_update_slice(
        early, jnp.sum(d_qkv.astype(f32), axis=0).reshape(3, part), (zero_index, part_start)
    )
    early = lax.dynamic_update_slice(
        early, jnp.sum(d_pre_up.astype(f32), axis=0).reshape(4, part), (jnp.int32(3), part_start)
    )
    out_sums = jnp.sum(back_float, axis=0)
    early = lax.dynamic_update_slice(early, jnp.stack([out_sums, out_sums]), (jnp.int32(7), col_start))
    late = lax.dynamic_update_slice(
        jnp.zeros((2, full_width), f32),
        jnp.stack([jnp.sum(d_normed * centred, axis=0), jnp.sum(d_normed, axis=0)]),
        (zero_index, col_start),
    )
    vec_grad = jnp.concatenate([sum_all(late), sum_all(early)], axis=0)
    qkv_new = adamw(w_qkv, m_qkv, v_qkv, red_qkv, D ** (-0.5), 0.1)
    up_new = adamw(w_up, m_up, v_up, red_up, D ** (-0.5), 0.1)
    dense_new = adamw(w_dense, m_dense, v_dense, red_dense, max(D // 128, 4) ** (-0.5), 0.1)
    down_new = adamw(w_down, m_down, v_down, red_down, FF ** (-0.5), 0.1)
    vec_new = adamw(vectors, m_vec, v_vec, vec_grad, 0.5, 0.0)
    return (
        block_out,
        grad_tokens,
        qkv_new[0],
        qkv_new[1],
        qkv_new[2],
        up_new[0],
        up_new[1],
        up_new[2],
        dense_new[0],
        dense_new[1],
        dense_new[2],
        down_new[0],
        down_new[1],
        down_new[2],
        vec_new[0],
        vec_new[1],
        vec_new[2],
    )


def solution(mesh):
    placed = (
        P(("dp", "row"), "col"),
        P(("dp", "row"), "col"),
        P(),
        P(),
        P(("col", "dp"), None, "row"),
        P(("col", "dp"), None, "row"),
        P(("row", "dp"), "col"),
        P(("row", "dp"), None, "col"),
        P(),
        P(("col", "dp"), None, "row"),
        P(("col", "dp"), None, "row"),
        P(("col", "dp"), None, "row"),
        P(("col", "dp"), None, "row"),
        P(("row", "dp"), "col"),
        P(("row", "dp"), "col"),
        P(("row", "dp"), None, "col"),
        P(("row", "dp"), None, "col"),
        P(),
        P(),
    )
    return jax.shard_map(
        per_device,
        mesh=mesh,
        in_specs=placed,
        out_specs=(
            P(("dp", "row"), "col"),
            P(("dp", "row"), "col"),
            P(("col", "dp"), None, "row"),
            P(("col", "dp"), None, "row"),
            P(("col", "dp"), None, "row"),
            P(("col", "dp"), None, "row"),
            P(("col", "dp"), None, "row"),
            P(("col", "dp"), None, "row"),
            P(("row", "dp"), "col"),
            P(("row", "dp"), "col"),
            P(("row", "dp"), "col"),
            P(("row", "dp"), None, "col"),
            P(("row", "dp"), None, "col"),
            P(("row", "dp"), None, "col"),
            P(),
            P(),
            P(),
        ),
        check_vma=False,
    )
```

time: 1550 us -> 719 us (0.46)
  waiting for transfers between devices: 1280 us -> 203 us
  Pallas kernels: 0 us -> 133 us
  starting transfers between devices: 1.91 us -> 72.9 us
  local copies, waits for them, and re-layouts: 50 us -> 80.1 us
  other arithmetic: 61.3 us -> 86.3 us
    reduce_scatter x10 -> x0, waiting for transfers between devices: 709 us -> none  [the longest x1 144 us: per_device(): lax.psum_scatter(g_up, 'dp', scatter_dimension=0, tiled=True)]
    all_gather x11 -> x0, waiting for transfers between devices: 447 us -> none  [the longest x1 78.5 us: per_device(): lax.all_gather(w_up.astype(jnp.bfloat16), 'dp', axis=0, tiled=True)]
    ppermute x0 -> x44, waiting for transfers between devices: none -> 203 us  [the longest x14 78.3 us: over_row(): return lax.ppermute(value, 'row', [(i, i ^ bits) for i in range(row_count)])]
    pallas_call x0 -> x1, Pallas kernels: none -> 133 us  [gather(): pl.pallas_call(functools.partial(gather_kernel, tier_count, order), out_s...]
    psum x1 -> x0, waiting for transfers between devices: 125 us -> none  [per_device(): vec_grad = lax.psum(vec_part, ('dp', 'row', 'col'))]
    ppermute x0 -> x44, starting transfers between devices: none -> 72.9 us  [the longest x18 49.3 us: over_line(): return lax.ppermute(value, 'dp', pairs)]
    unnamed x97 -> x138, local copies, waits for them, and re-layouts: 41 us -> 21 us
    dot_general x24 -> x18, matrix products: 120 us -> 131 us  [the longest x4 38.9 us: mm_t(): lax.dot_general(a, b, (((1,), (1,)), ((), ())), preferred_element_type=f32)]
  transfers between devices with their start and end apart: 22 -> 44, of which waited for: 21 -> 16; matrix products, arithmetic and copies ran while one was open for 13% -> 21% of each run, Pallas kernels for 0% -> 0%
where the time goes in v1:
time: 719 us; the launch traced here: 708 us
  waiting for transfers between devices  203 us (28%)
  Pallas kernels  133 us (18%)
  matrix products  131 us (18%)
  other arithmetic  86.3 us (12%)
  local copies, waits for them, and re-layouts  80.1 us (11%)
  starting transfers between devices  72.9 us (10%)
    pallas_call x1, Pallas kernels, gather(): pl.pallas_call(functools.partial(gather_kernel, tier_count, order), out_s...  133 us
    ppermute x14, waiting for transfers between devices, over_row(): return lax.ppermute(value, 'row', [(i, i ^ bits) for i in range(row_count)])  78.3 us
    ppermute x18, waiting for transfers between devices, over_line(): return lax.ppermute(value, 'dp', pairs)  65.5 us
    ppermute x12, waiting for transfers between devices, over_col(): return lax.ppermute(value, 'col', [(0, 1), (1, 0)])  59.2 us
    ppermute x18, starting transfers between devices, over_line(): return lax.ppermute(value, 'dp', pairs)  49.3 us
    dot_general x4, matrix products, mm_t(): lax.dot_general(a, b, (((1,), (1,)), ((), ())), preferred_element_type=f32)  38.9 us
    dot_general x4, matrix products, mm(): return jnp.dot(a, b, preferred_element_type=f32)  32.2 us
    sub x5, other arithmetic, adamw(): return (first_next, second_next, weight - rate * (update + decay * weight))  22.2 us
  transfers between devices with their start and end apart: 44, of which 16 were waited for; matrix products, arithmetic and copies ran while one was open for 21% of the time, Pallas kernels for 0%

profile of v1, /device:TPU:0, one launch (start us, length us, event | category | flops | bytes accessed | tf_op | source)
XLA Modules:
  0.0 708.5 jit_solution(10646896859365481755)
XLA Ops:
  6.1 2.1 convert_bitcast_fusion
  19.4 132.8 %shard_map.314 = (bf16[2,4,256,2048]{3,2,1,0:T(8,128)(2,1)S(1)}, bf16[2,4,256,2048]{3,2,1,0:T(8,128)(2,1)}, bf16[2,4,256,384]{3,2,1,0:T(8,128)(2,1)S(1)}, bf16[2...) custom-call(bf16[256,1024]{1,0:T(8,128)(2,1)S(1)} %copy-done, bf16[256,1024]{1,0:T(8,128)(2,1)S(1)} %get-tuple-element.43.cot, ...), custom_call_target="tpu_custom_call" | custom-call | tf_op jit(solution)/shard_map/pallas_call | solution.py:269
  156.1 2.7 copy-done.6
  158.7 6.3 convolution_add_fusion
  165.0 7.2 %reshape.641 = f32[2,1024,3,2,64]{4,3,2,1,0:T(2,128)} reshape(f32[2048,384]{1,0:T(8,128)} %convolution_add_fusion) | data formatting | bytes 6291456 | tf_op jit(solution)/shard_map/reshape | solution.py:411
  172.2 3.8 fusion.90
  176.0 3.3 slice.250
  179.3 3.9 copy.145
  183.2 2.1 copy.146
  192.5 1.9 compare_and_fusion
  194.4 7.7 %fusion.94 = (f32[2,2,1024]{2,1,0:T(2,128)S(1)}, f32[2,2,1024,1024]{2,3,1,0:T(8,128)}) fusion(bf16[2,1024,2,32]{1,3,2,0:T(8,128)(2,1)S(1)} %slice.393, bf16[2,1024,2,16]{1,3,2,0:T(8,128)(2,1)S(1)} %get-tuple-element.103, bf16[2,1024,2,16]{1,3,2,0:T(8,128)(2,1)S(1)} %get-tuple-element.104, bf16[2,1024,2,32]{1,3,2,0:T(8,128)(2,1)S(1)} %slice.394, ...), kind=kOutput, calls=%fused_computation.253 | convolution fusion | flops 552595456 | bytes 19939328 | tf_op jit(solution)/shard_map/pqhd,pkhd->phqk/dot_general | solution.py:422
  202.2 8.1 %fusion = f32[2,2,1024]{2,1,0:T(2,128)S(1)} fusion(f32[2,2,1024,1024]{2,3,1,0:T(8,128)} %get-tuple-element.135, f32[2,2,1024]{2,1,0:T(2,128)S(1)} %get-tuple-element.134), kind=kLoop, calls=%fused_computation.8 | loop fusion | flops 8384512 | bytes 16809984 | tf_op jit(solution)/shard_map/reduce_sum | solution.py:429
  211.1 6.0 convolution_convert_fusion
  218.2 10.7 %multiply_reduce_fusion = (f32[2,2,1024]{2,1,0:T(2,128)S(1)}, f32[2,2,1024,1024]{2,3,1,0:T(8,128)}) fusion(f32[2,2,1024,1024]{2,3,1,0:T(8,128)} %get-tuple-element.135, f32[2,2,1024]{2,1,0:T(2,128)S(1)} %log_add_fusion, bf16[2,1024,2,64]{1,3,2,0:T(8,128)(2,1)S(1)} %copy.121, bf16[2,1024,1,2,64]{1,4,3,0,2:T(8,128)(2,1)S(1)} %copy.144), kind=kOutput, calls=%fused_computation.2 | convolution fusion | flops 549449728 | bytes 34635776 | tf_op jit(solution)/shard_map/pqhd,pkhd->phqk/dot_general | solution.py:467
  229.0 12.6 %multiply_convert_fusion = bf16[2,2,1024,1024]{2,3,1,0:T(8,128)(2,1)S(1)} fusion(f32[2,2,1024,1024]{2,3,1,0:T(8,128)} %get-tuple-element.137, f32[2,2,1024,1024]{2,3,1,0:T(8,128)} %get-tuple-element.135, f32[2,2,1024]{2,1,0:T(2,128)S(1)} %get-tuple-element.136, f32[2,2,1024]{2,1,0:T(2,128)S(1)} %log_add_fusion), kind=kLoop, calls=%fused_computation.1 | loop fusion | flops 16777216 | bytes 41975808 | tf_op jit(solution)/shard_map/convert_element_type | solution.py:469
  243.3 2.7 fusion.35
  245.9 8.6 %fusion.41 = bf16[2,1024,1,2,64]{1,4,3,0,2:T(8,128)(2,1)S(1)} fusion(bf16[2,1024,2,64]{1,3,2,0:T(8,128)(2,1)S(1)} %copy.121, f32[2,2,1024,1024]{2,3,1,0:T(8,128)} %get-tuple-element.135, f32[2,2,1024]{2,1,0:T(2,128)S(1)} %log_add_fusion), kind=kOutput, calls=%fused_computation.94 | convolution fusion | flops 545521664 | bytes 17842176 | tf_op jit(solution)/shard_map/phqk,pqhd->pkhd/dot_general | solution.py:472
  256.2 6.2 fusion.95
  263.9 14.0 %convert_reduce_fusion = (f32[512]{0:T(512)S(1)}, bf16[2048,512]{1,0:T(8,128)(2,1)}) fusion(f32[2048,512]{1,0:T(8,128)} %fusion.95, f32[512]{0:T(512)S(1)} %fusion.71, bf16[2048,2048]{1,0:T(8,128)(2,1)} %bitcast.193, bf16[640,2048]{1,0:T(8,128)(2,1)} %copy-done.4), kind=kOutput, calls=%fused_computation.27 | convolution fusion | flops 4319084032 | bytes 16781312 | tf_op jit(solution)/shard_map/dot_general | solution.py:405
  280.3 4.0 collective-permute-start.38
  284.3 3.0 copy.126
  289.0 8.8 %fusion.96 = f32[2048,2048]{1,0:T(8,128)} fusion(bf16[2048,512]{1,0:T(8,128)(2,1)S(1)} %copy-done.55, bf16[2048,512]{1,0:T(8,128)(2,1)S(1)} %bitcast.185), kind=kOutput, calls=%fused_computation.255 | convolution fusion | flops 4294967296 | bytes 20971520 | tf_op jit(solution)/shard_map/dot_general | solution.py:405
  297.7 10.3 %add_convert_fusion = bf16[2048,2048]{1,0:T(8,128)(2,1)} fusion(f32[2048,2048]{1,0:T(8,128)} %fusion.96, bf16[2048,384]{0,1:T(8,128)(2,1)S(1)} %bitcast.198, bf16[2048,384]{1,0:T(8,128)(2,1)S(1)} %bitcast.175), kind=kOutput, calls=%fused_computation | convolution fusion | flops 3229614080 | bytes 28311552 | tf_op jit(solution)/shard_map/dot_general | solution.py:405
  308.0 4.9 slice_bitcast_fusion.5
  313.1 2.2 collective-permute-start.9
  315.3 8.2 %fusion.44 = bf16[2,1024,2,64]{1,3,2,0:T(8,128)(2,1)S(1)} fusion(f32[2,2,1024,1024]{2,3,1,0:T(8,128)} %get-tuple-element.135, f32[2,2,1024]{2,1,0:T(2,128)S(1)} %copy-done.48, f32[2,2,1024]{2,1,0:T(2,128)S(1)} %copy-done.46, bf16[2,1024,1,2,64]{1,4,3,0,2:T(8,128)(2,1)S(1)} %copy-done.23), kind=kOutput, calls=%fused_computation.95 | convolution fusion | flops 549715968 | bytes 17858560 | tf_op jit(solution)/shard_map/phqk,pkhd->pqhd/dot_general | solution.py:431
  323.5 6.2 fusion.97
  329.8 5.2 fusion.99
  335.0 11.7 %fusion.28 = f32[2048,2048]{1,0:T(8,128)} fusion(bf16[640,2048]{1,0:T(8,128)(2,1)S(1)} %copy-done.5, f32[2048,512]{1,0:T(8,128)} %fusion.95, f32[512]{0:T(512)S(1)} %fusion.71), kind=kOutput, calls=%fused_computation.72 | convolution fusion | flops 4305453056 | bytes 23070720 | tf_op jit(solution)/shard_map/dot_general | solution.py:402
  346.6 6.6 fusion.79
  353.9 2.3 fusion.98
  356.2 8.1 %add_convert_fusion.1 = bf16[2048,2048]{1,0:T(8,128)(2,1)S(1)} fusion(f32[2048,2048]{1,0:T(8,128)} %fusion.28, bf16[2048,128]{0,1:T(8,128)(2,1)S(1)} %bitcast.202, bf16[640,2048]{1,0:T(8,128)(2,1)S(1)} %copy-done.5), kind=kOutput, calls=%fused_computation.4 | convolution fusion | flops 1082130432 | bytes 26214400 | tf_op jit(solution)/shard_map/dot_general | solution.py:402
  364.4 3.0 slice_bitcast_fusion.7
  370.3 2.7 slice.388
  374.5 2.7 slice.387
  380.7 3.6 collective-permute-done.40
  389.6 38.2 %collective-permute-done.43 = f32[9,2048]{1,0:T(8,128)S(1)} collective-permute-done((f32[9,2048]{1,0:T(8,128)S(1)}, f32[9,2048]{1,0:T(8,128)S(1)}, u32[]{:S(2)}, u32[]{:S(2)}) %collective-permute-start.43) | collective-permute-done | bytes 73760 | tf_op jit(solution)/shard_map/ppermute | solution.py:331
  427.9 1.8 fusion.34
  430.2 2.0 collective-permute-start.22
  432.2 2.1 collective-permute-start.23
  435.8 3.9 collective-permute-done.21
  439.6 9.3 %collective-permute-done.22 = bf16[256,384]{0,1:T(8,128)(2,1)S(1)} collective-permute-done((bf16[256,384]{0,1:T(8,128)(2,1)S(1)}, bf16[256,384]{0,1:T(8,128)(2,1)S(1)}, u32[]{:S(2)}, u32[]{:S(2)}) %collective-permute-start.22) | collective-permute-done | bytes 196640 | tf_op jit(solution)/shard_map/ppermute | solution.py:325
  451.9 5.2 multiply_subtract_fusion.2
  460.3 12.6 %collective-permute-done.29 = bf16[512,1024]{1,0:T(8,128)(2,1)} collective-permute-done((bf16[512,1024]{1,0:T(8,128)(2,1)}, bf16[512,1024]{1,0:T(8,128)(2,1)}, u32[]{:S(2)}, u32[]{:S(2)}) %collective-permute-start.29) | collective-permute-done | bytes 1048608 | tf_op jit(solution)/shard_map/ppermute | solution.py:331
  475.4 7.1 %multiply_subtract_fusion = (f32[128,4,1024]{2,1,0:T(4,128)}, f32[128,4,1024]{2,1,0:T(4,128)}, f32[128,4,1024]{2,1,0:T(4,128)}) fusion(f32[128,4,1024]{2,1,0:T(4,128)S(1)} %copy-done.11, f32[4,128,1024]{2,1,0:T(8,128)S(1)} %bitcast.200, f32[128,4,1024]{2,1,0:T(4,128)S(1)} %copy-done.24, f32[128,4,1024]{2,1,0:T(4,128)S(1)} %copy-done.25), kind=kLoop, calls=%fused_computation.62 | loop fusion | flops 7864320 | bytes 14680064 | tf_op jit(solution)/shard_map/sub | solution.py:72
  485.8 1.8 copy.131
  492.1 7.6 %multiply_subtract_fusion.1 = (f32[256,4,512]{2,1,0:T(4,128)}, f32[256,4,512]{2,1,0:T(4,128)}, f32[256,4,512]{2,1,0:T(4,128)}) fusion(f32[256,4,512]{2,1,0:T(4,128)S(1)} %copy-done.13, bf16[256,4,128]{2,1,0:T(4,128)(2,1)} %copy.134, bf16[256,4,128]{2,1,0:T(4,128)(2,1)} %copy.133, bf16[256,4,128]{2,1,0:T(4,128)(2,1)} %copy.132, ...), kind=kLoop, calls=%fused_computation.63 | loop fusion | flops 12058624 | bytes 13631488 | tf_op jit(solution)/shard_map/sub | solution.py:72
  499.8 5.5 convert_add_fusion.1
  506.5 2.7 collective-permute-start.11
  510.3 5.9 convert_add_fusion.3
  517.9 2.1 collective-permute-start.1
  520.2 13.3 %collective-permute-done.11 = bf16[256,2048]{1,0:T(8,128)(2,1)} collective-permute-done((bf16[256,2048]{1,0:T(8,128)(2,1)}, bf16[256,2048]{1,0:T(8,128)(2,1)}, u32[]{:S(2)}, u32[]{:S(2)}) %collective-permute-start.11) | collective-permute-done | bytes 1048608 | tf_op jit(solution)/shard_map/ppermute | solution.py:328
  536.5 19.5 %collective-permute-done.16 = bf16[256,2048]{1,0:T(8,128)(2,1)} collective-permute-done((bf16[256,2048]{1,0:T(8,128)(2,1)}, bf16[256,2048]{1,0:T(8,128)(2,1)}, u32[]{:S(2)}, u32[]{:S(2)}) %collective-permute-start.16) | collective-permute-done | bytes 1048608 | tf_op jit(solution)/shard_map/ppermute | solution.py:328
  559.0 19.4 %collective-permute-done.1 = bf16[256,2048]{1,0:T(8,128)(2,1)S(1)} collective-permute-done((bf16[256,2048]{1,0:T(8,128)(2,1)S(1)}, bf16[256,2048]{1,0:T(8,128)(2,1)S(1)}, u32[]{:S(2)}, u32[]{:S(2)}) %collective-permute-start.1) | collective-permute-done | bytes 1048608 | tf_op jit(solution)/shard_map/ppermute | solution.py:328
  580.1 19.0 %collective-permute-done.6 = bf16[256,2048]{1,0:T(8,128)(2,1)S(1)} collective-permute-done((bf16[256,2048]{1,0:T(8,128)(2,1)S(1)}, bf16[256,2048]{1,0:T(8,128)(2,1)S(1)}, u32[]{:S(2)}, u32[]{:S(2)}) %collective-permute-start.6) | collective-permute-done | bytes 1048608 | tf_op jit(solution)/shard_map/ppermute | solution.py:328
  601.6 2.4 collective-permute-start.14
  606.3 5.4 collective-permute-done.7
  612.3 48.0 %collective-permute-done.13 = bf16[256,1024]{1,0:T(8,128)(2,1)S(1)} collective-permute-done((bf16[256,1024]{1,0:T(8,128)(2,1)S(1)}, bf16[256,1024]{1,0:T(8,128)(2,1)S(1)}, u32[]{:S(2)}, u32[]{:S(2)}) %collective-permute-start.13) | collective-permute-done | bytes 524320 | tf_op jit(solution)/shard_map/ppermute | solution.py:325
  662.5 12.3 %collective-permute-start.31 = (f32[2,2048]{1,0:T(2,128)S(1)}, f32[2,2048]{1,0:T(2,128)S(1)}, u32[]{:S(2)}, u32[]{:S(2)}) collective-permute-start(f32[2,2048]{1,0:T(2,128)S(1)} %maximum_dynamic-update-slice_fusion), channel_id=1, source_target_pairs={{0,16},{8,24},{16,0},{24,8},{1,17},{9,25},{17,1},{25,9},{2,18},{10... | collective-permute-start | bytes 49160 | tf_op jit(solution)/shard_map/ppermute | solution.py:325
  674.8 19.7 %collective-permute-start.8 = (bf16[256,1024]{1,0:T(8,128)(2,1)S(1)}, bf16[256,1024]{1,0:T(8,128)(2,1)S(1)}, u32[]{:S(2)}, u32[]{:S(2)}) collective-permute-start(bf16[256,1024]{1,0:T(8,128)(2,1)S(1)} %broadcast_select_fusion.4), channel_id=1, source_target_pairs={{0,8},{8,0},{16,24},{24,16},{1,9},{9,1},{17,25},{25,17},{2,10},{10... | collective-permute-start | bytes 1572872 | tf_op jit(solution)/shard_map/ppermute | solution.py:325
  695.1 3.0 collective-permute-done.19
  699.8 2.0 collective-permute-done.34
  702.5 2.8 collective-permute-done.8
  705.3 1.9 convert_add_fusion.5
  (311 shorter events, 93.6 us)
Async XLA Ops:
  192.4 9.7 %copy-start.30 = (bf16[2,1024,2,16]{1,3,2,0:T(8,128)(2,1)}, bf16[2,1024,2,16]{1,3,2,0:T(8,128)(2,1)S(1)}, u32[]{:S(2)}) copy-start(bf16[2,1024,2,16]{1,3,2,0:T(8,128)(2,1)S(1)} %get-tuple-element.89) | copy-start | bytes 393220
  228.9 12.6 %copy-start.29 = (bf16[2,1024,2,32]{1,3,2,0:T(8,128)(2,1)S(1)}, bf16[2,1024,2,32]{1,3,2,0:T(8,128)(2,1)}, u32[]{:S(2)}) copy-start(bf16[2,1024,2,32]{1,3,2,0:T(8,128)(2,1)} %copy-done.28) | copy-start | bytes 786436
  229.0 12.6 %copy-start.35 = (bf16[2,1024,2,16]{1,3,2,0:T(8,128)(2,1)S(1)}, bf16[2,1024,2,16]{1,3,2,0:T(8,128)(2,1)}, u32[]{:S(2)}) copy-start(bf16[2,1024,2,16]{1,3,2,0:T(8,128)(2,1)} %copy-done.34) | copy-start | bytes 393220
  229.0 12.6 %copy-start.37 = (bf16[2,1024,2,16]{1,3,2,0:T(8,128)(2,1)S(1)}, bf16[2,1024,2,16]{1,3,2,0:T(8,128)(2,1)}, u32[]{:S(2)}) copy-start(bf16[2,1024,2,16]{1,3,2,0:T(8,128)(2,1)} %copy-done.36) | copy-start | bytes 393220
  243.2 12.6 %slice-start = ((s8[8388608]{0:T(1024)(128)(4,1)}), s8[4194304]{0:T(1024)(128)(4,1)S(1)}, s32[]{:S(2)}) async-start(s8[8388608]{0:T(1024)(128)(4,1)} %bitcast.177), calls=%async_computation | async-start | bytes 8388608
  245.9 9.8 %copy-start.38 = (f32[2,1024,16]{1,2,0:T(8,128)S(1)}, f32[2,1024,16]{1,2,0:T(8,128)}, u32[]{:S(2)}) copy-start(f32[2,1024,16]{1,2,0:T(8,128)} %get-tuple-element.105) | copy-start | bytes 393220
  245.9 9.9 %slice-start.1 = ((s8[8388608]{0:T(1024)(128)(4,1)}), s8[4194304]{0:T(1024)(128)(4,1)S(1)}, s32[]{:S(2)}) async-start(s8[8388608]{0:T(1024)(128)(4,1)} %bitcast.177), calls=%async_computation.1 | async-start | bytes 8388608
  279.7 98.1 %collective-permute-start.37 = (f32[9,2048]{1,0:T(8,128)S(1)}, f32[9,2048]{1,0:T(8,128)S(1)}, u32[]{:S(2)}, u32[]{:S(2)}) collective-permute-start(f32[9,2048]{1,0:T(8,128)S(1)} %dynamic_update_slice.15), channel_id=1, source_target_pairs={{0,24},{8,16},{16,8},{24,0},{1,25},{9,17},{17,9},{25,1},{2,26},{10... | collective-permute-start | bytes 221192 | tf_op jit(solution)/shard_map/ppermute | solution.py:325
  280.3 97.5 %collective-permute-start.38 = (f32[9,2048]{1,0:T(8,128)S(1)}, f32[9,2048]{1,0:T(8,128)S(1)}, u32[]{:S(2)}, u32[]{:S(2)}) collective-permute-start(f32[9,2048]{1,0:T(8,128)S(1)} %dynamic_update_slice.15), channel_id=1, source_target_pairs={{0,16},{8,24},{16,0},{24,8},{1,17},{9,25},{17,1},{25,9},{2,18},{10... | collective-permute-start | bytes 221192 | tf_op jit(solution)/shard_map/ppermute | solution.py:325
  284.3 93.5 %collective-permute-start.39 = (f32[9,2048]{1,0:T(8,128)S(1)}, f32[9,2048]{1,0:T(8,128)}, u32[]{:S(2)}, u32[]{:S(2)}) collective-permute-start(f32[9,2048]{1,0:T(8,128)S(1)} %dynamic_update_slice.15), channel_id=1, source_target_pairs={{0,8},{8,0},{16,24},{24,16},{1,9},{9,1},{17,25},{25,17},{2,10},{10... | collective-permute-start | bytes 221192 | tf_op jit(solution)/shard_map/ppermute | solution.py:325
  312.8 186.9 %collective-permute-start.10 = (bf16[2,256,2048]{2,1,0:T(8,128)(2,1)}, bf16[2,256,2048]{2,1,0:T(8,128)(2,1)}, u32[]{:S(2)}, u32[]{:S(2)}) collective-permute-start(bf16[2,256,2048]{2,1,0:T(8,128)(2,1)} %get-tuple-element.65), channel_id=1, source_target_pairs={{0,2},{2,0},{4,6},{6,4},{1,3},{3,1},{5,7},{7,5},{8,10},{10,8},{12,... | collective-permute-start | bytes 6291464 | tf_op jit(solution)/shard_map/ppermute | solution.py:328
  313.1 10.4 %slice-start.2 = ((s8[8388608]{0:T(1024)(128)(4,1)}), s8[4194304]{0:T(1024)(128)(4,1)S(1)}, s32[]{:S(2)}) async-start(s8[8388608]{0:T(1024)(128)(4,1)} %bitcast.180), calls=%async_computation.2 | async-start | bytes 8388608
  313.1 10.4 %slice-start.3 = ((s8[8388608]{0:T(1024)(128)(4,1)}), s8[4194304]{0:T(1024)(128)(4,1)S(1)}, s32[]{:S(2)}) async-start(s8[8388608]{0:T(1024)(128)(4,1)} %bitcast.180), calls=%async_computation.3 | async-start | bytes 8388608
  313.1 10.4 %copy-start.56 = (bf16[2048,512]{1,0:T(8,128)(2,1)S(1)}, bf16[2048,512]{1,0:T(8,128)(2,1)}, u32[]{:S(2)}) copy-start(bf16[2048,512]{1,0:T(8,128)(2,1)} %get-tuple-element.139) | copy-start | bytes 6291460
  313.1 64.1 %collective-permute-start.9 = (f32[2,256]{1,0:T(2,128)S(1)}, f32[2,256]{1,0:T(2,128)S(1)}, u32[]{:S(2)}, u32[]{:S(2)}) collective-permute-start(f32[2,256]{1,0:T(2,128)S(1)} %pad_maximum_fusion.17), channel_id=1, source_target_pairs={{0,1},{1,0},{2,3},{3,2},{4,5},{5,4},{6,7},{7,6},{8,9},{9,8},{10,11... | collective-permute-start | bytes 6152 | tf_op jit(solution)/shard_map/ppermute | solution.py:331
  329.8 16.9 %slice-start.6 = ((s8[8388608]{0:T(1024)(128)(4,1)}), s8[4194304]{0:T(1024)(128)(4,1)S(1)}, s32[]{:S(2)}) async-start(s8[8388608]{0:T(1024)(128)(4,1)} %bitcast.194), calls=%async_computation.6 | async-start | bytes 8388608
  335.0 11.7 %slice-start.7 = ((s8[8388608]{0:T(1024)(128)(4,1)}), s8[4194304]{0:T(1024)(128)(4,1)S(1)}, s32[]{:S(2)}) async-start(s8[8388608]{0:T(1024)(128)(4,1)} %bitcast.194), calls=%async_computation.7 | async-start | bytes 8388608
  335.0 11.7 %copy-start.57 = (f32[2048,512]{1,0:T(8,128)S(1)}, f32[2048,512]{1,0:T(8,128)}, u32[]{:S(2)}) copy-start(f32[2048,512]{1,0:T(8,128)} %fusion.95) | copy-start | bytes 12582916
  377.3 50.6 %collective-permute-start.20 = (bf16[1024,384]{0,1:T(8,128)(2,1)S(1)}, bf16[1024,384]{0,1:T(8,128)(2,1)S(1)}, u32[]{:S(2)}, u32[]{:S(2)}) collective-permute-start(bf16[1024,384]{0,1:T(8,128)(2,1)S(1)} %slice.389), channel_id=1, source_target_pairs={{0,1},{1,0},{2,3},{3,2},{4,5},{5,4},{6,7},{7,6},{8,9},{9,8},{10,11... | collective-permute-start | bytes 2359304 | tf_op jit(solution)/shard_map/ppermute | solution.py:331
  378.8 5.6 collective-permute-start.40
  379.2 8.3 %collective-permute-start.41 = (f32[9,2048]{1,0:T(8,128)S(1)}, f32[9,2048]{1,0:T(8,128)S(1)}, u32[]{:S(2)}, u32[]{:S(2)}) collective-permute-start(f32[9,2048]{1,0:T(8,128)S(1)} %select_add_fusion.1), channel_id=1, source_target_pairs={{0,4},{2,6},{4,0},{6,2},{1,5},{3,7},{5,1},{7,3},{8,12},{10,14},{12... | collective-permute-start | bytes 221192 | tf_op jit(solution)/shard_map/ppermute | solution.py:328
  380.7 8.3 %collective-permute-start.42 = (f32[9,2048]{1,0:T(8,128)S(1)}, f32[9,2048]{1,0:T(8,128)S(1)}, u32[]{:S(2)}, u32[]{:S(2)}) collective-permute-start(f32[9,2048]{1,0:T(8,128)S(1)} %select_add_fusion.1), channel_id=1, source_target_pairs={{0,2},{2,0},{4,6},{6,4},{1,3},{3,1},{5,7},{7,5},{8,10},{10,8},{12,... | collective-permute-start | bytes 221192 | tf_op jit(solution)/shard_map/ppermute | solution.py:328
  384.3 47.9 %collective-permute-start.28 = (bf16[128,1024]{1,0:T(8,128)(2,1)S(1)}, bf16[128,1024]{1,0:T(8,128)(2,1)S(1)}, u32[]{:S(2)}, u32[]{:S(2)}) collective-permute-start(bf16[128,1024]{1,0:T(8,128)(2,1)S(1)} %slice.390), channel_id=1, source_target_pairs={{0,1},{1,0},{2,3},{3,2},{4,5},{5,4},{6,7},{7,6},{8,9},{9,8},{10,11... | collective-permute-start | bytes 786440 | tf_op jit(solution)/shard_map/ppermute | solution.py:331
  387.4 69.7 %collective-permute-start.24 = (bf16[1024,512]{0,1:T(8,128)(2,1)}, bf16[1024,512]{0,1:T(8,128)(2,1)}, u32[]{:S(2)}, u32[]{:S(2)}) collective-permute-start(bf16[1024,512]{0,1:T(8,128)(2,1)} %slice.388), channel_id=1, source_target_pairs={{0,1},{1,0},{2,3},{3,2},{4,5},{5,4},{6,7},{7,6},{8,9},{9,8},{10,11... | collective-permute-start | bytes 3145736 | tf_op jit(solution)/shard_map/ppermute | solution.py:331
  389.0 38.8 %collective-permute-start.43 = (f32[9,2048]{1,0:T(8,128)S(1)}, f32[9,2048]{1,0:T(8,128)S(1)}, u32[]{:S(2)}, u32[]{:S(2)}) collective-permute-start(f32[9,2048]{1,0:T(8,128)S(1)} %select_add_fusion), channel_id=1, source_target_pairs={{0,1},{1,0},{2,3},{3,2},{4,5},{5,4},{6,7},{7,6},{8,9},{9,8},{10,11... | collective-permute-start | bytes 221192 | tf_op jit(solution)/shard_map/ppermute | solution.py:331
  429.8 9.8 %collective-permute-start.21 = (bf16[256,384]{0,1:T(8,128)(2,1)S(1)}, bf16[256,384]{0,1:T(8,128)(2,1)S(1)}, u32[]{:S(2)}, u32[]{:S(2)}) collective-permute-start(bf16[256,384]{0,1:T(8,128)(2,1)S(1)} %get-tuple-element.98), channel_id=1, source_target_pairs={{0,24},{8,16},{16,8},{24,0},{1,25},{9,17},{17,9},{25,1},{2,26},{10... | collective-permute-start | bytes 589832 | tf_op jit(solution)/shard_map/ppermute | solution.py:325
  430.2 18.7 %collective-permute-start.22 = (bf16[256,384]{0,1:T(8,128)(2,1)S(1)}, bf16[256,384]{0,1:T(8,128)(2,1)S(1)}, u32[]{:S(2)}, u32[]{:S(2)}) collective-permute-start(bf16[256,384]{0,1:T(8,128)(2,1)S(1)} %get-tuple-element.97), channel_id=1, source_target_pairs={{0,16},{8,24},{16,0},{24,8},{1,17},{9,25},{17,1},{25,9},{2,18},{10... | collective-permute-start | bytes 589832 | tf_op jit(solution)/shard_map/ppermute | solution.py:325
  432.2 18.2 %collective-permute-start.23 = (bf16[256,384]{0,1:T(8,128)(2,1)S(1)}, bf16[256,384]{0,1:T(8,128)(2,1)S(1)}, u32[]{:S(2)}, u32[]{:S(2)}) collective-permute-start(bf16[256,384]{0,1:T(8,128)(2,1)S(1)} %get-tuple-element.96), channel_id=1, source_target_pairs={{0,8},{8,0},{16,24},{24,16},{1,9},{9,1},{17,25},{25,17},{2,10},{10... | collective-permute-start | bytes 589832 | tf_op jit(solution)/shard_map/ppermute | solution.py:325
  435.8 16.2 %copy-start.15 = (f32[256,3,512]{2,0,1:T(8,128)S(1)}, f32[256,3,512]{2,0,1:T(8,128)}, u32[]{:S(2)}) copy-start(f32[256,3,512]{2,0,1:T(8,128)} %param.23) | copy-start | bytes 4718596
  439.6 60.1 %collective-permute-start.15 = (bf16[2,256,2048]{2,1,0:T(8,128)(2,1)}, bf16[2,256,2048]{2,1,0:T(8,128)(2,1)}, u32[]{:S(2)}, u32[]{:S(2)}) collective-permute-start(bf16[2,256,2048]{2,1,0:T(8,128)(2,1)} %get-tuple-element.66), channel_id=1, source_target_pairs={{0,2},{2,0},{4,6},{6,4},{1,3},{3,1},{5,7},{7,5},{8,10},{10,8},{12,... | collective-permute-start | bytes 6291464 | tf_op jit(solution)/shard_map/ppermute | solution.py:328
  448.9 24.0 %collective-permute-start.29 = (bf16[512,1024]{1,0:T(8,128)(2,1)}, bf16[512,1024]{1,0:T(8,128)(2,1)}, u32[]{:S(2)}, u32[]{:S(2)}) collective-permute-start(bf16[512,1024]{1,0:T(8,128)(2,1)} %slice.387), channel_id=1, source_target_pairs={{0,1},{1,0},{2,3},{3,2},{4,5},{5,4},{6,7},{7,6},{8,9},{9,8},{10,11... | collective-permute-start | bytes 3145736 | tf_op jit(solution)/shard_map/ppermute | solution.py:331
  457.1 15.8 %copy-start.20 = (f32[512,2048]{1,0:T(8,128)S(1)}, f32[512,2048]{1,0:T(8,128)}, u32[]{:S(2)}) copy-start(f32[512,2048]{1,0:T(8,128)} %fusion.79) | copy-start | bytes 12582916
  458.9 15.8 %copy-start.25 = (f32[128,4,1024]{2,1,0:T(4,128)S(1)}, f32[128,4,1024]{2,1,0:T(4,128)}, u32[]{:S(2)}) copy-start(f32[128,4,1024]{2,1,0:T(4,128)} %param.34) | copy-start | bytes 6291460
  459.0 23.5 %collective-permute-start.25 = (bf16[256,512]{0,1:T(8,128)(2,1)S(1)}, bf16[256,512]{0,1:T(8,128)(2,1)S(1)}, u32[]{:S(2)}, u32[]{:S(2)}) collective-permute-start(bf16[256,512]{0,1:T(8,128)(2,1)S(1)} %get-tuple-element.95), channel_id=1, source_target_pairs={{0,24},{8,16},{16,8},{24,0},{1,25},{9,17},{17,9},{25,1},{2,26},{10... | collective-permute-start | bytes 786440 | tf_op jit(solution)/shard_map/ppermute | solution.py:325
  460.3 22.3 %collective-permute-start.26 = (bf16[256,512]{0,1:T(8,128)(2,1)S(1)}, bf16[256,512]{0,1:T(8,128)(2,1)S(1)}, u32[]{:S(2)}, u32[]{:S(2)}) collective-permute-start(bf16[256,512]{0,1:T(8,128)(2,1)S(1)} %get-tuple-element.94), channel_id=1, source_target_pairs={{0,16},{8,24},{16,0},{24,8},{1,17},{9,25},{17,1},{25,9},{2,18},{10... | collective-permute-start | bytes 786440 | tf_op jit(solution)/shard_map/ppermute | solution.py:325
  472.9 11.5 %collective-permute-start.27 = (bf16[256,512]{0,1:T(8,128)(2,1)S(1)}, bf16[256,512]{0,1:T(8,128)(2,1)S(1)}, u32[]{:S(2)}, u32[]{:S(2)}) collective-permute-start(bf16[256,512]{0,1:T(8,128)(2,1)S(1)} %get-tuple-element.93), channel_id=1, source_target_pairs={{0,8},{8,0},{16,24},{24,16},{1,9},{9,1},{17,25},{25,17},{2,10},{10... | collective-permute-start | bytes 786440 | tf_op jit(solution)/shard_map/ppermute | solution.py:325
  482.5 27.8 %collective-permute-start = (bf16[2,256,2048]{2,1,0:T(8,128)(2,1)}, bf16[2,256,2048]{2,1,0:T(8,128)(2,1)}, u32[]{:S(2)}, u32[]{:S(2)}) collective-permute-start(bf16[2,256,2048]{2,1,0:T(8,128)(2,1)} %get-tuple-element.69), channel_id=1, source_target_pairs={{0,2},{2,0},{4,6},{6,4},{1,3},{3,1},{5,7},{7,5},{8,10},{10,8},{12,... | collective-permute-start | bytes 6291464 | tf_op jit(solution)/shard_map/ppermute | solution.py:328
  482.6 27.8 %collective-permute-start.5 = (bf16[2,256,2048]{2,1,0:T(8,128)(2,1)}, bf16[2,256,2048]{2,1,0:T(8,128)(2,1)}, u32[]{:S(2)}, u32[]{:S(2)}) collective-permute-start(bf16[2,256,2048]{2,1,0:T(8,128)(2,1)} %get-tuple-element.70), channel_id=1, source_target_pairs={{0,2},{2,0},{4,6},{6,4},{1,3},{3,1},{5,7},{7,5},{8,10},{10,8},{12,... | collective-permute-start | bytes 6291464 | tf_op jit(solution)/shard_map/ppermute | solution.py:328
  492.1 18.2 %slice-start.4 = ((s8[8388608]{0:T(1024)(128)(4,1)}), s8[4194304]{0:T(1024)(128)(4,1)S(1)}, s32[]{:S(2)}) async-start(s8[8388608]{0:T(1024)(128)(4,1)} %bitcast.189), calls=%async_computation.4 | async-start | bytes 8388608
  499.8 10.6 %slice-start.5 = ((s8[8388608]{0:T(1024)(128)(4,1)}), s8[4194304]{0:T(1024)(128)(4,1)S(1)}, s32[]{:S(2)}) async-start(s8[8388608]{0:T(1024)(128)(4,1)} %bitcast.189), calls=%async_computation.5 | async-start | bytes 8388608
  506.5 27.1 %collective-permute-start.11 = (bf16[256,2048]{1,0:T(8,128)(2,1)}, bf16[256,2048]{1,0:T(8,128)(2,1)}, u32[]{:S(2)}, u32[]{:S(2)}) collective-permute-start(bf16[256,2048]{1,0:T(8,128)(2,1)} %fusion.58), channel_id=1, source_target_pairs={{0,4},{2,6},{4,0},{6,2},{1,5},{3,7},{5,1},{7,3},{8,12},{10,14},{12... | collective-permute-start | bytes 3145736 | tf_op jit(solution)/shard_map/ppermute | solution.py:328
  510.3 45.7 %collective-permute-start.16 = (bf16[256,2048]{1,0:T(8,128)(2,1)}, bf16[256,2048]{1,0:T(8,128)(2,1)}, u32[]{:S(2)}, u32[]{:S(2)}) collective-permute-start(bf16[256,2048]{1,0:T(8,128)(2,1)} %fusion.59), channel_id=1, source_target_pairs={{0,4},{2,6},{4,0},{6,2},{1,5},{3,7},{5,1},{7,3},{8,12},{10,14},{12... | collective-permute-start | bytes 3145736 | tf_op jit(solution)/shard_map/ppermute | solution.py:328
  517.9 60.5 %collective-permute-start.1 = (bf16[256,2048]{1,0:T(8,128)(2,1)S(1)}, bf16[256,2048]{1,0:T(8,128)(2,1)S(1)}, u32[]{:S(2)}, u32[]{:S(2)}) collective-permute-start(bf16[256,2048]{1,0:T(8,128)(2,1)S(1)} %fusion.56), channel_id=1, source_target_pairs={{0,4},{2,6},{4,0},{6,2},{1,5},{3,7},{5,1},{7,3},{8,12},{10,14},{12... | collective-permute-start | bytes 3145736 | tf_op jit(solution)/shard_map/ppermute | solution.py:328
  520.2 78.9 %collective-permute-start.6 = (bf16[256,2048]{1,0:T(8,128)(2,1)S(1)}, bf16[256,2048]{1,0:T(8,128)(2,1)S(1)}, u32[]{:S(2)}, u32[]{:S(2)}) collective-permute-start(bf16[256,2048]{1,0:T(8,128)(2,1)S(1)} %fusion.57), channel_id=1, source_target_pairs={{0,4},{2,6},{4,0},{6,2},{1,5},{3,7},{5,1},{7,3},{8,12},{10,14},{12... | collective-permute-start | bytes 3145736 | tf_op jit(solution)/shard_map/ppermute | solution.py:328
  535.2 43.2 %copy-start.10 = (f32[2,256,2048]{2,1,0:T(8,128)S(1)}, f32[2,256,2048]{2,1,0:T(8,128)}, u32[]{:S(2)}) copy-start(f32[2,256,2048]{2,1,0:T(8,128)} %get-tuple-element.67) | copy-start | bytes 12582916
  535.2 65.7 %collective-permute-start.12 = (bf16[256,1024]{1,0:T(8,128)(2,1)S(1)}, bf16[256,1024]{1,0:T(8,128)(2,1)S(1)}, u32[]{:S(2)}, u32[]{:S(2)}) collective-permute-start(bf16[256,1024]{1,0:T(8,128)(2,1)S(1)} %slice.277), channel_id=1, source_target_pairs={{0,1},{1,0},{2,3},{3,2},{4,5},{5,4},{6,7},{7,6},{8,9},{9,8},{10,11... | collective-permute-start | bytes 1572872 | tf_op jit(solution)/shard_map/ppermute | solution.py:331
  557.6 46.3 %collective-permute-start.17 = (bf16[256,1024]{1,0:T(8,128)(2,1)S(1)}, bf16[256,1024]{1,0:T(8,128)(2,1)S(1)}, u32[]{:S(2)}, u32[]{:S(2)}) collective-permute-start(bf16[256,1024]{1,0:T(8,128)(2,1)S(1)} %slice.281), channel_id=1, source_target_pairs={{0,1},{1,0},{2,3},{3,2},{4,5},{5,4},{6,7},{7,6},{8,9},{9,8},{10,11... | collective-permute-start | bytes 1572872 | tf_op jit(solution)/shard_map/ppermute | solution.py:331
  578.8 25.9 %collective-permute-start.2 = (bf16[256,1024]{1,0:T(8,128)(2,1)S(1)}, bf16[256,1024]{1,0:T(8,128)(2,1)S(1)}, u32[]{:S(2)}, u32[]{:S(2)}) collective-permute-start(bf16[256,1024]{1,0:T(8,128)(2,1)S(1)} %slice.261), channel_id=1, source_target_pairs={{0,1},{1,0},{2,3},{3,2},{4,5},{5,4},{6,7},{7,6},{8,9},{9,8},{10,11... | collective-permute-start | bytes 1572872 | tf_op jit(solution)/shard_map/ppermute | solution.py:331
  599.5 12.2 %collective-permute-start.7 = (bf16[256,1024]{1,0:T(8,128)(2,1)S(1)}, bf16[256,1024]{1,0:T(8,128)(2,1)S(1)}, u32[]{:S(2)}, u32[]{:S(2)}) collective-permute-start(bf16[256,1024]{1,0:T(8,128)(2,1)S(1)} %slice.265), channel_id=1, source_target_pairs={{0,1},{1,0},{2,3},{3,2},{4,5},{5,4},{6,7},{7,6},{8,9},{9,8},{10,11... | collective-permute-start | bytes 1572872 | tf_op jit(solution)/shard_map/ppermute | solution.py:331
  601.0 59.4 %collective-permute-start.13 = (bf16[256,1024]{1,0:T(8,128)(2,1)S(1)}, bf16[256,1024]{1,0:T(8,128)(2,1)S(1)}, u32[]{:S(2)}, u32[]{:S(2)}) collective-permute-start(bf16[256,1024]{1,0:T(8,128)(2,1)S(1)} %get-tuple-element.77), channel_id=1, source_target_pairs={{0,16},{8,24},{16,0},{24,8},{1,17},{9,25},{17,1},{25,9},{2,18},{10... | collective-permute-start | bytes 1572872 | tf_op jit(solution)/shard_map/ppermute | solution.py:325
  601.6 58.8 %collective-permute-start.14 = (bf16[256,1024]{1,0:T(8,128)(2,1)S(1)}, bf16[256,1024]{1,0:T(8,128)(2,1)S(1)}, u32[]{:S(2)}, u32[]{:S(2)}) collective-permute-start(bf16[256,1024]{1,0:T(8,128)(2,1)S(1)} %get-tuple-element.78), channel_id=1, source_target_pairs={{0,24},{8,16},{16,8},{24,0},{1,25},{9,17},{17,9},{25,1},{2,26},{10... | collective-permute-start | bytes 1572872 | tf_op jit(solution)/shard_map/ppermute | solution.py:325
  604.0 56.3 %copy-start.50 = (f32[1,1024]{1,0:T(1,128)S(1)}, f32[1,1024]{1,0:T(1,128)}, u32[]{:S(2)}) copy-start(f32[1,1024]{1,0:T(1,128)} %copy-done.49) | copy-start | bytes 12292
  604.0 56.3 %collective-permute-start.18 = (bf16[256,1024]{1,0:T(8,128)(2,1)S(1)}, bf16[256,1024]{1,0:T(8,128)(2,1)S(1)}, u32[]{:S(2)}, u32[]{:S(2)}) collective-permute-start(bf16[256,1024]{1,0:T(8,128)(2,1)S(1)} %broadcast_select_fusion.1), channel_id=1, source_target_pairs={{0,8},{8,0},{16,24},{24,16},{1,9},{9,1},{17,25},{25,17},{2,10},{10... | collective-permute-start | bytes 1572872 | tf_op jit(solution)/shard_map/ppermute | solution.py:325
  604.8 97.7 %collective-permute-start.3 = (bf16[256,1024]{1,0:T(8,128)(2,1)S(1)}, bf16[256,1024]{1,0:T(8,128)(2,1)S(1)}, u32[]{:S(2)}, u32[]{:S(2)}) collective-permute-start(bf16[256,1024]{1,0:T(8,128)(2,1)S(1)} %get-tuple-element.79), channel_id=1, source_target_pairs={{0,16},{8,24},{16,0},{24,8},{1,17},{9,25},{17,1},{25,9},{2,18},{10... | collective-permute-start | bytes 1572872 | tf_op jit(solution)/shard_map/ppermute | solution.py:325
  611.7 90.8 %collective-permute-start.4 = (bf16[256,1024]{1,0:T(8,128)(2,1)S(1)}, bf16[256,1024]{1,0:T(8,128)(2,1)S(1)}, u32[]{:S(2)}, u32[]{:S(2)}) collective-permute-start(bf16[256,1024]{1,0:T(8,128)(2,1)S(1)} %get-tuple-element.80), channel_id=1, source_target_pairs={{0,24},{8,16},{16,8},{24,0},{1,25},{9,17},{17,9},{25,1},{2,26},{10... | collective-permute-start | bytes 1572872 | tf_op jit(solution)/shard_map/ppermute | solution.py:325
  661.2 13.5 %collective-permute-start.30 = (f32[2,2048]{1,0:T(2,128)S(1)}, f32[2,2048]{1,0:T(2,128)S(1)}, u32[]{:S(2)}, u32[]{:S(2)}) collective-permute-start(f32[2,2048]{1,0:T(2,128)S(1)} %maximum_dynamic-update-slice_fusion), channel_id=1, source_target_pairs={{0,24},{8,16},{16,8},{24,0},{1,25},{9,17},{17,9},{25,1},{2,26},{10... | collective-permute-start | bytes 49160 | tf_op jit(solution)/shard_map/ppermute | solution.py:325
  662.5 32.0 %collective-permute-start.31 = (f32[2,2048]{1,0:T(2,128)S(1)}, f32[2,2048]{1,0:T(2,128)S(1)}, u32[]{:S(2)}, u32[]{:S(2)}) collective-permute-start(f32[2,2048]{1,0:T(2,128)S(1)} %maximum_dynamic-update-slice_fusion), channel_id=1, source_target_pairs={{0,16},{8,24},{16,0},{24,8},{1,17},{9,25},{17,1},{25,9},{2,18},{10... | collective-permute-start | bytes 49160 | tf_op jit(solution)/shard_map/ppermute | solution.py:325
  674.7 20.2 %collective-permute-start.32 = (f32[2,2048]{1,0:T(2,128)S(1)}, f32[2,2048]{1,0:T(2,128)S(1)}, u32[]{:S(2)}, u32[]{:S(2)}) collective-permute-start(f32[2,2048]{1,0:T(2,128)S(1)} %maximum_dynamic-update-slice_fusion), channel_id=1, source_target_pairs={{0,8},{8,0},{16,24},{24,16},{1,9},{9,1},{17,25},{25,17},{2,10},{10... | collective-permute-start | bytes 49160 | tf_op jit(solution)/shard_map/ppermute | solution.py:325
  674.8 30.5 %collective-permute-start.8 = (bf16[256,1024]{1,0:T(8,128)(2,1)S(1)}, bf16[256,1024]{1,0:T(8,128)(2,1)S(1)}, u32[]{:S(2)}, u32[]{:S(2)}) collective-permute-start(bf16[256,1024]{1,0:T(8,128)(2,1)S(1)} %broadcast_select_fusion.4), channel_id=1, source_target_pairs={{0,8},{8,0},{16,24},{24,16},{1,9},{9,1},{17,25},{25,17},{2,10},{10... | collective-permute-start | bytes 1572872 | tf_op jit(solution)/shard_map/ppermute | solution.py:325
  694.4 3.6 collective-permute-start.19
  695.0 4.8 collective-permute-start.33
  698.0 3.8 collective-permute-start.34
  699.8 2.0 collective-permute-start.35
  701.9 5.3 collective-permute-start.36
  (46 other events, 211.9 us)

commit v2 on v1

--- a/solution.py
+++ b/solution.py
@@ -37,30 +37,14 @@
     segment = jnp.sum(member * number[None, :], axis=1, dtype=jnp.int32) - 1
     seq_first = jnp.sum(member * starts[None, :], axis=1, dtype=jnp.int32)
     position = jnp.where(segment >= 0, places - seq_first, places - total_len)
-    return (segment, position, total_len)
+    return position
 
 
 def turn_angles(position):
     half_rot = ROT // 2
     freq_base = jnp.power(10000.0, -2.0 * jnp.arange(half_rot, dtype=jnp.float32) / ROT)
-    angle = position.astype(jnp.float32)[:, None] * freq_base[None, :]
+    angle = position.astype(jnp.float32)[..., None] * freq_base
     return (jnp.cos(angle), jnp.sin(angle))
-
-
-def rotate(heads_view, cos_part, sin_part):
-    half_rot = ROT // 2
-    lead_part = heads_view[..., :half_rot]
-    trail_part = heads_view[..., half_rot:ROT]
-    cos_wide = cos_part[..., None, :]
-    sin_wide = sin_part[..., None, :]
-    return jnp.concatenate(
-        [
-            lead_part * cos_wide - trail_part * sin_wide,
-            trail_part * cos_wide + lead_part * sin_wide,
-            heads_view[..., ROT:],
-        ],
-        axis=-1,
-    )
 
 
 def adamw(weight, first_moment, second_moment, gradient, rate, decay):
@@ -277,6 +261,418 @@
                         pltpu.SemaphoreType.DMA((80,)), pltpu.SemaphoreType.DMA((80,)), pltpu.SemaphoreType.DMA((24,))],
         compiler_params=pltpu.CompilerParams(collective_id=1, has_side_effects=True, vmem_limit_bytes=32 << 20),
     )(tok, cot, norm_vec, wq, wu, dh)
+
+def mm(a, b):
+    return jnp.dot(a, b, preferred_element_type=f32)
+
+
+def mm_t(a, b):
+    return lax.dot_general(a, b, (((1,), (1,)), ((), ())), preferred_element_type=f32)
+
+
+def t_mm(a, b):
+    return lax.dot_general(a, b, (((0,), (0,)), ((), ())), preferred_element_type=f32)
+
+
+def gelu_both(v):
+    root = 0.7978845608028654
+    square = v * v
+    slope = root * (1.0 + 3 * 0.044715 * square)
+    tanh = jnp.tanh(root * v * (1.0 + 0.044715 * square))
+    outer = 0.5 * (1.0 + tanh)
+    return v * outer, outer + 0.5 * v * (1.0 - tanh * tanh) * slope
+
+
+def local_kernel(x_ref, b_ref, wq_ref, wu_ref, d_ref, bias_ref, cos_ref, lead_ref, trail_ref, from_ref, place_ref, key_ref,
+                 attn_ref, hidden_ref, dqkv_ref, dup_ref, sums_ref,
+                 q_s, k_s, v_s, da_s, dk_s, dv_s):
+    slots, part = q_s.shape
+    qb = 256
+    scale = HDIM ** (-0.5)
+    quarter = ROT // 2
+
+    def turn(value, at, sign):
+        left = jnp.roll(value, -quarter, axis=1)
+        right = jnp.roll(value, quarter, axis=1)
+        return value * cos_ref[0, at, :] + sign * (left * lead_ref[0, at, :] + right * trail_ref[0, at, :])
+
+    def project(i, carry):
+        at = pl.ds(pl.multiple_of(i * qb, qb), qb)
+        pre = mm(x_ref[0, at, :], wq_ref[...]) + bias_ref[0:1, 0:3 * part]
+        q_s[at, :] = (turn(pre[:, 0:part], at, 1.0)).astype(bf16)
+        k_s[at, :] = (turn(pre[:, part:2 * part], at, 1.0)).astype(bf16)
+        v_s[at, :] = pre[:, 2 * part:].astype(bf16)
+        back = b_ref[0, at, :]
+        da_s[at, :] = mm_t(back, d_ref[0:part, :]).astype(bf16)
+        return carry
+
+    lax.fori_loop(0, slots // qb, project, 0)
+
+    def up(i, carry):
+        at = pl.ds(pl.multiple_of(i * qb, qb), qb)
+        pre = mm(x_ref[0, at, :], wu_ref[...]) + bias_ref[0:1, 3 * part:]
+        value, slope = gelu_both(pre)
+        hidden_ref[0, at, :] = value.astype(bf16)
+        d_up = (mm_t(b_ref[0, at, :], d_ref[part:, :]) * slope).astype(bf16)
+        dup_ref[0, at, :] = d_up
+        return carry + jnp.sum(d_up.astype(f32), axis=0, keepdims=True)
+
+    up_sum = lax.fori_loop(0, slots // qb, up, jnp.zeros((1, 4 * part), f32))
+    sums_ref[0, 0:1, 3 * part:] = up_sum
+
+    dk_s[...] = jnp.zeros_like(dk_s)
+    dv_s[...] = jnp.zeros_like(dv_s)
+    lane = lax.broadcasted_iota(jnp.int32, (qb, part), 1)
+
+    def attend(i, q_sum):
+        at = pl.ds(pl.multiple_of(i * qb, qb), qb)
+        key_place = key_ref[0:1, :]
+        allowed = (key_place >= from_ref[0, at, :]) & (key_place <= place_ref[0, at, :])
+        queries, d_attn = q_s[at, :], da_s[at, :]
+        out = jnp.zeros((qb, part), f32)
+        d_q = jnp.zeros((qb, part), f32)
+        for h in range(part // HDIM):
+            head = (lane >= h * HDIM) & (lane < (h + 1) * HDIM)
+            q_h = jnp.where(head, queries, jnp.zeros_like(queries))
+            da_h = jnp.where(head, d_attn, jnp.zeros_like(d_attn))
+            scores = jnp.where(allowed, mm_t(q_h, k_s[...]) * scale, -1e30)
+            weights = jnp.exp(scores - jnp.max(scores, axis=-1, keepdims=True))
+            probs = weights * (1.0 / jnp.sum(weights, axis=-1, keepdims=True))
+            low = probs.astype(bf16)
+            d_probs = mm_t(da_h, v_s[...])
+            delta = jnp.sum(probs * d_probs, axis=-1, keepdims=True)
+            d_scores = (probs * (d_probs - delta)).astype(bf16)
+            out = jnp.where(head, mm(low, v_s[...]), out)
+            d_q = jnp.where(head, mm(d_scores, k_s[...]), d_q)
+            dk_s[...] += t_mm(q_h, d_scores)
+            dv_s[...] += t_mm(da_h, low)
+        attn_ref[0, at, :] = out.astype(bf16)
+        d_q = turn(d_q * scale, at, -1.0).astype(bf16)
+        dqkv_ref[0, at, 0:part] = d_q
+        return q_sum + jnp.sum(d_q.astype(f32), axis=0, keepdims=True)
+
+    sums_ref[0, 0:1, 0:part] = lax.fori_loop(0, slots // qb, attend, jnp.zeros((1, part), f32))
+    whole = pl.ds(0, slots)
+    d_k = turn(dk_s[...].T * scale, whole, -1.0).astype(bf16)
+    d_v = dv_s[...].T.astype(bf16)
+    dqkv_ref[0, :, part:2 * part] = d_k
+    dqkv_ref[0, :, 2 * part:] = d_v
+    sums_ref[0, 0:1, part:2 * part] = jnp.sum(d_k.astype(f32), axis=0, keepdims=True)
+    sums_ref[0, 0:1, 2 * part:3 * part] = jnp.sum(d_v.astype(f32), axis=0, keepdims=True)
+
+
+def local_part(normed, back, qkv_mat, up_mat, out_mat, bias, cosine, lead, trail, first, place, key_place):
+    groups, slots, width = normed.shape
+    part = out_mat.shape[0] // 5
+
+    def each(last):
+        return pl.BlockSpec((1, slots, last), lambda p: (p, 0, 0))
+
+    def once(value):
+        return pl.BlockSpec(value.shape, lambda p: (0,) * value.ndim, pipeline_mode=pl.Buffered(1))
+
+    def like(last, kind=bf16):
+        return jax.ShapeDtypeStruct((groups, slots, last), kind)
+
+    return pl.pallas_call(
+        local_kernel,
+        grid=(groups,),
+        out_shape=[like(part), like(4 * part), like(3 * part), like(4 * part), jax.ShapeDtypeStruct((groups, 8, 7 * part), f32)],
+        in_specs=[each(width), each(width), once(qkv_mat), once(up_mat), once(out_mat), once(bias),
+                  each(part), each(part), each(part), each(1), each(1), once(key_place)],
+        out_specs=[each(part), each(4 * part), each(3 * part), each(4 * part), pl.BlockSpec((1, 8, 7 * part), lambda p: (p, 0, 0))],
+        scratch_shapes=[pltpu.VMEM((slots, part), bf16)] * 4 + [pltpu.VMEM((part, slots), f32)] * 2,
+        compiler_params=pltpu.CompilerParams(vmem_limit_bytes=56 << 20),
+    )(normed, back, qkv_mat, up_mat, out_mat, bias, cosine, lead, trail, first, place, key_place)
+
+def scatter_kernel(tier_count, order, attn, hidden, dqkv, dup, x_in, b_in, wq, wu, dm, tok, bias_ref,
+                   block_out, dn_out, g_out, gd_out,
+                   a_v, h_v, q_v, u_v, wq_v, wu_v, d_v, at_v, col_v, part_s, near_r, far_r, line_s, line_r,
+                   go_s, go_r, gm_s, do_s, do_r, dm_s, dn_s, send_sems, recv_sems, load_sems, col_sems):
+    line_id, flips, line, core, far, col = neighbours(tier_count)
+    bit = (line_id % 2 + lax.axis_index("col")) % 2
+    middle = (line_id == 1) | (line_id == 2)
+    ends = (line_id == 0) | (line_id == 3)
+    rows, half = tok.shape
+    chunk = rows // CH
+    width = 2 * half
+    step = half // 2
+    part = a_v.shape[1]
+    block = half // 4
+    copies = Copies(send_sems, recv_sems)
+    loads = []
+    for src, dst in ((attn, a_v), (hidden, h_v), (dm, d_v), (dup, u_v), (dqkv, q_v), (wu, wu_v), (wq, wq_v)):
+        load = pltpu.make_async_copy(src, dst, load_sems.at[len(loads)])
+        load.start()
+        loads.append([load, False])
+
+    def need(*which):
+        for i in which:
+            if not loads[i][1]:
+                loads[i][0].wait()
+                loads[i][1] = True
+
+    sent = []
+
+    def send(src, dst, device, when=None, slot=None):
+        copy = copies.make(src, dst, device, slot)
+        if when is None:
+            copy.start()
+        else:
+            pl.when(when)(copy.start)
+        sent.append([copy, when])
+        return copy
+
+    def wait_sent(copy):
+        for entry in sent:
+            if entry[0] is copy:
+                sent[:] = [e for e in sent if e is not entry]
+                if entry[1] is None:
+                    copy.wait_send()
+                else:
+                    pl.when(entry[1])(copy.wait_send)
+
+    wanted = []
+    for what, *args in order:
+        if what in ("go", "gm"):
+            first = flips[args[0]] * block + (half if what == "go" else 0)
+            wanted.append((x_in, first))
+        if what in ("do", "dm"):
+            wanted.append((b_in, args[0] * block + (half if what == "do" else 0)))
+    taken = [0]
+    fetches = []
+
+    def fetch(i):
+        src, first = wanted[i]
+        if not isinstance(first, int):
+            first = pl.multiple_of(first, block)
+        copy = pltpu.make_async_copy(src.at[:, pl.ds(first, block)], col_v.at[i % 2], col_sems.at[i % 2])
+        copy.start()
+        fetches.append(copy)
+
+    def take():
+        i = taken[0]
+        taken[0] += 1
+        if i + 1 < len(wanted):
+            fetch(i + 1)
+        fetches[i].wait()
+        return col_v.at[i % 2]
+
+    if wanted:
+        fetch(0)
+    meet([line[1], line[2], line[3], core, far, col])
+
+    def cut(c):
+        return pl.ds(c * chunk, chunk)
+
+    class Stream:
+        def __init__(self, number):
+            self.number = number
+            self.near, self.far, self.col, self.one, self.two, self.three, self.relay = {}, {}, {}, {}, {}, {}, {}
+
+        def compute(self, p, c):
+            place = 2 * p + c
+            out = part_s.at[place]
+            if self.number:
+                for copy in old.near[p, c] + [old.far[p, c], old.col[p, c]]:
+                    wait_sent(copy)
+                left, right = (q_v, wq_v), (u_v, wu_v)
+                need(3, 4, 5, 6)
+            else:
+                left, right = (a_v, None), (h_v, None)
+                need(0, 1, 2)
+
+            def body(n, carry):
+                at = pl.ds(pl.multiple_of(n * step, step), step)
+
+                def lhs(ref):
+                    base = p * 4 * rows + c * chunk
+                    return jnp.concatenate([ref[pl.ds(base + t * rows, chunk), :] for t in range(4)], axis=0)
+
+                if self.number:
+                    total = mm_t(lhs(q_v), wq_v[at, :]) + mm_t(lhs(u_v), wu_v[at, :])
+                else:
+                    total = mm(lhs(a_v), d_v[0:part, at]) + mm(lhs(h_v), d_v[part:, at])
+                low = total.astype(bf16)
+                for t in range(4):
+                    out[t, :, at] = low[t * chunk:(t + 1) * chunk]
+                return carry
+
+            lax.fori_loop(0, width // step, body, 0)
+            into = near_r.at[4 * self.number + place]
+            self.near[p, c] = [send(out.at[1], into.at[0], core), send(out.at[3], into.at[1], core)]
+
+        def give_far(self, p, c):
+            place = 2 * p + c
+            self.near[p, c][1].wait_recv()
+            mine = part_s.at[place, 2]
+            mine[...] = (mine[...].astype(f32) + near_r[4 * self.number + place, 1].astype(f32)).astype(bf16)
+            self.far[p, c] = send(mine, far_r.at[4 * self.number + place], far)
+
+        def give_col(self, p, c):
+            place = 2 * p + c
+            self.near[p, c][0].wait_recv()
+            self.far[p, c].wait_recv()
+            mine = part_s.at[place, 0]
+            total = mine[...].astype(f32) + near_r[4 * self.number + place, 0].astype(f32)
+            total = (total + far_r[4 * self.number + place].astype(f32)).astype(bf16)
+            line_s[self.number, 2 * p + bit, cut(c), :] = total[:, :half]
+            mine[:, pl.ds(half, half)] = total[:, half:]
+            self.col[p, c] = send(mine.at[:, pl.ds(half, half)], line_s.at[self.number, 2 * p + bit, cut(c)], col)
+
+        def give_line(self, p, c):
+            self.col[p, c].wait_recv()
+            own, got = line_s.at[self.number], line_r.at[self.number]
+            if p == 0:
+                self.one[c] = send(own.at[1, cut(c)], got.at[0, cut(c)], line[1])
+            else:
+                self.relay[c] = send(own.at[3, cut(c)], got.at[3, cut(c)], line[1], ends)
+                self.three[c] = send(own.at[3, cut(c)], got.at[2, cut(c)], line[3], middle)
+                slot = copies.slot()
+                self.two[c] = send(own.at[2, cut(c)], got.at[1, cut(c)], line[2], ends, slot)
+
+        def relay_line(self, c):
+            own, got = line_s.at[self.number], line_r.at[self.number]
+
+            @pl.when(middle)
+            def _():
+                self.relay[c].wait_recv()
+                own[2, cut(c), :] = (own[2, cut(c), :].astype(f32) + got[3, cut(c), :].astype(f32)).astype(bf16)
+                self.two[c].start()
+
+            sent[:] = [[e[0], None] if e[0] is self.two[c] else e for e in sent]
+
+        def finish(self, c):
+            own, got = line_s.at[self.number], line_r.at[self.number]
+            self.one[c].wait_recv()
+            self.two[c].wait_recv()
+            total = own[0, cut(c), :].astype(f32) + got[0, cut(c), :].astype(f32) + got[1, cut(c), :].astype(f32)
+            dn_s[cut(c), :] = total
+
+            @pl.when(middle)
+            def _():
+                self.three[c].wait_recv()
+                dn_s[cut(c), :] += got[2, cut(c), :].astype(f32)
+
+            if self.number:
+                dn_out[cut(c), :] = dn_s[cut(c), :]
+            else:
+                block_out[cut(c), :] = (tok[cut(c), :].astype(f32) + dn_s[cut(c), :] + bias_ref[0:1, :]).astype(bf16)
+
+    g_near, g_line, d_near = {}, {}, {}
+    q_width, u_width = q_v.shape[1], u_v.shape[1]
+
+    def grad_block(dst):
+        need(3, 4)
+        source = take()
+        dst[:, pl.ds(0, q_width)] = t_mm(source[...], q_v[...]).astype(bf16)
+        dst[:, pl.ds(q_width, u_width)] = t_mm(source[...], u_v[...]).astype(bf16)
+
+    def grad_other(s):
+        grad_block(go_s.at[s])
+        g_near[s] = send(go_s.at[s], go_r.at[s], col)
+
+    def grad_line(s):
+        g_near[s].wait_recv()
+        gm_s[s] = (gm_s[s].astype(f32) + go_r[s].astype(f32)).astype(bf16)
+        if s:
+            g_line[s] = send(gm_s.at[s], g_out.at[line_id], line[s])
+        else:
+            load = pltpu.make_async_copy(gm_s.at[0], g_out.at[line_id], load_sems.at[len(loads)])
+            load.start()
+            loads.append([load, False])
+
+    turned = [False]
+
+    def out_block(j, other):
+        need(0, 1)
+        if not turned[0]:
+            at_v[0:part, :] = a_v[...].T
+            at_v[part:, :] = h_v[...].T
+            turned[0] = True
+        source = take()
+        at = pl.ds(j * block, block)
+        value = mm(at_v[...], source[...])
+        if other:
+            do_s[j] = value.astype(bf16)
+            d_near[j] = send(do_s.at[j], do_r.at[j], col)
+        else:
+            dm_s[:, at] = value
+
+    def out_finish(j):
+        d_near[j].wait_recv()
+        at = pl.ds(j * block, block)
+        dm_s[:, at] += do_r[j].astype(f32)
+        load = pltpu.make_async_copy(dm_s.at[:, at], gd_out.at[:, at], load_sems.at[len(loads)])
+        load.start()
+        loads.append([load, False])
+
+    old, new = Stream(0), Stream(1)
+    both = (old, new)
+    for what, *args in order:
+        if what == "c": both[args[0]].compute(*args[1:])
+        if what == "x": both[args[0]].give_far(*args[1:])
+        if what == "y": both[args[0]].give_col(*args[1:])
+        if what == "z": both[args[0]].give_line(*args[1:])
+        if what == "r": both[args[0]].relay_line(*args[1:])
+        if what == "f": both[args[0]].finish(*args[1:])
+        if what == "go": grad_other(*args)
+        if what == "gm": grad_block(gm_s.at[args[0]])
+        if what == "gz": grad_line(*args)
+        if what == "do": out_block(args[0], True)
+        if what == "dm": out_block(args[0], False)
+        if what == "df": out_finish(*args)
+    for copy in g_line.values():
+        copy.wait_recv()
+    need(*range(len(loads)))
+    for copy, when in list(sent):
+        wait_sent(copy)
+
+
+def scatter_order():
+    return [
+        ("c", 0, 1, 0), ("go", 1), ("c", 0, 1, 1), ("x", 0, 1, 0), ("go", 2), ("x", 0, 1, 1),
+        ("c", 0, 0, 0), ("gm", 1), ("x", 0, 0, 0), ("c", 0, 0, 1), ("gm", 2), ("x", 0, 0, 1),
+        ("gz", 1), ("y", 0, 1, 0), ("go", 3), ("gm", 3), ("z", 0, 1, 0), ("y", 0, 1, 1), ("gz", 2),
+        ("c", 1, 1, 0), ("x", 1, 1, 0), ("z", 0, 1, 1), ("r", 0, 0), ("y", 0, 0, 0), ("c", 1, 1, 1), ("x", 1, 1, 1), ("go", 0), ("gm", 0),
+        ("r", 0, 1), ("z", 0, 0, 0), ("y", 0, 0, 1), ("c", 1, 0, 0), ("x", 1, 0, 0), ("gz", 3),
+        ("z", 0, 0, 1), ("c", 1, 0, 1), ("x", 1, 0, 1), ("do", 0), ("f", 0, 0), ("y", 1, 1, 0), ("do", 1), ("gz", 0),
+        ("z", 1, 1, 0), ("y", 1, 1, 1), ("f", 0, 1), ("do", 2), ("r", 1, 0), ("z", 1, 1, 1), ("y", 1, 0, 0), ("do", 3),
+        ("r", 1, 1), ("z", 1, 0, 0), ("dm", 0), ("dm", 1), ("y", 1, 0, 1), ("dm", 2), ("dm", 3), ("z", 1, 0, 1),
+        ("f", 1, 0), ("df", 0), ("df", 1), ("df", 2), ("df", 3), ("f", 1, 1),
+    ]
+
+
+def scatter(tier_count, attn, hidden, dqkv, dup, normed, back, qkv_mat, up_mat, out_mat, tok, bias, order=None):
+    rows, half = tok.shape
+    width = 2 * half
+    chunk = rows // CH
+    all_rows = attn.shape[0]
+    part = attn.shape[1]
+    sds = jax.ShapeDtypeStruct
+    any_ = pl.BlockSpec(memory_space=pl.ANY)
+    vmem = pl.BlockSpec(memory_space=pltpu.VMEM)
+    block = half // 4
+
+    def buf(*shape, kind=bf16):
+        return pltpu.VMEM(shape, kind)
+
+    return pl.pallas_call(
+        functools.partial(scatter_kernel, tier_count, order or scatter_order()),
+        out_shape=[sds((rows, half), bf16), sds((rows, half), f32), sds((4, block, 7 * part), bf16), sds((5 * part, half), f32)],
+        in_specs=[any_] * 9 + [vmem, vmem],
+        out_specs=[vmem, vmem, any_, any_],
+        scratch_shapes=[
+            buf(all_rows, part), buf(all_rows, 4 * part), buf(all_rows, 3 * part), buf(all_rows, 4 * part),
+            buf(width, 3 * part), buf(width, 4 * part), buf(5 * part, width), buf(5 * part, all_rows),
+            buf(2, all_rows, block), buf(4, 4, chunk, width), buf(8, 2, chunk, width), buf(8, chunk, width),
+            buf(2, 4, rows, half), buf(2, 4, rows, half),
+            buf(4, block, 7 * part), buf(4, block, 7 * part), buf(4, block, 7 * part),
+            buf(4, 5 * part, block), buf(4, 5 * part, block), buf(5 * part, half, kind=f32), buf(rows, half, kind=f32),
+            pltpu.SemaphoreType.DMA((64,)), pltpu.SemaphoreType.DMA((64,)), pltpu.SemaphoreType.DMA((16,)), pltpu.SemaphoreType.DMA((2,)),
+        ],
+        compiler_params=pltpu.CompilerParams(collective_id=2, has_side_effects=True, vmem_limit_bytes=62 << 20),
+    )(attn, hidden, dqkv, dup, normed, back, qkv_mat, up_mat, out_mat, tok, bias)
 
 
 def per_device(
@@ -316,7 +712,6 @@
     row_width = full_width // row_count
     part = row_width // LINE
     heads_dev = part // HDIM
-    score_scale = HDIM ** (-0.5)
     zero_index = jnp.int32(0)
     tier_groups = [[line * tier_count + tier for tier in range(tier_count)] for line in range(LINE)]
 
@@ -357,16 +752,23 @@
     places = jnp.concatenate(
         [(row_id ^ t) * tok_dev + jnp.arange(tok_dev, dtype=jnp.int32) for t in range(4)]
     )
-    segments, cosines, sines = [], [], []
+    positions = []
     for p in range(2):
         group_id = (line_id ^ first_bits ^ (2 * p)) * tier_count + tier_id
-        segment, position, unused = seq_layout(doc_lengths, doc_groups, group_id, places)
-        cos_part, sin_part = turn_angles(position)
-        segments.append(segment)
-        cosines.append(cos_part)
-        sines.append(sin_part)
-    cos_part = jnp.stack(cosines)
-    sin_part = jnp.stack(sines)
+        positions.append(seq_layout(doc_lengths, doc_groups, group_id, places))
+    positions = jnp.stack(positions)
+    cos_part, sin_part = turn_angles(positions)
+    nothing = jnp.zeros((2, slot_count, HDIM - ROT), f32)
+    still = jnp.zeros_like(sin_part)
+
+    def over_heads(*pieces):
+        return jnp.tile(jnp.concatenate(pieces, axis=-1), (1, 1, heads_dev))
+
+    cosine = over_heads(cos_part, cos_part, nothing + 1.0)
+    lead = over_heads(-sin_part, still, nothing)
+    trail = over_heads(still, sin_part, nothing)
+    seq_from = (places[None] - positions)[:, :, None]
+    place_col = jnp.broadcast_to(places[None, :, None], seq_from.shape)
     total_len = jnp.sum(jnp.where(doc_groups == dp_id, doc_lengths, 0), dtype=jnp.int32)
     own_valid = places[:tok_dev] < total_len
     back_own = jnp.where(own_valid[:, None], cotangent, jnp.zeros_like(cotangent))
@@ -398,85 +800,37 @@
     bias_qkv = lax.dynamic_slice(vectors[2:5], (zero_index, part_start), (3, part)).reshape(3 * part)
     bias_up = lax.dynamic_slice(vectors[5:9], (zero_index, part_start), (4, part)).reshape(4 * part)
 
-    def mm(a, b):
-        return jnp.dot(a, b, preferred_element_type=f32)
-
-    def mm_t(a, b):
-        return lax.dot_general(a, b, (((1,), (1,)), ((), ())), preferred_element_type=f32)
-
-    def t_mm(a, b):
-        return lax.dot_general(a, b, (((0,), (0,)), ((), ())), preferred_element_type=f32)
-
-    pre_qkv = mm(normed, qkv_mat) + bias_qkv
-    heads_view = pre_qkv.reshape(2, slot_count, 3, heads_dev, HDIM)
-    queries = rotate(heads_view[:, :, 0], cos_part, sin_part).astype(bf16)
-    key_rows = rotate(heads_view[:, :, 1], cos_part, sin_part).astype(bf16)
-    values = heads_view[:, :, 2].astype(bf16)
-    segment_all = jnp.stack(segments)
-    allowed = (segment_all[:, :, None] == segment_all[:, None, :]) & (
-        places[None, :, None] >= places[None, None, :]
+    bias = jnp.concatenate([bias_qkv, bias_up])[None]
+    attn, hidden, d_qkv, d_pre_up, bias_sums = local_part(
+        normed.reshape(2, slot_count, full_width),
+        back.reshape(2, slot_count, full_width),
+        qkv_mat,
+        up_mat,
+        out_mat,
+        bias,
+        cosine,
+        lead,
+        trail,
+        seq_from,
+        place_col,
+        places[None],
     )
-
-    def scores_of():
-        scores = (
-            jnp.einsum("pqhd,pkhd->phqk", queries, key_rows, preferred_element_type=f32) * score_scale
-        )
-        return jnp.where(allowed[:, None], scores, -1e30)
-
-    scores = scores_of()
-    top_score = jnp.max(scores, axis=-1, keepdims=True)
-    weights = jnp.exp(scores - top_score)
-    denominator = jnp.sum(weights, axis=-1, keepdims=True)
-    probs_low = (weights / denominator).astype(bf16)
-    attn = jnp.einsum("phqk,pkhd->pqhd", probs_low, values, preferred_element_type=f32)
-    attn = attn.reshape(rows_all, part).astype(bf16)
-    total = top_score + jnp.log(denominator)
-
-    pre_up = mm(normed, up_mat) + bias_up
-    hidden = jax.nn.gelu(pre_up, approximate=True).astype(bf16)
-
-    def scatter_rows(partial):
-        low = partial.astype(bf16).reshape(2, 4, tok_dev, full_width)
-        kept = []
-        for p in range(2):
-            near = low[p, 0::2].astype(f32) + over_row(low[p, 1::2], 1).astype(f32)
-            mine = near[0] + over_row(near[1].astype(bf16), 2).astype(f32)
-            kept.append(mine.astype(bf16))
-        out = None
-        for p in (1, 0):
-            mine = kept[p][:, :half_width]
-            theirs = over_col(kept[p][:, half_width:])
-            even_block = jnp.where(odd, theirs, mine)
-            odd_block = jnp.where(odd, mine, theirs)
-            first = over_line(even_block, 2) if p else even_block
-            both = first.astype(f32) + over_line(odd_block, 2 * p + 1).astype(f32)
-            out = both if out is None else out + both
-        return out
-
-    branch = scatter_rows(mm(attn, dense_mat) + mm(hidden, down_mat))
     out_bias = lax.dynamic_slice_in_dim(vectors[9] + vectors[10], col_start, half_width, 0)
-    block_out = (tokens.astype(f32) + branch + out_bias[None, :]).astype(bf16)
-
-    d_attn = mm_t(back, dense_mat).astype(bf16).reshape(2, slot_count, heads_dev, HDIM)
-    d_hidden = mm_t(back, down_mat)
-    unused_value, gelu_back = jax.vjp(lambda inputs: jax.nn.gelu(inputs, approximate=True), pre_up)
-    d_pre_up = gelu_back(d_hidden)[0].astype(bf16)
-
-    probs_full = jnp.exp(scores_of() - total)
-    probs_back = probs_full.astype(bf16)
-    d_probs = jnp.einsum("pqhd,pkhd->phqk", d_attn, values, preferred_element_type=f32)
-    delta_rows = jnp.sum(probs_full * d_probs, axis=-1, keepdims=True)
-    d_scores = (probs_full * (d_probs - delta_rows)).astype(bf16)
-    d_queries = jnp.einsum("phqk,pkhd->pqhd", d_scores, key_rows, preferred_element_type=f32) * score_scale
-    d_keys = jnp.einsum("phqk,pqhd->pkhd", d_scores, queries, preferred_element_type=f32) * score_scale
-    d_values = jnp.einsum("phqk,pqhd->pkhd", probs_back, d_attn, preferred_element_type=f32)
-    d_qkv = jnp.stack(
-        [rotate(d_queries, cos_part, -sin_part), rotate(d_keys, cos_part, -sin_part), d_values], axis=2
+    block_out, d_normed, grad_in, grad_out = scatter(
+        tier_count,
+        attn.reshape(rows_all, part),
+        hidden.reshape(rows_all, 4 * part),
+        d_qkv.reshape(rows_all, 3 * part),
+        d_pre_up.reshape(rows_all, 4 * part),
+        normed,
+        back,
+        qkv_mat,
+        up_mat,
+        out_mat,
+        tokens,
+        out_bias[None],
     )
-    d_qkv = d_qkv.astype(bf16).reshape(rows_all, 3 * part)
-
-    def scatter_out(grad):
-        return grad[:, :half_width] + over_col(grad[:, half_width:].astype(bf16)).astype(f32)
+    bias_sums = jnp.sum(bias_sums[:, 0], axis=0).reshape(7, part)
 
     def tier_sum(value):
         if tier_count > 1:
@@ -485,26 +839,14 @@
             )
         return value
 
-    red_dense = tier_sum(scatter_out(t_mm(attn, back)))
-    red_down = scatter_out(t_mm(hidden, back)).reshape(4, part, half_width).transpose(1, 0, 2)
-    red_down = tier_sum(red_down)
-
-    def scatter_in(grad, parts):
-        half = grad[:half_width] + over_col(grad[half_width:].astype(bf16)).astype(f32)
-        low = half.astype(bf16)
-        rows = half_width // LINE
-        pieces = []
-        for s in range(LINE):
-            piece = lax.dynamic_slice_in_dim(low, (line_id ^ s) * rows, rows, 0)
-            piece = over_line(piece, s) if s else piece
-            pieces.append(piece.reshape(rows, parts, part))
-        own = jnp.concatenate(reorder(pieces, line_id), axis=2)
-        return tier_sum(own.astype(f32))
-
-    red_up = scatter_in(t_mm(normed, d_pre_up), 4)
-    red_qkv = scatter_in(t_mm(normed, d_qkv), 3)
-
-    d_normed = scatter_rows(mm_t(d_qkv, qkv_mat) + mm_t(d_pre_up, up_mat))
+    def own_columns(value, parts):
+        value = value.astype(f32).reshape(LINE, half_width // LINE, parts, part)
+        return tier_sum(value.transpose(1, 2, 0, 3).reshape(half_width // LINE, parts, row_width))
+
+    red_qkv = own_columns(grad_in[:, :, : 3 * part], 3)
+    red_up = own_columns(grad_in[:, :, 3 * part :], 4)
+    red_dense = tier_sum(grad_out[:part])
+    red_down = tier_sum(grad_out[part:].reshape(4, part, half_width).transpose(1, 0, 2))
     tokens_own = tokens.astype(f32)
     own_sums = jnp.stack([jnp.sum(tokens_own, axis=-1), jnp.sum(tokens_own * tokens_own, axis=-1)])
     own_sums = (own_sums + over_col(own_sums)) / full_width
@@ -519,12 +861,7 @@
     grad_tokens = inv_own * (d_hat - hat_sums[0][:, None] - centred * hat_sums[1][:, None]) + back_float
 
     early = jnp.zeros((9, full_width), f32)
-    early = lax.dynamic_update_slice(
-        early, jnp.sum(d_qkv.astype(f32), axis=0).reshape(3, part), (zero_index, part_start)
-    )
-    early = lax.dynamic_update_slice(
-        early, jnp.sum(d_pre_up.astype(f32), axis=0).reshape(4, part), (jnp.int32(3), part_start)
-    )
+    early = lax.dynamic_update_slice(early, bias_sums, (zero_index, part_start))
     out_sums = jnp.sum(back_float, axis=0)
     early = lax.dynamic_update_slice(early, jnp.stack([out_sums, out_sums]), (jnp.int32(7), col_start))
     late = lax.dynamic_update_slice(

time: 719 us -> 460 us (0.64)
  Pallas kernels: 133 us -> 327 us
  waiting for transfers between devices: 203 us -> 15 us
  matrix products: 131 us -> 0 us
  starting transfers between devices: 72.9 us -> 15.1 us
  other arithmetic: 86.3 us -> 41.3 us
  local copies, waits for them, and re-layouts: 80.1 us -> 55.4 us
    pallas_call x0 -> x2, Pallas kernels: none -> 194 us  [the longest x1 146 us: scatter(): pl.pallas_call(functools.partial(scatter_kernel, tier_count, order or sca...]
    dot_general x18 -> x0, matrix products: 131 us -> none  [the longest x4 38.9 us: mm_t(): lax.dot_general(a, b, (((1,), (1,)), ((), ())), preferred_element_type=f32)]
    ppermute x14 -> x6, waiting for transfers between devices: 78.3 us -> 5.46 us  [over_row(): return lax.ppermute(value, 'row', [(i, i ^ bits) for i in range(row_count)])]
    ppermute x18 -> x6, waiting for transfers between devices: 65.5 us -> 4.77 us  [over_line(): return lax.ppermute(value, 'dp', pairs)]
    ppermute x12 -> x4, waiting for transfers between devices: 59.2 us -> 4.79 us  [over_col(): return lax.ppermute(value, 'col', [(0, 1), (1, 0)])]
    ppermute x18 -> x6, starting transfers between devices: 49.3 us -> 6.42 us  [over_line(): return lax.ppermute(value, 'dp', pairs)]
    convert_element_type x9 -> x2, other arithmetic: 21.2 us -> 0.09 us  [the longest x1 0.08 us: pieces_of(): low = tier_gather(weight.astype(bf16))]
    slice x14 -> x1, local copies, waits for them, and re-layouts: 17.8 us -> 1.98 us  [per_device(): grad_out[part:].reshape(4, part, half_width).transpose(1, 0, 2)]
  transfers between devices with their start and end apart: 44 -> 16, of which waited for: 16 -> 7; matrix products, arithmetic and copies ran while one was open for 21% -> 12% of each run, Pallas kernels for 0% -> 32%
where the time goes in v2:
time: 460 us; the launch traced here: 456 us
  Pallas kernels  327 us (71%)
  local copies, waits for them, and re-layouts  55.4 us (12%)
  other arithmetic  41.3 us (9%)
  starting transfers between devices  15.1 us (3%)
  waiting for transfers between devices  15 us (3%)
    pallas_call x1, Pallas kernels, scatter(): pl.pallas_call(functools.partial(scatter_kernel, tier_count, order or sca...  146 us
    pallas_call x1, Pallas kernels, gather(): pl.pallas_call(functools.partial(gather_kernel, tier_count, order), out_s...  133 us
    pallas_call x1, Pallas kernels, local_part(): pl.pallas_call(local_kernel, grid=(groups,), out_shape=[like(part), like(...  48.1 us
    unnamed x65, local copies, waits for them, and re-layouts  27.3 us
    sub x5, other arithmetic, adamw(): return (first_next, second_next, weight - rate * (update + decay * weight))  20.6 us
  transfers between devices with their start and end apart: 16, of which 7 were waited for; matrix products, arithmetic and copies ran while one was open for 12% of the time, Pallas kernels for 32%

profile of v2, /device:TPU:0, one launch (start us, length us, event | category | flops | bytes accessed | tf_op | source)
XLA Modules:
  0.0 455.8 jit_solution(16360678390229464393)
XLA Ops:
  0.7 1.0 fusion.33
  1.7 0.9 slice.48
  2.5 0.9 slice.49
  3.4 0.7 fusion.20
  4.1 1.3 fusion.31
  8.4 1.3 copy.104.lead_ref
  9.8 1.3 copy.105.trail_ref
  11.4 1.3 copy.103.cos_ref
  12.9 1.0 copy.101
  14.6 1.9 copy.96
  16.6 1.1 copy.97
  17.7 1.5 copy.100.wq
  19.2 2.1 convert_bitcast_fusion
  21.4 1.3 copy.99
  23.3 1.3 bitcast_bitcast_fusion
  24.6 1.9 reshape.687.wu
  27.2 1.2 add_subtract_fusion.from_ref
  28.4 1.3 convert_reduce_fusion.1
  29.7 1.3 pad_maximum_fusion.dh
  31.1 133.0 %shard_map.314 = (bf16[2,4,256,2048]{3,2,1,0:T(8,128)(2,1)S(1)}, bf16[2,4,256,2048]{3,2,1,0:T(8,128)(2,1)}, bf16[2,4,256,384]{3,2,1,0:T(8,128)(2,1)S(1)}, bf16[2...) custom-call(bf16[256,1024]{1,0:T(8,128)(2,1)S(1)} %copy-done.1, bf16[256,1024]{1,0:T(8,128)(2,1)S(1)} %get-tuple-element.112.cot, ...), custom_call_target="tpu_custom_call" | custom-call | tf_op jit(solution)/shard_map/pallas_call | solution.py:253
  164.1 3.2 copy-done
  167.3 1.5 copy-done.3
  168.8 1.3 copy-done.4
  170.1 1.1 copy-done.5
  171.3 1.2 sub.162.place_ref
  172.4 48.1 %shard_map.315 = (bf16[2,1024,128]{2,1,0:T(8,128)(2,1)}, bf16[2,1024,512]{2,1,0:T(8,128)(2,1)}, bf16[2,1024,384]{2,1,0:T(8,128)(2,1)}, bf16[2,1024,512]{2,1,0:T(8,128)(2,1)}, f32[2,8,896]{2,1,0:T(8,128)}) custom-call(bf16[2,1024,2048]{2,1,0:T(8,128)(2,1)} %bitcast.93, bf16[2,1024,2048]{2,1,0:T(8,128)(2,1)} %bitcast.99, bf16[2048,384]{1,0:T(8,128)(2,1)} %bitcast.97, ...), custom_call_target="tpu_custom_call" | custom-call | tf_op jit(solution)/shard_map/pallas_call | solution.py:377
  220.5 0.8 slice_reduce_fusion
  221.9 0.8 dynamic_update_slice.11
  222.8 3.1 collective-permute-start.11
  226.2 1.1 collective-permute-start
  227.9 146.2 %shard_map.316 = (bf16[256,1024]{1,0:T(8,128)(2,1)}, f32[256,1024]{1,0:T(8,128)}, bf16[4,256,896]{2,1,0:T(8,128)(2,1)}, f32[640,1024]{1,0:T(8,128)}) custom-call(bf16[2048,128]{1,0:T(8,128)(2,1)} %bitcast.112, bf16[2048,512]{1,0:T(8,128)(2,1)} %bitcast.109, bf16[2048,384]{1,0:T(8,128)(2,1)} %bitcast.111, bf16[2048,512]{1,0:T(8,128)(2,1)} %bitcast.110, ...), custom_call_target="tpu_custom_call" | custom-call | tf_op jit(solution)/shard_map/pallas_call | solution.py:660
  374.0 2.5 slice_convert_fusion.1
  376.5 1.6 slice_convert_fusion
  378.1 3.0 copy.107
  381.2 2.7 copy.108
  383.8 3.0 copy.106
  386.8 3.0 copy.109
  389.9 3.1 reshape.720
  393.0 2.0 slice.59
  395.5 5.1 %multiply_subtract_fusion.2 = (f32[256,3,512]{0,2,1:T(8,128)}, f32[256,3,512]{0,2,1:T(8,128)}, f32[256,3,512]{0,2,1:T(8,128)}) fusion(f32[256,3,512]{0,2,1:T(8,128)S(1)} %copy-done.7, f32[256,3,4,128]{0,3,2,1:T(8,128)S(1)} %copy-done.12, f32[256,3,512]{0,2,1:T(8,128)} %copy.109, f32[256,3,512]{0,2,1:T(8,128)} %copy.106), kind=kLoop, calls=%fused_computation.14 | loop fusion | flops 5898240 | bytes 11010048 | tf_op jit(solution)/shard_map/sub | solution.py:56
  400.6 1.0 copy-done.15
  401.6 5.2 %multiply_subtract_fusion.1 = (f32[256,4,512]{2,1,0:T(4,128)}, f32[256,4,512]{2,1,0:T(4,128)}, f32[256,4,512]{2,1,0:T(4,128)}) fusion(f32[256,4,512]{2,1,0:T(4,128)S(1)} %copy-done.9, f32[256,4,512]{2,1,0:T(4,128)S(1)} %copy-done.14, f32[256,4,512]{2,1,0:T(4,128)S(1)} %copy-done.15, f32[4,256,4,128]{3,2,1,0:T(4,128)S(1)} %copy-done.11), kind=kLoop, calls=%fused_computation.10 | loop fusion | flops 7864320 | bytes 14680064 | tf_op jit(solution)/shard_map/sub | solution.py:56
  406.8 7.0 %multiply_subtract_fusion = (f32[128,4,1024]{2,1,0:T(4,128)}, f32[128,4,1024]{2,1,0:T(4,128)}, f32[128,4,1024]{2,1,0:T(4,128)}) fusion(f32[128,4,1024]{2,1,0:T(4,128)S(1)} %copy-done.10, f32[4,128,1024]{2,1,0:T(8,128)S(1)} %bitcast.101, f32[128,4,1024]{2,1,0:T(4,128)S(1)} %copy-done.16, f32[128,4,1024]{2,1,0:T(4,128)S(1)} %copy-done.17), kind=kLoop, calls=%fused_computation.9 | loop fusion | flops 7864320 | bytes 14680064 | tf_op jit(solution)/shard_map/sub | solution.py:56
  413.9 2.5 multiply_subtract_fusion.3
  416.3 3.0 copy.114
  419.3 3.0 copy.115
  422.4 3.1 copy.116
  426.1 0.8 collective-permute-start.1
  427.0 0.9 collective-permute-start.2
  427.9 1.9 collective-permute-done.1
  429.8 1.6 collective-permute-start.4
  431.4 1.3 collective-permute-done.2
  432.7 0.7 collective-permute-start.9
  433.8 2.2 collective-permute-start.6
  436.0 3.4 collective-permute-done.9
  439.6 1.6 collective-permute-start.13
  441.5 1.2 collective-permute-start.8
  442.7 2.5 collective-permute-done.12
  445.2 2.9 collective-permute-done.13
  448.2 1.2 collective-permute-start.15
  449.4 1.4 convert_add_fusion
  450.8 2.9 collective-permute-done.15
  453.7 0.8 multiply_subtract_fusion.4
  454.6 0.8 copy.132
  (129 shorter events, 9.1 us)
Async XLA Ops:
  5.9 165.4 %copy-start.28 = (s32[1024]{0:T(1024)}, s32[1024]{0:T(1024)S(1)}, u32[]{:S(2)}) copy-start(s32[1024]{0:T(1024)S(1)} %pad_add_fusion) | copy-start | bytes 12292
  16.5 2.7 copy-start.6
  19.2 3.4 copy-start.18
  21.3 2.0 copy-start.8
  23.3 3.9 copy-start.20
  28.4 2.7 copy-start.1
  164.1 3.2 copy-start
  167.3 1.5 copy-start.3
  168.8 1.3 copy-start.4
  170.1 1.1 copy-start.5
  222.8 213.2 %collective-permute-start.10 = (f32[9,2048]{1,0:T(8,128)S(1)}, f32[9,2048]{1,0:T(8,128)S(1)}, u32[]{:S(2)}, u32[]{:S(2)}) collective-permute-start(f32[9,2048]{1,0:T(8,128)S(1)} %dynamic_update_slice.11), channel_id=1, source_target_pairs={{0,16},{8,24},{16,0},{24,8},{1,17},{9,25},{17,1},{25,9},{2,18},{10... | collective-permute-start | bytes 221192 | tf_op jit(solution)/shard_map/ppermute | solution.py:720
  222.8 213.2 %collective-permute-start.11 = (f32[9,2048]{1,0:T(8,128)S(1)}, f32[9,2048]{1,0:T(8,128)S(1)}, u32[]{:S(2)}, u32[]{:S(2)}) collective-permute-start(f32[9,2048]{1,0:T(8,128)S(1)} %dynamic_update_slice.11), channel_id=1, source_target_pairs={{0,8},{8,0},{16,24},{24,16},{1,9},{9,1},{17,25},{25,17},{2,10},{10... | collective-permute-start | bytes 221192 | tf_op jit(solution)/shard_map/ppermute | solution.py:720
  226.2 199.4 %collective-permute-start = (f32[2,256]{1,0:T(2,128)S(1)}, f32[2,256]{1,0:T(2,128)S(1)}, u32[]{:S(2)}, u32[]{:S(2)}) collective-permute-start(f32[2,256]{1,0:T(2,128)S(1)} %pad_maximum_fusion.7), channel_id=1, source_target_pairs={{0,1},{1,0},{2,3},{3,2},{4,5},{5,4},{6,7},{7,6},{8,9},{9,8},{10,11... | collective-permute-start | bytes 6152 | tf_op jit(solution)/shard_map/ppermute | solution.py:726
  374.0 2.5 copy-start.21
  393.0 2.0 copy-start.7
  393.0 2.5 copy-start.12
  395.5 5.1 %copy-start.9 = (f32[256,4,512]{2,1,0:T(4,128)S(1)}, f32[256,4,512]{2,1,0:T(4,128)}, u32[]{:S(2)}) copy-start(f32[256,4,512]{2,1,0:T(4,128)} %param.24) | copy-start | bytes 6291460
  395.5 5.1 %copy-start.11 = (f32[4,256,4,128]{3,2,1,0:T(4,128)S(1)}, f32[4,256,4,128]{3,2,1,0:T(4,128)}, u32[]{:S(2)}) copy-start(f32[4,256,4,128]{3,2,1,0:T(4,128)} %reshape.720) | copy-start | bytes 6291460
  395.5 5.1 %copy-start.14 = (f32[256,4,512]{2,1,0:T(4,128)S(1)}, f32[256,4,512]{2,1,0:T(4,128)}, u32[]{:S(2)}) copy-start(f32[256,4,512]{2,1,0:T(4,128)} %param.31) | copy-start | bytes 6291460
  395.5 6.1 %copy-start.15 = (f32[256,4,512]{2,1,0:T(4,128)S(1)}, f32[256,4,512]{2,1,0:T(4,128)}, u32[]{:S(2)}) copy-start(f32[256,4,512]{2,1,0:T(4,128)} %param.30) | copy-start | bytes 6291460
  401.6 5.2 %copy-start.10 = (f32[128,4,1024]{2,1,0:T(4,128)S(1)}, f32[128,4,1024]{2,1,0:T(4,128)}, u32[]{:S(2)}) copy-start(f32[128,4,1024]{2,1,0:T(4,128)} %param.26) | copy-start | bytes 6291460
  401.6 5.2 %copy-start.16 = (f32[128,4,1024]{2,1,0:T(4,128)S(1)}, f32[128,4,1024]{2,1,0:T(4,128)}, u32[]{:S(2)}) copy-start(f32[128,4,1024]{2,1,0:T(4,128)} %param.35) | copy-start | bytes 6291460
  401.6 5.2 %copy-start.17 = (f32[128,4,1024]{2,1,0:T(4,128)S(1)}, f32[128,4,1024]{2,1,0:T(4,128)}, u32[]{:S(2)}) copy-start(f32[128,4,1024]{2,1,0:T(4,128)} %param.34) | copy-start | bytes 6291460
  406.8 7.0 %copy-start.19 = (f32[128,1024]{1,0:T(8,128)S(1)}, f32[128,1024]{1,0:T(8,128)}, u32[]{:S(2)}) copy-start(f32[128,1024]{1,0:T(8,128)} %param.25) | copy-start | bytes 1572868
  406.8 7.0 %copy-start.22 = (f32[128,1024]{1,0:T(8,128)S(1)}, f32[128,1024]{1,0:T(8,128)}, u32[]{:S(2)}) copy-start(f32[128,1024]{1,0:T(8,128)} %param.33) | copy-start | bytes 1572868
  406.8 7.0 %copy-start.23 = (f32[128,1024]{1,0:T(8,128)S(1)}, f32[128,1024]{1,0:T(8,128)}, u32[]{:S(2)}) copy-start(f32[128,1024]{1,0:T(8,128)} %param.32) | copy-start | bytes 1572868
  422.4 3.2 copy-start.2
  422.4 3.2 copy-start.13
  426.1 3.6 collective-permute-start.1
  427.0 5.7 %collective-permute-start.2 = (f32[2,2048]{1,0:T(2,128)S(1)}, f32[2,2048]{1,0:T(2,128)S(1)}, u32[]{:S(2)}, u32[]{:S(2)}) collective-permute-start(f32[2,2048]{1,0:T(2,128)S(1)} %maximum_dynamic-update-slice_fusion), channel_id=1, source_target_pairs={{0,24},{8,16},{16,8},{24,0},{1,25},{9,17},{17,9},{25,1},{2,26},{10... | collective-permute-start | bytes 49160 | tf_op jit(solution)/shard_map/ppermute | solution.py:720
  427.9 5.5 %collective-permute-start.3 = (f32[2,2048]{1,0:T(2,128)S(1)}, f32[2,2048]{1,0:T(2,128)S(1)}, u32[]{:S(2)}, u32[]{:S(2)}) collective-permute-start(f32[2,2048]{1,0:T(2,128)S(1)} %maximum_dynamic-update-slice_fusion), channel_id=1, source_target_pairs={{0,16},{8,24},{16,0},{24,8},{1,17},{9,25},{17,1},{25,9},{2,18},{10... | collective-permute-start | bytes 49160 | tf_op jit(solution)/shard_map/ppermute | solution.py:720
  429.8 3.7 collective-permute-start.4
  432.7 6.8 %collective-permute-start.9 = (f32[9,2048]{1,0:T(8,128)S(1)}, f32[9,2048]{1,0:T(8,128)S(1)}, u32[]{:S(2)}, u32[]{:S(2)}) collective-permute-start(f32[9,2048]{1,0:T(8,128)S(1)} %dynamic_update_slice.11), channel_id=1, source_target_pairs={{0,24},{8,16},{16,8},{24,0},{1,25},{9,17},{17,9},{25,1},{2,26},{10... | collective-permute-start | bytes 221192 | tf_op jit(solution)/shard_map/ppermute | solution.py:720
  433.5 7.7 %collective-permute-start.5 = (f32[2,2048]{1,0:T(2,128)S(1)}, f32[2,2048]{1,0:T(2,128)S(1)}, u32[]{:S(2)}, u32[]{:S(2)}) collective-permute-start(f32[2,2048]{1,0:T(2,128)S(1)} %select_add_fusion.3), channel_id=1, source_target_pairs={{0,6},{2,4},{4,2},{6,0},{1,7},{3,5},{5,3},{7,1},{8,14},{10,12},{12... | collective-permute-start | bytes 49160 | tf_op jit(solution)/shard_map/ppermute | solution.py:723
  433.8 7.6 %collective-permute-start.6 = (f32[2,2048]{1,0:T(2,128)S(1)}, f32[2,2048]{1,0:T(2,128)S(1)}, u32[]{:S(2)}, u32[]{:S(2)}) collective-permute-start(f32[2,2048]{1,0:T(2,128)S(1)} %select_add_fusion.3), channel_id=1, source_target_pairs={{0,4},{2,6},{4,0},{6,2},{1,5},{3,7},{5,1},{7,3},{8,12},{10,14},{12... | collective-permute-start | bytes 49160 | tf_op jit(solution)/shard_map/ppermute | solution.py:723
  436.0 5.4 %collective-permute-start.7 = (f32[2,2048]{1,0:T(2,128)S(1)}, f32[2,2048]{1,0:T(2,128)S(1)}, u32[]{:S(2)}, u32[]{:S(2)}) collective-permute-start(f32[2,2048]{1,0:T(2,128)S(1)} %select_add_fusion.3), channel_id=1, source_target_pairs={{0,2},{2,0},{4,6},{6,4},{1,3},{3,1},{5,7},{7,5},{8,10},{10,8},{12,... | collective-permute-start | bytes 49160 | tf_op jit(solution)/shard_map/ppermute | solution.py:723
  439.5 5.7 %collective-permute-start.12 = (f32[9,2048]{1,0:T(8,128)S(1)}, f32[9,2048]{1,0:T(8,128)S(1)}, u32[]{:S(2)}, u32[]{:S(2)}) collective-permute-start(f32[9,2048]{1,0:T(8,128)S(1)} %select_add_fusion.1), channel_id=1, source_target_pairs={{0,6},{2,4},{4,2},{6,0},{1,7},{3,5},{5,3},{7,1},{8,14},{10,12},{12... | collective-permute-start | bytes 221192 | tf_op jit(solution)/shard_map/ppermute | solution.py:723
  439.6 8.6 %collective-permute-start.13 = (f32[9,2048]{1,0:T(8,128)S(1)}, f32[9,2048]{1,0:T(8,128)S(1)}, u32[]{:S(2)}, u32[]{:S(2)}) collective-permute-start(f32[9,2048]{1,0:T(8,128)S(1)} %select_add_fusion.1), channel_id=1, source_target_pairs={{0,4},{2,6},{4,0},{6,2},{1,5},{3,7},{5,1},{7,3},{8,12},{10,14},{12... | collective-permute-start | bytes 221192 | tf_op jit(solution)/shard_map/ppermute | solution.py:723
  441.2 6.9 %collective-permute-start.14 = (f32[9,2048]{1,0:T(8,128)S(1)}, f32[9,2048]{1,0:T(8,128)S(1)}, u32[]{:S(2)}, u32[]{:S(2)}) collective-permute-start(f32[9,2048]{1,0:T(8,128)S(1)} %select_add_fusion.1), channel_id=1, source_target_pairs={{0,2},{2,0},{4,6},{6,4},{1,3},{3,1},{5,7},{7,5},{8,10},{10,8},{12,... | collective-permute-start | bytes 221192 | tf_op jit(solution)/shard_map/ppermute | solution.py:723
  441.5 12.2 %copy-start.25 = (f32[11,2048]{1,0:T(8,128)S(1)}, f32[11,2048]{1,0:T(8,128)}, u32[]{:S(2)}) copy-start(f32[11,2048]{1,0:T(8,128)} %param.27) | copy-start | bytes 270340
  441.5 12.2 %copy-start.26 = (f32[11,2048]{1,0:T(8,128)S(1)}, f32[11,2048]{1,0:T(8,128)}, u32[]{:S(2)}) copy-start(f32[11,2048]{1,0:T(8,128)} %param.37) | copy-start | bytes 270340
  441.5 12.2 %copy-start.27 = (f32[11,2048]{1,0:T(8,128)S(1)}, f32[11,2048]{1,0:T(8,128)}, u32[]{:S(2)}) copy-start(f32[11,2048]{1,0:T(8,128)} %param.36) | copy-start | bytes 270340
  441.5 9.3 %collective-permute-start.8 = (f32[2,2048]{1,0:T(2,128)S(1)}, f32[2,2048]{1,0:T(2,128)S(1)}, u32[]{:S(2)}, u32[]{:S(2)}) collective-permute-start(f32[2,2048]{1,0:T(2,128)S(1)} %select_add_fusion.2), channel_id=1, source_target_pairs={{0,1},{1,0},{2,3},{3,2},{4,5},{5,4},{6,7},{7,6},{8,9},{9,8},{10,11... | collective-permute-start | bytes 49160 | tf_op jit(solution)/shard_map/ppermute | solution.py:726
  448.2 5.4 %collective-permute-start.15 = (f32[9,2048]{1,0:T(8,128)S(1)}, f32[9,2048]{1,0:T(8,128)S(1)}, u32[]{:S(2)}, u32[]{:S(2)}) collective-permute-start(f32[9,2048]{1,0:T(8,128)S(1)} %select_add_fusion), channel_id=1, source_target_pairs={{0,1},{1,0},{2,3},{3,2},{4,5},{5,4},{6,7},{7,6},{8,9},{9,8},{10,11... | collective-permute-start | bytes 221192 | tf_op jit(solution)/shard_map/ppermute | solution.py:726
  449.4 5.2 %copy-start.24 = (bf16[256,1024]{1,0:T(8,128)(2,1)S(1)}, bf16[256,1024]{1,0:T(8,128)(2,1)}, u32[]{:S(2)}) copy-start(bf16[256,1024]{1,0:T(8,128)(2,1)} %get-tuple-element.174) | copy-start | bytes 1572868

commit v3 on v2

--- a/solution.py
+++ b/solution.py
@@ -19,32 +19,6 @@
 eps_norm = 1e-05
 f32 = jnp.float32
 bf16 = jnp.bfloat16
-
-
-def seq_layout(doc_lengths, doc_groups, group_id, places):
-    in_group = (doc_groups == group_id).astype(jnp.int32)
-    group_sizes = doc_lengths * in_group
-    seq_ends = jnp.cumsum(group_sizes, dtype=jnp.int32)
-    starts = seq_ends - group_sizes
-    total_len = jnp.sum(group_sizes, dtype=jnp.int32)
-    member = (
-        (places[:, None] >= starts[None, :])
-        & (places[:, None] < seq_ends[None, :])
-        & (in_group[None, :] == 1)
-    )
-    member = member.astype(jnp.int32)
-    number = jnp.arange(doc_lengths.shape[0], dtype=jnp.int32) + 1
-    segment = jnp.sum(member * number[None, :], axis=1, dtype=jnp.int32) - 1
-    seq_first = jnp.sum(member * starts[None, :], axis=1, dtype=jnp.int32)
-    position = jnp.where(segment >= 0, places - seq_first, places - total_len)
-    return position
-
-
-def turn_angles(position):
-    half_rot = ROT // 2
-    freq_base = jnp.power(10000.0, -2.0 * jnp.arange(half_rot, dtype=jnp.float32) / ROT)
-    angle = position.astype(jnp.float32)[..., None] * freq_base
-    return (jnp.cos(angle), jnp.sin(angle))
 
 
 def adamw(weight, first_moment, second_moment, gradient, rate, decay):
@@ -90,8 +64,10 @@
 
 CH = 2
 
-def gather_kernel(tier_count, order, tok, cot, norm_ref, wq, wu, dh, x_out, b_out, wq_out, wu_out, d_out,
-                  tz, cz, ty, xs, send_sems, recv_sems, local_sems):
+def gather_kernel(tier_count, order, lengths, groups, tok, cot, vec_ref, w_qkv, w_up, w_dense, w_down,
+                  x_out, b_out, wq_out, wu_out, d_out,
+                  tz, cz, ty, xs, cot_s, qkv_f, up_f, dense_f, down_f, wq, wu, dh,
+                  send_sems, recv_sems, local_sems, load_sems):
     line_id, flips, line, core, far, col = neighbours(tier_count)
     bit = (line_id % 2 + lax.axis_index("col")) % 2
     middle = (line_id == 1) | (line_id == 2)
@@ -170,6 +146,9 @@
             self.spread[c, p].wait_recv()
             last.append(send(self.out.at[p, 2, cut(c)], self.out.at[p, 3, cut(c)], core))
 
+    norm_ref = [[vec_ref.at[i:i + 1, pl.ds(pl.multiple_of(side * half, half), half)] for i in range(2)]
+                for side in (lax.axis_index("col"), 1 - lax.axis_index("col"))]
+
     def norm(c, p):
         step = 64
         def body(i, carry):
@@ -180,8 +159,8 @@
             mean = (jnp.sum(one, axis=-1, keepdims=True) + jnp.sum(two, axis=-1, keepdims=True)) / width
             square = (jnp.sum(one * one, axis=-1, keepdims=True) + jnp.sum(two * two, axis=-1, keepdims=True)) / width
             inv = lax.rsqrt(square - mean * mean + eps_norm)
-            xs[p, at, pl.ds(0, half)] = ((one - mean) * inv * norm_ref[0:1, 0:half] + norm_ref[1:2, 0:half]).astype(bf16)
-            xs[p, at, pl.ds(half, half)] = ((two - mean) * inv * norm_ref[0:1, half:] + norm_ref[1:2, half:]).astype(bf16)
+            xs[p, at, pl.ds(0, half)] = ((one - mean) * inv * norm_ref[0][0][...] + norm_ref[0][1][...]).astype(bf16)
+            xs[p, at, pl.ds(half, half)] = ((two - mean) * inv * norm_ref[1][0][...] + norm_ref[1][1][...]).astype(bf16)
             return carry
         lax.fori_loop(0, chunk // step, body, 0)
 
@@ -203,6 +182,36 @@
                 last.append(send(self.out.at[0, flips[s]], self.out.at[1, flips[s]], col))
 
     part = dh.shape[0] // 5
+    loads = []
+    for i, (src, dst) in enumerate(((w_qkv, qkv_f), (w_up, up_f), (w_dense, dense_f), (w_down, down_f), (cot, cot_s))):
+        loads.append(pltpu.make_async_copy(src, dst, load_sems.at[i]))
+        loads[-1].start()
+
+    def prepare(what):
+        if what == 0:
+            loads[0].wait()
+            for j in range(LINE):
+                for k in range(3):
+                    wq[j, :, k * part:(k + 1) * part] = qkv_f[k, :, j * part:(j + 1) * part].astype(bf16)
+        if what == 1:
+            loads[1].wait()
+            for j in range(LINE):
+                for k in range(4):
+                    wu[j, :, k * part:(k + 1) * part] = up_f[:, k, j * part:(j + 1) * part].astype(bf16)
+        if what == 2:
+            loads[2].wait()
+            dh[0:part, :] = dense_f[...].astype(bf16)
+        if what == 3:
+            loads[3].wait()
+            for k in range(4):
+                dh[(k + 1) * part:(k + 2) * part, :] = down_f[:, k, :].astype(bf16)
+        if what == 4:
+            loads[4].wait()
+            total = jnp.int32(0)
+            for i in range(lengths.shape[0]):
+                total = total + jnp.where(groups[i] == lax.axis_index("dp"), lengths[i], 0)
+            place = lax.axis_index("row") * rows + lax.broadcasted_iota(jnp.int32, (rows, half), 0)
+            cot_s[...] = jnp.where(place < total, cot_s[...], jnp.zeros_like(cot_s))
 
     def dense(i):
         at = pl.ds(i * part, part)
@@ -210,10 +219,11 @@
 
     meet([line[1], line[2], line[3], core, far, col])
     T = Stream(tok, tz, x_out, True)
-    C = Stream(cot, cz, b_out, False)
+    C = Stream(cot_s, cz, b_out, False)
     Q = Weight(wq, wq_out)
     U = Weight(wu, wu_out)
     for what, *args in order:
+        if what == "P": prepare(*args)
         if what == "Ts": T.start(*args)
         if what == "Ty": T.swap_cols(*args)
         if what == "Tx": T.give(*args)
@@ -239,28 +249,34 @@
     for copy in mid_sent:
         pl.when(middle)(copy.wait_send)
 
-ORDER_A = [("Ts",0),("Ts",1),("Qo",),("Uo",),("D",0),("Dl",),
+ORDER_A = [("Ts",0),("Ts",1),("P",0),("Qo",),("P",1),("Uo",),("P",2),("D",0),("P",3),("Dl",),("P",4),
  ("Ty",0,0),("Ty",0,1),("Tx",0,0),("Tx",0,1),
  ("Ty",1,0),("Ty",1,1),("Cs",0),("Tx",1,0),("Tx",1,1),("D",1),("D",2),
  ("Tk",0,0),("Tk",0,1),("Cy",0,0),("Cy",0,1),("Qs",),("Cs",1),("Cx",0,0),("Cx",0,1),("Tk",1,0),("Tk",1,1),
  ("Qy",),("Cy",1,0),("Cy",1,1),("Us",),("Cx",1,0),("Cx",1,1),("D",3),("D",4),("Ck",0,0),("Ck",0,1),
  ("Uy",),("Ck",1,0),("Ck",1,1)]
 
-def gather(tier_count, tok, cot, norm_vec, wq, wu, dh, order=ORDER_A):
+def gather(tier_count, lengths, groups, tok, cot, vectors, w_qkv, w_up, w_dense, w_down):
     rows, half = tok.shape
+    part = w_dense.shape[0]
+    c_rows = w_up.shape[0]
     sds = jax.ShapeDtypeStruct
     any_ = pl.BlockSpec(memory_space=pl.ANY)
+    smem = pl.BlockSpec(memory_space=pltpu.SMEM)
     return pl.pallas_call(
-        functools.partial(gather_kernel, tier_count, order),
+        functools.partial(gather_kernel, tier_count, ORDER_A),
         out_shape=[sds((2, 4, rows, 2 * half), bf16), sds((2, 4, rows, 2 * half), bf16),
-                   sds((2, *wq.shape), bf16), sds((2, *wu.shape), bf16), sds((dh.shape[0], 2 * half), bf16)],
-        in_specs=[any_, any_, pl.BlockSpec(memory_space=pltpu.VMEM), any_, any_, any_],
+                   sds((2, LINE, c_rows, 3 * part), bf16), sds((2, LINE, c_rows, 4 * part), bf16), sds((5 * part, 2 * half), bf16)],
+        in_specs=[smem, smem, any_, any_, pl.BlockSpec(memory_space=pltpu.VMEM), any_, any_, any_, any_],
         out_specs=[any_] * 5,
         scratch_shapes=[pltpu.VMEM((4, rows, half), bf16), pltpu.VMEM((4, rows, half), bf16), pltpu.VMEM((2, rows, half), bf16),
-                        pltpu.VMEM((2, rows, 2 * half), bf16),
-                        pltpu.SemaphoreType.DMA((80,)), pltpu.SemaphoreType.DMA((80,)), pltpu.SemaphoreType.DMA((24,))],
-        compiler_params=pltpu.CompilerParams(collective_id=1, has_side_effects=True, vmem_limit_bytes=32 << 20),
-    )(tok, cot, norm_vec, wq, wu, dh)
+                        pltpu.VMEM((2, rows, 2 * half), bf16), pltpu.VMEM((rows, half), bf16),
+                        pltpu.VMEM(w_qkv.shape, f32), pltpu.VMEM(w_up.shape, f32), pltpu.VMEM(w_dense.shape, f32), pltpu.VMEM(w_down.shape, f32),
+                        pltpu.VMEM((LINE, c_rows, 3 * part), bf16), pltpu.VMEM((LINE, c_rows, 4 * part), bf16), pltpu.VMEM((5 * part, half), bf16),
+                        pltpu.SemaphoreType.DMA((80,)), pltpu.SemaphoreType.DMA((80,)), pltpu.SemaphoreType.DMA((24,)), pltpu.SemaphoreType.DMA((5,))],
+        compiler_params=pltpu.CompilerParams(collective_id=1, has_side_effects=True, vmem_limit_bytes=60 << 20),
+    )(lengths, groups, tok, cot, vectors, w_qkv, w_up, w_dense, w_down)
+
 
 def mm(a, b):
     return jnp.dot(a, b, preferred_element_type=f32)
@@ -283,18 +299,64 @@
     return v * outer, outer + 0.5 * v * (1.0 - tanh * tanh) * slope
 
 
-def local_kernel(x_ref, b_ref, wq_ref, wu_ref, d_ref, bias_ref, cos_ref, lead_ref, trail_ref, from_ref, place_ref, key_ref,
+def local_kernel(tier_count, lengths, groups, x_ref, b_ref, wq_ref, wu_ref, d_ref, bias_ref,
                  attn_ref, hidden_ref, dqkv_ref, dup_ref, sums_ref,
-                 q_s, k_s, v_s, da_s, dk_s, dv_s):
+                 q_s, k_s, v_s, da_s, dk_s, dv_s, cos_s, sin_s, from_s):
     slots, part = q_s.shape
-    qb = 256
+    qb = slots // 4
     scale = HDIM ** (-0.5)
     quarter = ROT // 2
+
+    row_id = lax.axis_index("row")
+    quarters = [row_id, row_id + 1 - 2 * (row_id % 2), (row_id + 2) % 4, 3 - row_id]
+    rows = slots // 4
+    line_id, tier_id = lax.axis_index("dp") // tier_count, lax.axis_index("dp") % tier_count
+    bit = (line_id % 2 + lax.axis_index("col")) % 2
+    group = line_id + bit * (1 - 2 * (line_id % 2))
+    group = ((group + 2 * pl.program_id(0)) % 4) * tier_count + tier_id
+    lanes = lax.broadcasted_iota(jnp.int32, (1, part), 1) % HDIM
+    turned = lanes < ROT
+    lead = lanes < quarter
+    powers = (lanes % quarter).astype(f32) * (-2.0 / ROT)
+    speed = jnp.where(turned, jnp.exp(powers * 9.210340371976184), 0.0)
+    key_place = jnp.concatenate([quarters[t] * rows + lax.broadcasted_iota(jnp.int32, (1, rows), 1) for t in range(4)], axis=1)
+    fine = lax.broadcasted_iota(jnp.int32, (32, part), 0).astype(f32) * speed
+    fine_cos, fine_sin = jnp.cos(fine), jnp.sin(fine)
+
+    def fill(t, carry):
+        quarter_id = jnp.where(t == 0, quarters[0], jnp.where(t == 1, quarters[1], jnp.where(t == 2, quarters[2], quarters[3])))
+        base = quarter_id * rows
+        coarse = (base + 32 * lax.broadcasted_iota(jnp.int32, (rows // 32, part), 0)).astype(f32) * speed
+        coarse_cos, coarse_sin = jnp.cos(coarse), jnp.sin(coarse)
+        place_cos = jnp.concatenate([coarse_cos[i:i + 1] * fine_cos - coarse_sin[i:i + 1] * fine_sin for i in range(rows // 32)])
+        place_sin = jnp.concatenate([coarse_sin[i:i + 1] * fine_cos + coarse_cos[i:i + 1] * fine_sin for i in range(rows // 32)])
+        place = base + lax.broadcasted_iota(jnp.int32, (rows, part), 0)
+        first = jnp.zeros((rows, part), jnp.int32)
+        first_cos = jnp.ones((rows, part), f32)
+        first_sin = jnp.zeros((rows, part), f32)
+        start = jnp.int32(0)
+        for i in range(lengths.shape[0] + 1):
+            here = groups[i] == group if i < lengths.shape[0] else True
+            after = place >= (jnp.where(here, start, 1 << 30) if i < lengths.shape[0] else start)
+            angle = start.astype(f32) * speed
+            first = jnp.where(after, start, first)
+            first_cos = jnp.where(after, jnp.cos(angle), first_cos)
+            first_sin = jnp.where(after, jnp.sin(angle), first_sin)
+            if i < lengths.shape[0]:
+                start = start + jnp.where(here, lengths[i], 0)
+        at = pl.ds(pl.multiple_of(t * rows, rows), rows)
+        from_s[at, :] = first
+        cos_s[at, :] = place_cos * first_cos + place_sin * first_sin
+        sin = place_sin * first_cos - place_cos * first_sin
+        sin_s[at, :] = jnp.where(lead, -sin, sin)
+        return carry
+
+    lax.fori_loop(0, 4, fill, 0)
 
     def turn(value, at, sign):
         left = jnp.roll(value, -quarter, axis=1)
         right = jnp.roll(value, quarter, axis=1)
-        return value * cos_ref[0, at, :] + sign * (left * lead_ref[0, at, :] + right * trail_ref[0, at, :])
+        return value * cos_s[at, :] + sign * (jnp.where(lead, left, right) * sin_s[at, :])
 
     def project(i, carry):
         at = pl.ds(pl.multiple_of(i * qb, qb), qb)
@@ -326,8 +388,9 @@
 
     def attend(i, q_sum):
         at = pl.ds(pl.multiple_of(i * qb, qb), qb)
-        key_place = key_ref[0:1, :]
-        allowed = (key_place >= from_ref[0, at, :]) & (key_place <= place_ref[0, at, :])
+        quarter_id = jnp.where(i == 0, quarters[0], jnp.where(i == 1, quarters[1], jnp.where(i == 2, quarters[2], quarters[3])))
+        place = quarter_id * rows + lax.broadcasted_iota(jnp.int32, (rows, 1), 0)
+        allowed = (key_place >= from_s[at, 0:1]) & (key_place <= place)
         queries, d_attn = q_s[at, :], da_s[at, :]
         out = jnp.zeros((qb, part), f32)
         d_q = jnp.zeros((qb, part), f32)
@@ -361,8 +424,8 @@
     sums_ref[0, 0:1, 2 * part:3 * part] = jnp.sum(d_v.astype(f32), axis=0, keepdims=True)
 
 
-def local_part(normed, back, qkv_mat, up_mat, out_mat, bias, cosine, lead, trail, first, place, key_place):
-    groups, slots, width = normed.shape
+def local_part(tier_count, lengths, groups, normed, back, qkv_mat, up_mat, out_mat, bias):
+    count, slots, width = normed.shape
     part = out_mat.shape[0] // 5
 
     def each(last):
@@ -372,18 +435,20 @@
         return pl.BlockSpec(value.shape, lambda p: (0,) * value.ndim, pipeline_mode=pl.Buffered(1))
 
     def like(last, kind=bf16):
-        return jax.ShapeDtypeStruct((groups, slots, last), kind)
-
+        return jax.ShapeDtypeStruct((count, slots, last), kind)
+
+    smem = pl.BlockSpec(memory_space=pltpu.SMEM)
     return pl.pallas_call(
-        local_kernel,
-        grid=(groups,),
-        out_shape=[like(part), like(4 * part), like(3 * part), like(4 * part), jax.ShapeDtypeStruct((groups, 8, 7 * part), f32)],
-        in_specs=[each(width), each(width), once(qkv_mat), once(up_mat), once(out_mat), once(bias),
-                  each(part), each(part), each(part), each(1), each(1), once(key_place)],
+        functools.partial(local_kernel, tier_count),
+        grid=(count,),
+        out_shape=[like(part), like(4 * part), like(3 * part), like(4 * part), jax.ShapeDtypeStruct((count, 8, 7 * part), f32)],
+        in_specs=[smem, smem, each(width), each(width), once(qkv_mat), once(up_mat), once(out_mat), once(bias)],
         out_specs=[each(part), each(4 * part), each(3 * part), each(4 * part), pl.BlockSpec((1, 8, 7 * part), lambda p: (p, 0, 0))],
-        scratch_shapes=[pltpu.VMEM((slots, part), bf16)] * 4 + [pltpu.VMEM((part, slots), f32)] * 2,
-        compiler_params=pltpu.CompilerParams(vmem_limit_bytes=56 << 20),
-    )(normed, back, qkv_mat, up_mat, out_mat, bias, cosine, lead, trail, first, place, key_place)
+        scratch_shapes=[pltpu.VMEM((slots, part), bf16)] * 4 + [pltpu.VMEM((part, slots), f32)] * 2
+        + [pltpu.VMEM((slots, part), f32)] * 2 + [pltpu.VMEM((slots, part), jnp.int32)],
+        compiler_params=pltpu.CompilerParams(vmem_limit_bytes=62 << 20),
+    )(lengths, groups, normed, back, qkv_mat, up_mat, out_mat, bias)
+
 
 def scatter_kernel(tier_count, order, attn, hidden, dqkv, dup, x_in, b_in, wq, wu, dm, tok, bias_ref,
                    block_out, dn_out, g_out, gd_out,
@@ -739,38 +804,11 @@
             value = lax.psum(value, "dp", axis_index_groups=tier_groups)
         return value
 
-    odd = ((line_id & 1) ^ col_id) == 1
-    first_bits = (line_id & 1) ^ col_id
     part_start = row_id * row_width + line_id * part
     col_start = col_id * half_width
 
-    def by_half(vector):
-        mine = lax.dynamic_slice_in_dim(vector, col_start, half_width, 0)
-        other = lax.dynamic_slice_in_dim(vector, (1 - col_id) * half_width, half_width, 0)
-        return jnp.concatenate([mine, other])
-
-    places = jnp.concatenate(
-        [(row_id ^ t) * tok_dev + jnp.arange(tok_dev, dtype=jnp.int32) for t in range(4)]
-    )
-    positions = []
-    for p in range(2):
-        group_id = (line_id ^ first_bits ^ (2 * p)) * tier_count + tier_id
-        positions.append(seq_layout(doc_lengths, doc_groups, group_id, places))
-    positions = jnp.stack(positions)
-    cos_part, sin_part = turn_angles(positions)
-    nothing = jnp.zeros((2, slot_count, HDIM - ROT), f32)
-    still = jnp.zeros_like(sin_part)
-
-    def over_heads(*pieces):
-        return jnp.tile(jnp.concatenate(pieces, axis=-1), (1, 1, heads_dev))
-
-    cosine = over_heads(cos_part, cos_part, nothing + 1.0)
-    lead = over_heads(-sin_part, still, nothing)
-    trail = over_heads(still, sin_part, nothing)
-    seq_from = (places[None] - positions)[:, :, None]
-    place_col = jnp.broadcast_to(places[None, :, None], seq_from.shape)
     total_len = jnp.sum(jnp.where(doc_groups == dp_id, doc_lengths, 0), dtype=jnp.int32)
-    own_valid = places[:tok_dev] < total_len
+    own_valid = row_id * tok_dev + jnp.arange(tok_dev, dtype=jnp.int32) < total_len
     back_own = jnp.where(own_valid[:, None], cotangent, jnp.zeros_like(cotangent))
 
     def tier_gather(value):
@@ -778,43 +816,46 @@
             value = lax.all_gather(value, "dp", axis=0, tiled=True, axis_index_groups=tier_groups)
         return value
 
-    def pieces_of(weight):
-        low = tier_gather(weight.astype(bf16))
-        rows, parts = low.shape[:2]
-        return low.reshape(rows, parts, LINE, part).transpose(2, 0, 1, 3).reshape(LINE, rows, parts * part)
-
-    down_low = tier_gather(w_down.astype(bf16)).transpose(1, 0, 2).reshape(4 * part, half_width)
-    out_low = jnp.concatenate([tier_gather(w_dense.astype(bf16)), down_low], axis=0)
-    norm_vec = jnp.stack([by_half(vectors[0]), by_half(vectors[1])])
+    if tier_count > 1:
+        full_qkv, full_up, full_dense, full_down = [
+            tier_gather(weight.astype(bf16)).astype(f32) for weight in (w_qkv, w_up, w_dense, w_down)
+        ]
+    else:
+        full_qkv, full_up, full_dense, full_down = w_qkv, w_up, w_dense, w_down
     normed, back, qkv_mat, up_mat, out_mat = gather(
-        tier_count, tokens, back_own, norm_vec, pieces_of(w_qkv), pieces_of(w_up), out_low
+        tier_count,
+        doc_lengths,
+        doc_groups,
+        tokens,
+        cotangent,
+        vectors,
+        full_qkv.transpose(1, 0, 2),
+        full_up,
+        full_dense,
+        full_down,
     )
     rows_all = 2 * slot_count
     normed = normed.reshape(rows_all, full_width)
     back = back.reshape(rows_all, full_width)
     qkv_mat = qkv_mat.reshape(full_width, 3 * part)
     up_mat = up_mat.reshape(full_width, 4 * part)
-    dense_mat = out_mat[:part]
-    down_mat = out_mat[part:]
 
     bias_qkv = lax.dynamic_slice(vectors[2:5], (zero_index, part_start), (3, part)).reshape(3 * part)
     bias_up = lax.dynamic_slice(vectors[5:9], (zero_index, part_start), (4, part)).reshape(4 * part)
 
     bias = jnp.concatenate([bias_qkv, bias_up])[None]
     attn, hidden, d_qkv, d_pre_up, bias_sums = local_part(
+        tier_count,
+        doc_lengths,
+        doc_groups,
         normed.reshape(2, slot_count, full_width),
         back.reshape(2, slot_count, full_width),
         qkv_mat,
         up_mat,
         out_mat,
         bias,
-        cosine,
-        lead,
-        trail,
-        seq_from,
-        place_col,
-        places[None],
     )
+    bias_sums = bias_sums[:, 0]
     out_bias = lax.dynamic_slice_in_dim(vectors[9] + vectors[10], col_start, half_width, 0)
     block_out, d_normed, grad_in, grad_out = scatter(
         tier_count,
@@ -830,7 +871,7 @@
         tokens,
         out_bias[None],
     )
-    bias_sums = jnp.sum(bias_sums[:, 0], axis=0).reshape(7, part)
+    bias_sums = jnp.sum(bias_sums, axis=0).reshape(7, part)
 
     def tier_sum(value):
         if tier_count > 1:

time: 460 us -> 420 us (0.913)
  local copies, waits for them, and re-layouts: 55.4 us -> 26 us
  other arithmetic: 41.3 us -> 30.4 us
    unnamed x65 -> x49, local copies, waits for them, and re-layouts: 27.3 us -> 15.5 us
    another operation x8 -> x0, local copies, waits for them, and re-layouts: 5.53 us -> none  [the longest x6 4.28 us: over_heads(): return jnp.tile(jnp.concatenate(pieces, axis=-1), (1, 1, heads_dev))]
    reshape x3, local copies, waits for them, and re-layouts: 8.79 us -> 3.96 us  [own_columns(): value.transpose(1, 2, 0, 3).reshape(half_width // LINE, parts, row_width)]
    ppermute x4, waiting for transfers between devices: 4.79 us -> 0.01 us  [over_col(): return lax.ppermute(value, 'col', [(0, 1), (1, 0)])]
  transfers between devices with their start and end apart: 16 -> 16, of which waited for: 7 -> 3; matrix products, arithmetic and copies ran while one was open for 12% -> 12% of each run, Pallas kernels for 32% -> 79%
where the time goes in v3:
time: 420 us; the launch traced here: 416 us
  Pallas kernels  328 us (78%)
  other arithmetic  30.4 us (7%)
  local copies, waits for them, and re-layouts  26 us (6%)
  starting transfers between devices  18.3 us (4%)
  waiting for transfers between devices  11 us (3%)
    pallas_call x1, Pallas kernels, scatter(): pl.pallas_call(functools.partial(scatter_kernel, tier_count, order or sca...  144 us
    pallas_call x1, Pallas kernels, gather(): pl.pallas_call(functools.partial(gather_kernel, tier_count, ORDER_A), out...  135 us
    pallas_call x1, Pallas kernels, local_part(): pl.pallas_call(functools.partial(local_kernel, tier_count), grid=(count,)...  49.5 us
    sub x5, other arithmetic, adamw(): return (first_next, second_next, weight - rate * (update + decay * weight))  20.1 us
    unnamed x49, local copies, waits for them, and re-layouts  15.5 us
    ppermute x6, starting transfers between devices, over_line(): return lax.ppermute(value, 'dp', pairs)  8.9 us
  transfers between devices with their start and end apart: 16, of which 3 were waited for; matrix products, arithmetic and copies ran while one was open for 12% of the time, Pallas kernels for 79%

profile of v3, /device:TPU:0, one launch (start us, length us, event | category | flops | bytes accessed | tf_op | source)
XLA Modules:
  0.0 415.6 jit_solution(9919873918023663612)
XLA Ops:
  0.7 0.0 copy-start.19
  0.7 0.0 copy-start.20
  0.7 1.3 convert_reduce_fusion
  2.0 3.0 collective-permute-start
  5.0 0.9 slice.43
  5.9 0.9 slice.42
  6.8 0.9 fusion.26
  7.8 0.6 broadcast_in_dim.27.bias_ref
  8.4 3.0 copy.47
  11.4 0.6 fusion.17
  12.0 0.6 dynamic-slice_add_fusion
  12.6 134.8 %shard_map.314 = (bf16[2,4,256,2048]{3,2,1,0:T(8,128)(2,1)}, bf16[2,4,256,2048]{3,2,1,0:T(8,128)(2,1)}, bf16[2,4,256,384]{3,2,1,0:T(8,128)(2,1)}, bf16[2,4,256,512]{3,2,1,0:T(8,128)(2,1)}, bf16[640,2048]{1,0:T(8,128)(2,1)}) custom-call(s32[12]{0:T(128)} %lengths.3, s32[12]{0:T(128)} %groups.3, bf16[256,1024]{1,0:T(8,128)(2,1)} %tok.3, ...), custom_call_target="tpu_custom_call" | custom-call | tf_op jit(solution)/shard_map/pallas_call | solution.py:266
  147.4 49.5 %shard_map.315 = (bf16[2,1024,128]{2,1,0:T(8,128)(2,1)}, bf16[2,1024,512]{2,1,0:T(8,128)(2,1)}, bf16[2,1024,384]{2,1,0:T(8,128)(2,1)}, bf16[2,1024,512]{2,1,0:T(8,128)(2,1)}, f32[2,8,896]{2,1,0:T(8,128)}) custom-call(s32[12]{0:T(128)} %lengths.3, s32[12]{0:T(128)} %groups.3, bf16[2,1024,2048]{2,1,0:T(8,128)(2,1)} %bitcast.57, ...), custom_call_target="tpu_custom_call" | custom-call | tf_op jit(solution)/shard_map/pallas_call | solution.py:441
  196.9 144.0 %shard_map.316 = (bf16[256,1024]{1,0:T(8,128)(2,1)}, f32[256,1024]{1,0:T(8,128)}, bf16[4,256,896]{2,1,0:T(8,128)(2,1)}, f32[640,1024]{1,0:T(8,128)}) custom-call(bf16[2048,128]{1,0:T(8,128)(2,1)} %bitcast.71, bf16[2048,512]{1,0:T(8,128)(2,1)} %bitcast.68, bf16[2048,384]{1,0:T(8,128)(2,1)} %bitcast.70, bf16[2048,512]{1,0:T(8,128)(2,1)} %bitcast.69, ...), custom_call_target="tpu_custom_call" | custom-call | tf_op jit(solution)/shard_map/pallas_call | solution.py:725
  341.0 1.4 slice_convert_fusion.1
  342.3 0.4 copy-done.12
  342.7 1.6 slice_convert_fusion
  344.3 0.8 slice_reduce_fusion
  345.1 0.5 copy.43
  345.6 0.0 copy-start.13
  345.6 1.3 copy.44
  346.9 0.6 copy-done.13
  347.6 1.6 copy.42
  349.2 1.6 copy.45
  350.8 2.2 reshape.148
  353.0 0.0 copy-start.1
  353.0 0.0 copy-start.9
  353.0 1.9 slice.54
  354.9 0.3 copy-done.1
  355.2 0.6 copy-done.9
  355.9 6.5 %multiply_subtract_fusion.1 = (f32[256,4,512]{2,1,0:T(4,128)}, f32[256,4,512]{2,1,0:T(4,128)}, f32[256,4,512]{2,1,0:T(4,128)}) fusion(f32[256,4,512]{2,1,0:T(4,128)S(1)} %copy-done.1, f32[256,4,512]{2,1,0:T(4,128)S(1)} %copy-done.9, f32[256,4,512]{2,1,0:T(4,128)} %param.30, f32[4,256,4,128]{3,2,1,0:T(4,128)S(1)} %reshape.148), kind=kLoop, calls=%fused_computation.10 | loop fusion | flops 7864320 | bytes 14680064 | tf_op jit(solution)/shard_map/sub | solution.py:30
  362.3 0.0 copy-start.4
  362.4 0.0 copy-start.5
  362.4 7.0 %multiply_subtract_fusion = (f32[128,4,1024]{2,1,0:T(4,128)}, f32[128,4,1024]{2,1,0:T(4,128)}, f32[128,4,1024]{2,1,0:T(4,128)}) fusion(f32[128,4,1024]{2,1,0:T(4,128)S(1)} %copy-done.2, f32[4,128,1024]{2,1,0:T(8,128)S(1)} %bitcast.61, f32[128,4,1024]{2,1,0:T(4,128)S(1)} %copy-done.10, f32[128,4,1024]{2,1,0:T(4,128)S(1)} %copy-done.11), kind=kLoop, calls=%fused_computation.9 | loop fusion | flops 7864320 | bytes 14680064 | tf_op jit(solution)/shard_map/sub | solution.py:30
  369.4 0.0 copy-start
  369.4 2.8 multiply_subtract_fusion.2
  372.3 0.7 add_compare_fusion
  373.0 0.5 dynamic_update_slice.10
  373.6 0.5 fusion.14
  374.1 0.3 collective-permute-start.1
  374.4 1.6 collective-permute-start.2
  376.0 2.8 collective-permute-start.4
  378.9 2.5 convert_reduce_fusion.1
  381.4 0.8 dynamic_update_slice.11
  382.3 0.2 collective-permute-start.10
  382.4 2.0 collective-permute-start.11
  384.4 2.3 collective-permute-start.9
  386.8 0.1 collective-permute-start.5
  386.8 0.5 collective-permute-start.6
  387.4 6.3 %collective-permute-done.10 = f32[9,2048]{1,0:T(8,128)S(1)} collective-permute-done((f32[9,2048]{1,0:T(8,128)S(1)}, f32[9,2048]{1,0:T(8,128)S(1)}, u32[]{:S(2)}, u32[]{:S(2)}) %collective-permute-start.10) | collective-permute-done | bytes 73760 | tf_op jit(solution)/shard_map/ppermute | solution.py:785
  393.6 0.1 select_add_fusion.1
  393.7 0.6 collective-permute-start.12
  394.3 1.6 collective-permute-start.13
  396.0 1.7 collective-permute-start.8
  397.6 1.3 collective-permute-done.12
  398.9 3.4 collective-permute-done.13
  402.4 0.1 select_add_fusion
  402.4 1.7 collective-permute-start.15
  404.1 2.9 multiply_subtract_fusion.3
  407.0 3.1 copy.50
  410.2 1.6 copy.51
  411.8 1.6 copy.52
  413.5 0.8 multiply_subtract_fusion.4
  414.3 0.8 copy.66
  (64 shorter events, 0.3 us)
Async XLA Ops:
  0.7 10.7 %copy-start.19 = (s32[12]{0:T(128)S(1)}, s32[12]{0:T(128)}, u32[]{:S(2)}) copy-start(s32[12]{0:T(128)} %lengths.3) | copy-start | bytes 148
  0.7 10.7 %copy-start.20 = (s32[12]{0:T(128)S(1)}, s32[12]{0:T(128)}, u32[]{:S(2)}) copy-start(s32[12]{0:T(128)} %groups.3) | copy-start | bytes 148
  2.0 371.5 %collective-permute-start = (f32[2,256]{1,0:T(2,128)S(1)}, f32[2,256]{1,0:T(2,128)S(1)}, u32[]{:S(2)}, u32[]{:S(2)}) collective-permute-start(f32[2,256]{1,0:T(2,128)S(1)} %pad_maximum_fusion.3), channel_id=1, source_target_pairs={{0,1},{1,0},{2,3},{3,2},{4,5},{5,4},{6,7},{7,6},{8,9},{9,8},{10,11... | collective-permute-start | bytes 6152 | tf_op jit(solution)/shard_map/ppermute | solution.py:791
  340.9 1.7 copy-start.12
  345.6 2.0 copy-start.13
  347.6 1.6 copy-start.14
  353.0 2.2 copy-start.1
  353.0 2.8 copy-start.9
  355.9 6.5 %copy-start.2 = (f32[128,4,1024]{2,1,0:T(4,128)S(1)}, f32[128,4,1024]{2,1,0:T(4,128)}, u32[]{:S(2)}) copy-start(f32[128,4,1024]{2,1,0:T(4,128)} %w_down.1) | copy-start | bytes 6291460
  355.9 6.5 %copy-start.10 = (f32[128,4,1024]{2,1,0:T(4,128)S(1)}, f32[128,4,1024]{2,1,0:T(4,128)}, u32[]{:S(2)}) copy-start(f32[128,4,1024]{2,1,0:T(4,128)} %param.35) | copy-start | bytes 6291460
  355.9 6.5 %copy-start.11 = (f32[128,4,1024]{2,1,0:T(4,128)S(1)}, f32[128,4,1024]{2,1,0:T(4,128)}, u32[]{:S(2)}) copy-start(f32[128,4,1024]{2,1,0:T(4,128)} %param.34) | copy-start | bytes 6291460
  362.3 7.1 %copy-start.4 = (f32[256,3,512]{0,2,1:T(8,128)S(1)}, f32[256,3,512]{0,2,1:T(8,128)}, u32[]{:S(2)}) copy-start(f32[256,3,512]{0,2,1:T(8,128)} %copy.47) | copy-start | bytes 4718596
  362.4 7.0 %copy-start.5 = (f32[256,3,4,128]{0,3,2,1:T(8,128)S(1)}, f32[256,3,4,128]{0,3,2,1:T(8,128)}, u32[]{:S(2)}) copy-start(f32[256,3,4,128]{0,3,2,1:T(8,128)} %copy.44) | copy-start | bytes 4718596
  362.4 7.0 %copy-start.6 = (f32[256,3,512]{0,2,1:T(8,128)S(1)}, f32[256,3,512]{0,2,1:T(8,128)}, u32[]{:S(2)}) copy-start(f32[256,3,512]{0,2,1:T(8,128)} %copy.42) | copy-start | bytes 4718596
  362.4 7.0 %copy-start.7 = (f32[256,3,512]{0,2,1:T(8,128)S(1)}, f32[256,3,512]{0,2,1:T(8,128)}, u32[]{:S(2)}) copy-start(f32[256,3,512]{0,2,1:T(8,128)} %copy.45) | copy-start | bytes 4718596
  369.4 4.1 copy-start
  369.4 4.1 copy-start.8
  374.1 4.7 %collective-permute-start.1 = (f32[2,256]{1,0:T(2,128)S(1)}, f32[2,256]{1,0:T(2,128)S(1)}, u32[]{:S(2)}, u32[]{:S(2)}) collective-permute-start(f32[2,256]{1,0:T(2,128)S(1)} %pad_maximum_fusion.4), channel_id=1, source_target_pairs={{0,1},{1,0},{2,3},{3,2},{4,5},{5,4},{6,7},{7,6},{8,9},{9,8},{10,11... | collective-permute-start | bytes 6152 | tf_op jit(solution)/shard_map/ppermute | solution.py:791
  374.4 10.0 %collective-permute-start.2 = (f32[2,2048]{1,0:T(2,128)S(1)}, f32[2,2048]{1,0:T(2,128)S(1)}, u32[]{:S(2)}, u32[]{:S(2)}) collective-permute-start(f32[2,2048]{1,0:T(2,128)S(1)} %maximum_dynamic-update-slice_fusion), channel_id=1, source_target_pairs={{0,24},{8,16},{16,8},{24,0},{1,25},{9,17},{17,9},{25,1},{2,26},{10... | collective-permute-start | bytes 49160 | tf_op jit(solution)/shard_map/ppermute | solution.py:785
  376.0 10.7 %collective-permute-start.3 = (f32[2,2048]{1,0:T(2,128)S(1)}, f32[2,2048]{1,0:T(2,128)S(1)}, u32[]{:S(2)}, u32[]{:S(2)}) collective-permute-start(f32[2,2048]{1,0:T(2,128)S(1)} %maximum_dynamic-update-slice_fusion), channel_id=1, source_target_pairs={{0,16},{8,24},{16,0},{24,8},{1,17},{9,25},{17,1},{25,9},{2,18},{10... | collective-permute-start | bytes 49160 | tf_op jit(solution)/shard_map/ppermute | solution.py:785
  376.0 10.7 %collective-permute-start.4 = (f32[2,2048]{1,0:T(2,128)S(1)}, f32[2,2048]{1,0:T(2,128)S(1)}, u32[]{:S(2)}, u32[]{:S(2)}) collective-permute-start(f32[2,2048]{1,0:T(2,128)S(1)} %maximum_dynamic-update-slice_fusion), channel_id=1, source_target_pairs={{0,8},{8,0},{16,24},{24,16},{1,9},{9,1},{17,25},{25,17},{2,10},{10... | collective-permute-start | bytes 49160 | tf_op jit(solution)/shard_map/ppermute | solution.py:785
  382.3 11.4 %collective-permute-start.10 = (f32[9,2048]{1,0:T(8,128)S(1)}, f32[9,2048]{1,0:T(8,128)S(1)}, u32[]{:S(2)}, u32[]{:S(2)}) collective-permute-start(f32[9,2048]{1,0:T(8,128)S(1)} %dynamic_update_slice.11), channel_id=1, source_target_pairs={{0,16},{8,24},{16,0},{24,8},{1,17},{9,25},{17,1},{25,9},{2,18},{10... | collective-permute-start | bytes 221192 | tf_op jit(solution)/shard_map/ppermute | solution.py:785
  382.4 11.2 %collective-permute-start.11 = (f32[9,2048]{1,0:T(8,128)S(1)}, f32[9,2048]{1,0:T(8,128)S(1)}, u32[]{:S(2)}, u32[]{:S(2)}) collective-permute-start(f32[9,2048]{1,0:T(8,128)S(1)} %dynamic_update_slice.11), channel_id=1, source_target_pairs={{0,8},{8,0},{16,24},{24,16},{1,9},{9,1},{17,25},{25,17},{2,10},{10... | collective-permute-start | bytes 221192 | tf_op jit(solution)/shard_map/ppermute | solution.py:785
  384.4 9.2 %collective-permute-start.9 = (f32[9,2048]{1,0:T(8,128)S(1)}, f32[9,2048]{1,0:T(8,128)S(1)}, u32[]{:S(2)}, u32[]{:S(2)}) collective-permute-start(f32[9,2048]{1,0:T(8,128)S(1)} %dynamic_update_slice.11), channel_id=1, source_target_pairs={{0,24},{8,16},{16,8},{24,0},{1,25},{9,17},{17,9},{25,1},{2,26},{10... | collective-permute-start | bytes 221192 | tf_op jit(solution)/shard_map/ppermute | solution.py:785
  386.8 9.1 %collective-permute-start.5 = (f32[2,2048]{1,0:T(2,128)S(1)}, f32[2,2048]{1,0:T(2,128)S(1)}, u32[]{:S(2)}, u32[]{:S(2)}) collective-permute-start(f32[2,2048]{1,0:T(2,128)S(1)} %select_add_fusion.3), channel_id=1, source_target_pairs={{0,6},{2,4},{4,2},{6,0},{1,7},{3,5},{5,3},{7,1},{8,14},{10,12},{12... | collective-permute-start | bytes 49160 | tf_op jit(solution)/shard_map/ppermute | solution.py:788
  386.8 9.1 %collective-permute-start.6 = (f32[2,2048]{1,0:T(2,128)S(1)}, f32[2,2048]{1,0:T(2,128)S(1)}, u32[]{:S(2)}, u32[]{:S(2)}) collective-permute-start(f32[2,2048]{1,0:T(2,128)S(1)} %select_add_fusion.3), channel_id=1, source_target_pairs={{0,4},{2,6},{4,0},{6,2},{1,5},{3,7},{5,1},{7,3},{8,12},{10,14},{12... | collective-permute-start | bytes 49160 | tf_op jit(solution)/shard_map/ppermute | solution.py:788
  393.6 2.3 collective-permute-start.7
  393.7 5.2 %collective-permute-start.12 = (f32[9,2048]{1,0:T(8,128)S(1)}, f32[9,2048]{1,0:T(8,128)S(1)}, u32[]{:S(2)}, u32[]{:S(2)}) collective-permute-start(f32[9,2048]{1,0:T(8,128)S(1)} %select_add_fusion.1), channel_id=1, source_target_pairs={{0,6},{2,4},{4,2},{6,0},{1,7},{3,5},{5,3},{7,1},{8,14},{10,12},{12... | collective-permute-start | bytes 221192 | tf_op jit(solution)/shard_map/ppermute | solution.py:788
  394.3 8.1 %collective-permute-start.13 = (f32[9,2048]{1,0:T(8,128)S(1)}, f32[9,2048]{1,0:T(8,128)S(1)}, u32[]{:S(2)}, u32[]{:S(2)}) collective-permute-start(f32[9,2048]{1,0:T(8,128)S(1)} %select_add_fusion.1), channel_id=1, source_target_pairs={{0,4},{2,6},{4,0},{6,2},{1,5},{3,7},{5,1},{7,3},{8,12},{10,14},{12... | collective-permute-start | bytes 221192 | tf_op jit(solution)/shard_map/ppermute | solution.py:788
  395.9 6.5 %collective-permute-start.14 = (f32[9,2048]{1,0:T(8,128)S(1)}, f32[9,2048]{1,0:T(8,128)S(1)}, u32[]{:S(2)}, u32[]{:S(2)}) collective-permute-start(f32[9,2048]{1,0:T(8,128)S(1)} %select_add_fusion.1), channel_id=1, source_target_pairs={{0,2},{2,0},{4,6},{6,4},{1,3},{3,1},{5,7},{7,5},{8,10},{10,8},{12,... | collective-permute-start | bytes 221192 | tf_op jit(solution)/shard_map/ppermute | solution.py:788
  396.0 17.5 %collective-permute-start.8 = (f32[2,2048]{1,0:T(2,128)S(1)}, f32[2,2048]{1,0:T(2,128)S(1)}, u32[]{:S(2)}, u32[]{:S(2)}) collective-permute-start(f32[2,2048]{1,0:T(2,128)S(1)} %select_add_fusion.2), channel_id=1, source_target_pairs={{0,1},{1,0},{2,3},{3,2},{4,5},{5,4},{6,7},{7,6},{8,9},{9,8},{10,11... | collective-permute-start | bytes 49160 | tf_op jit(solution)/shard_map/ppermute | solution.py:791
  402.4 11.0 %collective-permute-start.15 = (f32[9,2048]{1,0:T(8,128)S(1)}, f32[9,2048]{1,0:T(8,128)S(1)}, u32[]{:S(2)}, u32[]{:S(2)}) collective-permute-start(f32[9,2048]{1,0:T(8,128)S(1)} %select_add_fusion), channel_id=1, source_target_pairs={{0,1},{1,0},{2,3},{3,2},{4,5},{5,4},{6,7},{7,6},{8,9},{9,8},{10,11... | collective-permute-start | bytes 221192 | tf_op jit(solution)/shard_map/ppermute | solution.py:791
  407.0 3.1 copy-start.3
  411.8 1.7 copy-start.15
  411.8 1.7 copy-start.17
  411.8 1.7 copy-start.18
  411.8 2.5 copy-start.16
